TPU v7x, 512 devices: a whole 4x4x16 slice. The times are simulated.
512 devices in a mesh: gx: 8 (over y, x_hi), gy: 4 (over x_lo, core), gz: 16 (over z).
Axes of the slice: x: 4 (x_hi: 2, x_lo: 2; x = x_hi * 2 + x_lo), y: 4, z: 16, core: 2. Of those that a mesh axis runs over, the one named last changes fastest.
Arguments:
- noise_vectors: bfloat16 [9, 65536, 128], P(None, ('gx', 'gy', 'gz')), may hold values from -6 to 6
- hamiltonian: bfloat16 [15, 9, 9, 65536], P(None, None, None, ('gx', 'gy', 'gz')), may hold values from -0.25 to 0.25
- derivative: bfloat16 [3, 15, 9, 9, 65536], P(None, None, None, None, ('gx', 'gy', 'gz')), may hold values from -0.625 to 0.625
- neighbours: int32 [65536, 15], P(('gx', 'gy', 'gz')), may hold values from 0 to 65535, as said below
- coefficients: float32 [4], replicated, may hold values from -1 to 1
Outputs:
- weighted: float32 [9, 65536, 128], P(None, ('gx', 'gy', 'gz'))
- forces: float32 [3, 65536], P(None, ('gx', 'gy', 'gz'))
Inputs may be any that keep to these rules, and one draw needn't show every extreme that they name: `neighbours`: slot 0 of every atom's list is the atom itself; the other 14 slots name distinct other atoms whose cells differ from its own by at most one along each dimension, periodically on the grid of 32 x 16 x 64 cells with two atoms a cell. Atom ids run over domains in the order gx, gy, gz, each domain holding 128 atoms numbered by (atom of the cell, first, second, third cell index within the domain).
All inputs are finite; a program needn't handle non-finite values.
Results may differ from a plain program's by a relative error of at most 0.0003.
Values may be sent and summed in bfloat16 or wider, within the bound.
No kernel may reach another device: no remote copies, remote signals or barrier semaphores. Data moves between devices by JAX's collectives and lax.ppermute only.
A program may use at most 128 MiB of HBM per device.

v0:
```python
import functools

import jax
import jax.numpy as jnp
from jax import lax
from jax.experimental import pallas as pl
from jax.experimental.pallas import tpu as pltpu
from jax.sharding import PartitionSpec as P

CX = 4
CY = 4
CZ = 4
ORB = 9
NEIGH = 15
ATOMS = 2 * CX * CY * CZ
VECS = 128
NX = 2 * CY * CZ
NY = 2 * (CX + 2) * CZ
NZ = 2 * (CX + 2) * (CY + 2)
NZ_PAD = 80
BEFORE_Y = ATOMS + 2 * NX
BEFORE_Z = BEFORE_Y + 2 * NY
SLOTS = BEFORE_Z + 2 * NZ
LANES_Z = 384
LANES = 640
F32 = jnp.float32
BF16 = jnp.bfloat16
VMEM = pl.BlockSpec(memory_space=pltpu.VMEM)
SMEM = pl.BlockSpec(memory_space=pltpu.SMEM)


def call(kernel, outs, in_specs, args, scratch=(), flops=0, mib=16):
    shapes = [jax.ShapeDtypeStruct(shape, dtype) for shape, dtype in outs]
    moved = sum(a.size * a.dtype.itemsize for a in args) + sum(s.size * s.dtype.itemsize for s in shapes)
    return pl.pallas_call(
        kernel,
        out_shape=shapes,
        in_specs=in_specs,
        out_specs=[VMEM] * len(shapes),
        scratch_shapes=list(scratch),
        compiler_params=pltpu.CompilerParams(vmem_limit_bytes=mib << 20),
        cost_estimate=pl.CostEstimate(flops=flops, bytes_accessed=moved, transcendentals=0),
    )(*args)


def shifted(value, axis, steps):
    count = lax.axis_size(axis)
    return lax.ppermute(value, axis, [(i, (i + steps) % count) for i in range(count)])


def prep_kernel(ham, rows, turned, wide):
    turned[...] = jnp.zeros_like(turned)
    wide[...] = jnp.zeros_like(wide)
    for a in range(ORB):
        for b in range(ORB):
            turned[pl.ds(b, NEIGH, stride=16), :] = ham[a, b].astype(F32)
        flat = turned[...].T
        wide[0, pl.ds(a, ATOMS, stride=16), :] = flat[:, 0:128]
        wide[1, pl.ds(a, ATOMS, stride=16), :] = flat[:, 128:256]

    def pack(i, carry):
        at = pl.ds(pl.multiple_of(i * 16, 16), 16)
        rows[i, :, 0:128] = wide[0, at, :].astype(BF16)
        rows[i, :, 128:256] = wide[1, at, :].astype(BF16)
        return carry

    lax.fori_loop(0, ATOMS, pack, 0, unroll=8)


def faces_y_kernel(own, x_low, x_high, low, high, held, picked):
    for b in range(ORB):
        held[0:ATOMS] = own[b].astype(F32)
        held[ATOMS : ATOMS + NX] = x_low[b].astype(F32)
        held[ATOMS + NX : BEFORE_Y] = x_high[b].astype(F32)
        for out, y in ((low, 0), (high, CY - 1)):
            for q in range(NY // CZ):
                picked[4 * q : 4 * q + 4] = held[16 * q + 4 * y : 16 * q + 4 * y + 4]
            out[b] = picked[...].astype(out.dtype)


def faces_z_kernel(own, x_low, x_high, y_low, y_high, low, high, held):
    pieces = ((own, ATOMS), (x_low, NX), (x_high, NX), (y_low, NY), (y_high, NY))
    rows = low.shape[1]
    held[BEFORE_Z:] = jnp.zeros((4 * NZ_PAD - BEFORE_Z, VECS), F32)
    for b in range(ORB):
        base = 0
        for ref, count in pieces:
            held[base : base + count] = ref[b].astype(F32)
            base += count
        for out, z in ((low, 0), (high, CZ - 1)):
            out[b] = held[pl.ds(z, rows, stride=4), :].astype(out.dtype)


def load_tiles(pieces, loose):
    zero = jnp.zeros((8, VECS), F32)

    def clear(j, carry):
        loose[pl.ds(pl.multiple_of(j * 16 + 8, 8), 8), :] = zero
        return carry

    lax.fori_loop(0, SLOTS, clear, 0, unroll=16)
    for b in range(ORB):
        base = 0
        for ref, count in pieces:
            loose[pl.ds(base * 16 + b, count, stride=16), :] = ref[b].astype(F32)[0:count]
            base += count


def split_tiles(loose, tiles):
    def split(j, carry):
        value = loose[pl.ds(pl.multiple_of(j * 16, 16), 16), :]
        high = value.astype(BF16)
        tiles[j, :, 0:128] = high
        if tiles.shape[2] == 256:
            tiles[j, :, 128:256] = (value - high.astype(F32)).astype(BF16)
        return carry

    lax.fori_loop(0, SLOTS, split, 0, unroll=16)


def gather(slots, tiles, i):
    taken = [tiles[slots[m, i]] for m in range(NEIGH)]
    return jnp.concatenate(taken + taken[:1], axis=0)


def apply_atoms(slots, rows, tiles, applied):
    def atom(i, carry):
        product = jnp.dot(rows[i], gather(slots, tiles, i), preferred_element_type=F32)
        if tiles.shape[2] == 256:
            product = product[:, 0:128] + product[:, 128:256]
        applied[pl.ds(pl.multiple_of(i * 16, 16), 16), :] = product
        return carry

    lax.fori_loop(0, ATOMS, atom, 0, unroll=16)


def put_faces(b, value, low, high):
    for p in range(2):
        low[b, 16 * p : 16 * p + 16] = value[64 * p : 64 * p + 16]
        high[b, 16 * p : 16 * p + 16] = value[64 * p + 48 : 64 * p + 64]


def first_kernel(coef, slots, rows, own, xl, xh, yl, yh, zl, zh, now, total, low, high, tiles, loose, applied):
    pieces = ((own, ATOMS), (xl, NX), (xh, NX), (yl, NY), (yh, NY), (zl, NZ), (zh, NZ))
    load_tiles(pieces, loose)
    split_tiles(loose, tiles)
    apply_atoms(slots, rows, tiles, applied)
    for a in range(ORB):
        value = applied[pl.ds(a, ATOMS, stride=16), :]
        now[a] = value
        total[a] = coef[0] * own[a].astype(F32) + coef[1] * value
        put_faces(a, value, low, high)


def second_kernel(coef, slots, rows, prev, sum_in, own, xl, xh, yl, yh, zl, zh, now, total, low, high, loose, tiles, applied):
    pieces = ((own, ATOMS), (xl, NX), (xh, NX), (yl, NY), (yh, NY), (zl, NZ), (zh, NZ))
    load_tiles(pieces, loose)
    split_tiles(loose, tiles)
    apply_atoms(slots, rows, tiles, applied)
    for a in range(ORB):
        value = 2.0 * applied[pl.ds(a, ATOMS, stride=16), :] - prev[a].astype(F32)
        now[a] = value
        total[a] = sum_in[a] + coef[2] * value
        put_faces(a, value, low, high)


def third_kernel(coef, slots, lanes, rows, prev, sum_in, noise_tiles, deriv, own, xl, xh, yl, yh, zl, zh,
                 total, forces, loose, tiles, applied, dense, turned, stacked):
    pieces = ((own, ATOMS), (xl, NX), (xh, NX), (yl, NY), (yh, NY), (zl, NZ), (zh, NZ))
    load_tiles(pieces, loose)
    split_tiles(loose, tiles)
    apply_atoms(slots, rows, tiles, applied)
    for a in range(ORB):
        at = pl.ds(a, ATOMS, stride=16)
        value = sum_in[a] + coef[3] * (2.0 * applied[at, :] - prev[a])
        total[a] = value
        applied[at, :] = value

    def atom(i, carry):
        at = pl.ds(pl.multiple_of(i * 16, 16), 16)
        value = applied[at, :]
        high = value.astype(BF16)
        low = (value - high.astype(F32)).astype(BF16)
        product = lax.dot_general(
            jnp.concatenate([high, low], axis=0),
            gather(slots, noise_tiles, i),
            (((1,), (1,)), ((), ())),
            preferred_element_type=F32,
        )
        product = product[0:16] + product[16:32]
        dense[0, at, :] = product[:, 0:128]
        dense[1, at, :] = product[:, 128:256]
        return carry

    lax.fori_loop(0, ATOMS, atom, 0, unroll=16)
    pair = [jnp.zeros((NEIGH, ATOMS), F32) for _ in range(3)]
    for a in range(ORB):
        at = pl.ds(a, ATOMS, stride=16)
        turned[0:128] = dense[0, at, :].T
        turned[128:256] = dense[1, at, :].T
        for b in range(ORB):
            density = turned[pl.ds(b, NEIGH, stride=16), :]
            for c in range(3):
                pair[c] = pair[c] + deriv[c, a, b].astype(F32) * density
    others = lax.broadcasted_iota(jnp.int32, (NEIGH, ATOMS), 0) > 0
    stacked[...] = jnp.zeros_like(stacked)
    own_rows = []
    for c in range(3):
        value = jnp.where(others, pair[c] * (1.0 / VECS), 0.0)
        high = value.astype(BF16).astype(F32)
        stacked[pl.ds(c, NEIGH, stride=16), :] = high
        stacked[pl.ds(8 + c, NEIGH, stride=16), :] = value - high
        own_rows.append(jnp.sum(value, axis=0, keepdims=True))
    lane = lax.broadcasted_iota(jnp.int32, (LANES, ATOMS), 0)
    summed = jnp.zeros((16, LANES), F32)
    for m in range(1, NEIGH):
        hit = jnp.where(lane == lanes[m : m + 1, :], 1.0, 0.0).astype(BF16)
        summed = summed + lax.dot_general(
            stacked[16 * m : 16 * m + 16].astype(BF16), hit, (((1,), (1,)), ((), ())), preferred_element_type=F32
        )
    forces[...] = summed[0:8] + summed[8:16]
    for c in range(3):
        forces[c : c + 1, 0:ATOMS] = forces[c : c + 1, 0:ATOMS] - own_rows[c]


def spread(value, place, width):
    row = lax.broadcasted_iota(jnp.int32, (VECS, width), 0)
    lane = lax.broadcasted_iota(jnp.int32, (VECS, width), 1)
    hit = jnp.where((lane == place(row)), 1.0, 0.0)
    return jnp.dot(value, hit, precision=lax.Precision.HIGHEST, preferred_element_type=F32)


def place_z(z):
    return lambda r: jnp.where(r < NZ, 4 * r + z, -1)


def place_y(y):
    return lambda r: jnp.where(r < NY, (r >> 2) * 16 + 4 * y + (r & 3), -1)


def place_x(x):
    return lambda r: jnp.where(r < NX, (r >> 4) * 64 + 16 * x + (r & 15), -1)


def merge_z_kernel(held, above, below, out, low, high):
    width = LANES_Z
    out[...] = held[:, 0:width] + spread(above[...], place_z(CZ - 1), width) + spread(below[...], place_z(0), width)
    low[...] = jnp.zeros_like(low)
    high[...] = jnp.zeros_like(high)
    low[:, 0:NY] = out[:, BEFORE_Y : BEFORE_Y + NY]
    high[:, 0:NY] = out[:, BEFORE_Y + NY : BEFORE_Z]


def merge_y_kernel(held, above, below, out, low, high):
    width = 256
    out[...] = held[:, 0:width] + spread(above[...], place_y(CY - 1), width) + spread(below[...], place_y(0), width)
    low[...] = jnp.zeros_like(low)
    high[...] = jnp.zeros_like(high)
    low[:, 0:NX] = out[:, ATOMS : ATOMS + NX]
    high[:, 0:NX] = out[:, ATOMS + NX : BEFORE_Y]


def merge_x_kernel(held, above, below, out):
    width = ATOMS
    value = held[:, 0:width] + spread(above[...], place_x(CX - 1), width) + spread(below[...], place_x(0), width)
    out[...] = value[0:3]


def slots_of(neighbours):
    cells = CX * CY * CZ
    size_x, size_y, size_z = (lax.axis_size(axis) for axis in ("gx", "gy", "gz"))
    partner = neighbours.T
    domain = partner // ATOMS
    within = partner % ATOMS
    basis = within // cells
    remain = within % cells
    ex = domain // (size_y * size_z) * CX + remain // (CY * CZ) - lax.axis_index("gx") * CX + 1
    ey = domain // size_z % size_y * CY + remain // CZ % CY - lax.axis_index("gy") * CY + 1
    ez = domain % size_z * CZ + remain % CZ - lax.axis_index("gz") * CZ + 1
    ex = jnp.remainder(ex, CX * size_x)
    ey = jnp.remainder(ey, CY * size_y)
    ez = jnp.remainder(ez, CZ * size_z)
    x_out = (ex == 0) | (ex == CX + 1)
    y_out = (ey == 0) | (ey == CY + 1)
    z_out = (ez == 0) | (ez == CZ + 1)
    q = jnp.where(x_out, 2 * CX + 2 * (ex == CX + 1) + basis, basis * CX + ex - 1)
    r_in = q * CY + ey - 1
    r_out = 2 * (CX + 2) * CY + (ey == CY + 1) * (2 * (CX + 2)) + q
    r = jnp.where(y_out, r_out, r_in)
    slots = jnp.where(z_out, BEFORE_Z + (ez == CZ + 1) * NZ + r, r * CZ + ez - 1)
    lanes = jnp.where(z_out, LANES_Z + (ez == CZ + 1) * 128 + r, r * CZ + ez - 1)
    return slots.astype(jnp.int32), lanes.astype(jnp.int32)


def exchange(own, low, high):
    dtype = own.dtype
    rows_z = NZ_PAD if dtype == BF16 else NZ
    face = lambda rows: ((ORB, rows, VECS), dtype)
    xl, xh = shifted(high, "gx", 1), shifted(low, "gx", -1)
    low, high = call(
        faces_y_kernel, [face(NY)] * 2, [VMEM] * 3, (own, xl, xh),
        [pltpu.VMEM((BEFORE_Y, VECS), F32), pltpu.VMEM((NY, VECS), F32)],
    )
    yl, yh = shifted(high, "gy", 1), shifted(low, "gy", -1)
    low, high = call(
        faces_z_kernel, [face(rows_z)] * 2, [VMEM] * 5, (own, xl, xh, yl, yh),
        [pltpu.VMEM((4 * NZ_PAD, VECS), F32)],
    )
    zl, zh = shifted(high, "gz", 1), shifted(low, "gz", -1)
    return xl, xh, yl, yh, zl, zh


def shards(noise_vectors, hamiltonian, derivative, neighbours, coefficients):
    slots, lanes = slots_of(neighbours)
    lattice = noise_vectors.reshape(ORB, 2, CX, CY * CZ, VECS)
    low = lattice[:, :, 0].reshape(ORB, NX, VECS)
    high = lattice[:, :, CX - 1].reshape(ORB, NX, VECS)
    (rows,) = call(
        prep_kernel, [((ATOMS, 16, 256), BF16)], [VMEM], (hamiltonian.transpose(1, 2, 0, 3),),
        [pltpu.VMEM((256, ATOMS), F32), pltpu.VMEM((2, ATOMS * 16, 128), F32)],
        flops=1 << 22,
    )
    whole = ((ORB, ATOMS, VECS), F32)
    plane = ((ORB, NX, VECS), F32)
    loose = pltpu.VMEM((SLOTS * 16, VECS), F32)
    applied = pltpu.VMEM((ATOMS * 16, VECS), F32)
    split = pltpu.VMEM((SLOTS, 16, 256), BF16)
    ghosts = exchange(noise_vectors, low, high)
    first, total, low, high, noise_tiles = call(
        first_kernel, [whole, whole, plane, plane, ((SLOTS, 16, VECS), BF16)], [SMEM, SMEM] + [VMEM] * 8,
        (coefficients, slots, rows, noise_vectors) + ghosts, [loose, applied], flops=1 << 30, mib=24,
    )
    ghosts = exchange(first, low, high)
    second, total, low, high = call(
        second_kernel, [whole, whole, plane, plane], [SMEM, SMEM] + [VMEM] * 10,
        (coefficients, slots, rows, noise_vectors, total, first) + ghosts, [loose, split, applied], flops=1 << 30, mib=24,
    )
    ghosts = exchange(second, low, high)
    weighted, held = call(
        third_kernel, [whole, ((8, LANES), F32)], [SMEM, SMEM] + [VMEM] * 13,
        (coefficients, slots, lanes, rows, first, total, noise_tiles, derivative.transpose(0, 2, 3, 1, 4), second) + ghosts,
        [loose, split, applied, pltpu.VMEM((2, ATOMS * 16, 128), F32), pltpu.VMEM((256, ATOMS), F32),
         pltpu.VMEM((NEIGH * 16, ATOMS), F32)],
        flops=1 << 31, mib=32,
    )
    tile = ((8, 128), F32)
    low, high = held[:, LANES_Z : LANES_Z + 128], held[:, LANES_Z + 128 :]
    above, below = shifted(low, "gz", -1), shifted(high, "gz", 1)
    held, low, high = call(merge_z_kernel, [((8, LANES_Z), F32), tile, tile], [VMEM] * 3, (held, above, below))
    above, below = shifted(low, "gy", -1), shifted(high, "gy", 1)
    held, low, high = call(merge_y_kernel, [((8, 256), F32), tile, tile], [VMEM] * 3, (held, above, below))
    above, below = shifted(low, "gx", -1), shifted(high, "gx", 1)
    (forces,) = call(merge_x_kernel, [((3, ATOMS), F32)], [VMEM] * 3, (held, above, below))
    return weighted, forces


def solution(mesh):
    in_specs = (
        P(None, ("gx", "gy", "gz"), None),
        P(None, None, None, ("gx", "gy", "gz")),
        P(None, None, None, None, ("gx", "gy", "gz")),
        P(("gx", "gy", "gz"), None),
        P(),
    )
    out_specs = (P(None, ("gx", "gy", "gz"), None), P(None, ("gx", "gy", "gz")))
    return jax.shard_map(shards, mesh=mesh, in_specs=in_specs, out_specs=out_specs, check_vma=False)
```

profile of v0, /device:TPU:1, one launch (start us, length us, event | category | flops | bytes accessed | tf_op | source)
XLA Modules:
  0.0 175.9 jit_solution(3896228202637913472)
XLA Ops:
  1.6 5.5 %collective-permute-start = (bf16[9,32,128]{2,1,0:T(8,128)(2,1)S(1)}, bf16[9,32,128]{2,1,0:T(8,128)(2,1)S(1)}, u32[]{:S(2)}, u32[]{:S(2)}) collective-permute-start(bf16[9,32,128]{2,1,0:T(8,128)(2,1)S(1)} %bitcast.49), channel_id=1, source_target_pairs={{0,64},{64,128},{128,192},{192,256},{256,320},{320,384},{384,448},... | collective-permute-start | bytes 221192 | tf_op jit(solution)/shard_map/ppermute | solution.py:48
  7.1 4.4 %collective-permute-start.1 = (bf16[9,32,128]{2,1,0:T(8,128)(2,1)S(1)}, bf16[9,32,128]{2,1,0:T(8,128)(2,1)S(1)}, u32[]{:S(2)}, u32[]{:S(2)}) collective-permute-start(bf16[9,32,128]{2,1,0:T(8,128)(2,1)S(1)} %bitcast.48), channel_id=1, source_target_pairs={{0,448},{64,0},{128,64},{192,128},{256,192},{320,256},{384,320},{4... | collective-permute-start | bytes 221192 | tf_op jit(solution)/shard_map/ppermute | solution.py:48
  14.9 4.2 %collective-permute-start.2 = (bf16[9,48,128]{2,1,0:T(8,128)(2,1)S(1)}, bf16[9,48,128]{2,1,0:T(8,128)(2,1)S(1)}, u32[]{:S(2)}, u32[]{:S(2)}) collective-permute-start(bf16[9,48,128]{2,1,0:T(8,128)(2,1)S(1)} %get-tuple-element.31), channel_id=1, source_target_pairs={{0,16},{16,32},{32,48},{48,0},{1,17},{17,33},{33,49},{49,1},{2,18}... | collective-permute-start | bytes 331784 | tf_op jit(solution)/shard_map/ppermute | solution.py:48
  19.1 5.8 %collective-permute-start.3 = (bf16[9,48,128]{2,1,0:T(8,128)(2,1)S(1)}, bf16[9,48,128]{2,1,0:T(8,128)(2,1)S(1)}, u32[]{:S(2)}, u32[]{:S(2)}) collective-permute-start(bf16[9,48,128]{2,1,0:T(8,128)(2,1)S(1)} %get-tuple-element.32), channel_id=1, source_target_pairs={{0,48},{16,0},{32,16},{48,32},{1,49},{17,1},{33,17},{49,33},{2,50}... | collective-permute-start | bytes 331784 | tf_op jit(solution)/shard_map/ppermute | solution.py:48
  29.8 8.5 %collective-permute-start.5 = (bf16[9,80,128]{2,1,0:T(8,128)(2,1)S(1)}, bf16[9,80,128]{2,1,0:T(8,128)(2,1)S(1)}, u32[]{:S(2)}, u32[]{:S(2)}) collective-permute-start(bf16[9,80,128]{2,1,0:T(8,128)(2,1)S(1)} %get-tuple-element.34), channel_id=1, source_target_pairs={{0,15},{1,0},{2,1},{3,2},{4,3},{5,4},{6,5},{7,6},{8,7},{9,8},{10,9... | collective-permute-start | bytes 552968 | tf_op jit(solution)/shard_map/ppermute | solution.py:48
  42.2 5.9 %shard_map.71 = (f32[9,128,128]{2,1,0:T(8,128)S(1)}, f32[9,128,128]{2,1,0:T(8,128)S(1)}, f32[9,32,128]{2,1,0:T(8,128)S(1)}, f32[9,32,128]{2,1,0:T(8,128)S(1)}, bf16[432,16,128]{2,1,0:T(8,128)(2,1)S(1)}) custom-call(f32[4]{0:T(128)S(1)} %copy-done.4, s32[15,128]{1,0:T(8,128)S(1)} %add_select_fusion.16.slots, bf16[128,16,256]{2,1,0:T(8,128)(2,1)S(1)} %shard_map.68.rows, ...), custom_call_target="tpu_custom_call" | custom-call | flops 1073741824 | bytes 5332496 | tf_op jit(solution)/shard_map/pallas_call | solution.py:35
  48.1 5.3 %collective-permute-start.6 = (f32[9,32,128]{2,1,0:T(8,128)S(1)}, f32[9,32,128]{2,1,0:T(8,128)S(1)}, u32[]{:S(2)}, u32[]{:S(2)}) collective-permute-start(f32[9,32,128]{2,1,0:T(8,128)S(1)} %get-tuple-element.37), channel_id=1, source_target_pairs={{0,64},{64,128},{128,192},{192,256},{256,320},{320,384},{384,448},... | collective-permute-start | bytes 442376 | tf_op jit(solution)/shard_map/ppermute | solution.py:48
  53.5 4.2 %collective-permute-start.7 = (f32[9,32,128]{2,1,0:T(8,128)S(1)}, f32[9,32,128]{2,1,0:T(8,128)S(1)}, u32[]{:S(2)}, u32[]{:S(2)}) collective-permute-start(f32[9,32,128]{2,1,0:T(8,128)S(1)} %get-tuple-element.38), channel_id=1, source_target_pairs={{0,448},{64,0},{128,64},{192,128},{256,192},{320,256},{384,320},{4... | collective-permute-start | bytes 442376 | tf_op jit(solution)/shard_map/ppermute | solution.py:48
  59.4 3.0 %collective-permute-done.7.x_high.xh = f32[9,32,128]{2,1,0:T(8,128)S(1)} collective-permute-done((f32[9,32,128]{2,1,0:T(8,128)S(1)}, f32[9,32,128]{2,1,0:T(8,128)S(1)}, u32[]{:S(2)}, u32[]{:S(2)}) %collective-permute-start.7) | collective-permute-done | bytes 147488 | tf_op jit(solution)/shard_map/ppermute | solution.py:48
  62.7 3.0 %collective-permute-start.8 = (f32[9,48,128]{2,1,0:T(8,128)S(1)}, f32[9,48,128]{2,1,0:T(8,128)S(1)}, u32[]{:S(2)}, u32[]{:S(2)}) collective-permute-start(f32[9,48,128]{2,1,0:T(8,128)S(1)} %get-tuple-element.39), channel_id=1, source_target_pairs={{0,16},{16,32},{32,48},{48,0},{1,17},{17,33},{33,49},{49,1},{2,18}... | collective-permute-start | bytes 663560 | tf_op jit(solution)/shard_map/ppermute | solution.py:48
  68.5 4.4 %collective-permute-done.9.y_high.yh = f32[9,48,128]{2,1,0:T(8,128)S(1)} collective-permute-done((f32[9,48,128]{2,1,0:T(8,128)S(1)}, f32[9,48,128]{2,1,0:T(8,128)S(1)}, u32[]{:S(2)}, u32[]{:S(2)}) %collective-permute-start.9) | collective-permute-done | bytes 221216 | tf_op jit(solution)/shard_map/ppermute | solution.py:48
  75.0 5.1 %collective-permute-start.11 = (f32[9,72,128]{2,1,0:T(8,128)S(1)}, f32[9,72,128]{2,1,0:T(8,128)S(1)}, u32[]{:S(2)}, u32[]{:S(2)}) collective-permute-start(f32[9,72,128]{2,1,0:T(8,128)S(1)} %get-tuple-element.42), channel_id=1, source_target_pairs={{0,15},{1,0},{2,1},{3,2},{4,3},{5,4},{6,5},{7,6},{8,7},{9,8},{10,9... | collective-permute-start | bytes 995336 | tf_op jit(solution)/shard_map/ppermute | solution.py:48
  80.1 5.7 %collective-permute-done.10.zl = f32[9,72,128]{2,1,0:T(8,128)S(1)} collective-permute-done((f32[9,72,128]{2,1,0:T(8,128)S(1)}, f32[9,72,128]{2,1,0:T(8,128)S(1)}, u32[]{:S(2)}, u32[]{:S(2)}) %collective-permute-start.10) | collective-permute-done | bytes 331808 | tf_op jit(solution)/shard_map/ppermute | solution.py:48
  87.6 6.4 %shard_map.74 = (f32[9,128,128]{2,1,0:T(8,128)S(1)}, f32[9,128,128]{2,1,0:T(8,128)S(1)}, f32[9,32,128]{2,1,0:T(8,128)S(1)}, f32[9,32,128]{2,1,0:T(8,128)S(1)}) custom-call(f32[4]{0:T(128)S(1)} %copy-done.4, s32[15,128]{1,0:T(8,128)S(1)} %add_select_fusion.16.slots, bf16[128,16,256]{2,1,0:T(8,128)(2,1)S(1)} %shard_map.68.rows, ...), custom_call_target="tpu_custom_call" | custom-call | flops 1073741824 | bytes 5406224 | tf_op jit(solution)/shard_map/pallas_call | solution.py:35
  94.0 4.2 %collective-permute-start.12 = (f32[9,32,128]{2,1,0:T(8,128)S(1)}, f32[9,32,128]{2,1,0:T(8,128)S(1)}, u32[]{:S(2)}, u32[]{:S(2)}) collective-permute-start(f32[9,32,128]{2,1,0:T(8,128)S(1)} %get-tuple-element.46), channel_id=1, source_target_pairs={{0,64},{64,128},{128,192},{192,256},{256,320},{320,384},{384,448},... | collective-permute-start | bytes 442376 | tf_op jit(solution)/shard_map/ppermute | solution.py:48
  98.3 4.8 %collective-permute-start.13 = (f32[9,32,128]{2,1,0:T(8,128)S(1)}, f32[9,32,128]{2,1,0:T(8,128)S(1)}, u32[]{:S(2)}, u32[]{:S(2)}) collective-permute-start(f32[9,32,128]{2,1,0:T(8,128)S(1)} %get-tuple-element.47), channel_id=1, source_target_pairs={{0,448},{64,0},{128,64},{192,128},{256,192},{320,256},{384,320},{4... | collective-permute-start | bytes 442376 | tf_op jit(solution)/shard_map/ppermute | solution.py:48
  113.4 4.4 %collective-permute-done.15.y_high.yh = f32[9,48,128]{2,1,0:T(8,128)S(1)} collective-permute-done((f32[9,48,128]{2,1,0:T(8,128)S(1)}, f32[9,48,128]{2,1,0:T(8,128)S(1)}, u32[]{:S(2)}, u32[]{:S(2)}) %collective-permute-start.15) | collective-permute-done | bytes 221216 | tf_op jit(solution)/shard_map/ppermute | solution.py:48
  119.8 5.0 %collective-permute-start.17 = (f32[9,72,128]{2,1,0:T(8,128)S(1)}, f32[9,72,128]{2,1,0:T(8,128)S(1)}, u32[]{:S(2)}, u32[]{:S(2)}) collective-permute-start(f32[9,72,128]{2,1,0:T(8,128)S(1)} %get-tuple-element.51), channel_id=1, source_target_pairs={{0,15},{1,0},{2,1},{3,2},{4,3},{5,4},{6,5},{7,6},{8,7},{9,8},{10,9... | collective-permute-start | bytes 995336 | tf_op jit(solution)/shard_map/ppermute | solution.py:48
  124.9 5.9 %collective-permute-done.16.zl = f32[9,72,128]{2,1,0:T(8,128)S(1)} collective-permute-done((f32[9,72,128]{2,1,0:T(8,128)S(1)}, f32[9,72,128]{2,1,0:T(8,128)S(1)}, u32[]{:S(2)}, u32[]{:S(2)}) %collective-permute-start.16) | collective-permute-done | bytes 331808 | tf_op jit(solution)/shard_map/ppermute | solution.py:48
  132.4 12.7 %shard_map.77 = (f32[9,128,128]{2,1,0:T(8,128)}, f32[8,640]{1,0:T(8,128)S(1)}) custom-call(f32[4]{0:T(128)S(1)} %copy-done.4, s32[15,128]{1,0:T(8,128)S(1)} %add_select_fusion.16.slots, s32[15,128]{1,0:T(8,128)S(1)} %get-tuple-element.60.lanes, bf16[128,16,256]{2,1,0:T(8,128)(2,1)S(1)} %shard_map.68.rows, f32[9,128,128]{2,1,0:T(8,128)S(1)} %get-tuple-element.35.own.prev, ...), custom_call_target="tpu_custom_call" | custom-call | flops 2147483648 | bytes 7547152 | tf_op jit(solution)/shard_map/pallas_call | solution.py:35
  147.2 5.2 %collective-permute-start.18 = (f32[8,128]{1,0:T(8,128)S(1)}, f32[8,128]{1,0:T(8,128)S(1)}, u32[]{:S(2)}, u32[]{:S(2)}) collective-permute-start(f32[8,128]{1,0:T(8,128)S(1)} %get-tuple-element.66), channel_id=1, source_target_pairs={{0,15},{1,0},{2,1},{3,2},{4,3},{5,4},{6,5},{7,6},{8,7},{9,8},{10,9... | collective-permute-start | bytes 12296 | tf_op jit(solution)/shard_map/ppermute | solution.py:48
  153.4 3.2 %collective-permute-start.20 = (f32[8,128]{1,0:T(8,128)S(1)}, f32[8,128]{1,0:T(8,128)S(1)}, u32[]{:S(2)}, u32[]{:S(2)}) collective-permute-start(f32[8,128]{1,0:T(8,128)S(1)} %get-tuple-element.55), channel_id=1, source_target_pairs={{0,48},{16,0},{32,16},{48,32},{1,49},{17,1},{33,17},{49,33},{2,50}... | collective-permute-start | bytes 12296 | tf_op jit(solution)/shard_map/ppermute | solution.py:48
  160.0 7.2 %collective-permute-start.22 = (f32[8,128]{1,0:T(8,128)S(1)}, f32[8,128]{1,0:T(8,128)S(1)}, u32[]{:S(2)}, u32[]{:S(2)}) collective-permute-start(f32[8,128]{1,0:T(8,128)S(1)} %get-tuple-element.58), channel_id=1, source_target_pairs={{0,448},{64,0},{128,64},{192,128},{256,192},{320,256},{384,320},{4... | collective-permute-start | bytes 12296 | tf_op jit(solution)/shard_map/ppermute | solution.py:48
  169.1 6.0 %collective-permute-done.23.below = f32[8,128]{1,0:T(8,128)S(1)} collective-permute-done((f32[8,128]{1,0:T(8,128)S(1)}, f32[8,128]{1,0:T(8,128)S(1)}, u32[]{:S(2)}, u32[]{:S(2)}) %collective-permute-start.23) | collective-permute-done | bytes 4128 | tf_op jit(solution)/shard_map/ppermute | solution.py:48
  (51 shorter events, 44.7 us)
Async XLA Ops:
  1.6 9.9 %collective-permute-start = (bf16[9,32,128]{2,1,0:T(8,128)(2,1)S(1)}, bf16[9,32,128]{2,1,0:T(8,128)(2,1)S(1)}, u32[]{:S(2)}, u32[]{:S(2)}) collective-permute-start(bf16[9,32,128]{2,1,0:T(8,128)(2,1)S(1)} %bitcast.49), channel_id=1, source_target_pairs={{0,64},{64,128},{128,192},{192,256},{256,320},{320,384},{384,448},... | collective-permute-start | bytes 221192 | tf_op jit(solution)/shard_map/ppermute | solution.py:48
  7.1 6.6 %collective-permute-start.1 = (bf16[9,32,128]{2,1,0:T(8,128)(2,1)S(1)}, bf16[9,32,128]{2,1,0:T(8,128)(2,1)S(1)}, u32[]{:S(2)}, u32[]{:S(2)}) collective-permute-start(bf16[9,32,128]{2,1,0:T(8,128)(2,1)S(1)} %bitcast.48), channel_id=1, source_target_pairs={{0,448},{64,0},{128,64},{192,128},{256,192},{320,256},{384,320},{4... | collective-permute-start | bytes 221192 | tf_op jit(solution)/shard_map/ppermute | solution.py:48
  14.9 12.8 %collective-permute-start.2 = (bf16[9,48,128]{2,1,0:T(8,128)(2,1)S(1)}, bf16[9,48,128]{2,1,0:T(8,128)(2,1)S(1)}, u32[]{:S(2)}, u32[]{:S(2)}) collective-permute-start(bf16[9,48,128]{2,1,0:T(8,128)(2,1)S(1)} %get-tuple-element.31), channel_id=1, source_target_pairs={{0,16},{16,32},{32,48},{48,0},{1,17},{17,33},{33,49},{49,1},{2,18}... | collective-permute-start | bytes 331784 | tf_op jit(solution)/shard_map/ppermute | solution.py:48
  19.1 8.6 %collective-permute-start.3 = (bf16[9,48,128]{2,1,0:T(8,128)(2,1)S(1)}, bf16[9,48,128]{2,1,0:T(8,128)(2,1)S(1)}, u32[]{:S(2)}, u32[]{:S(2)}) collective-permute-start(bf16[9,48,128]{2,1,0:T(8,128)(2,1)S(1)} %get-tuple-element.32), channel_id=1, source_target_pairs={{0,48},{16,0},{32,16},{48,32},{1,49},{17,1},{33,17},{49,33},{2,50}... | collective-permute-start | bytes 331784 | tf_op jit(solution)/shard_map/ppermute | solution.py:48
  27.9 13.4 %collective-permute-start.4 = (bf16[9,80,128]{2,1,0:T(8,128)(2,1)S(1)}, bf16[9,80,128]{2,1,0:T(8,128)(2,1)S(1)}, u32[]{:S(2)}, u32[]{:S(2)}) collective-permute-start(bf16[9,80,128]{2,1,0:T(8,128)(2,1)S(1)} %get-tuple-element.33), channel_id=1, source_target_pairs={{0,1},{1,2},{2,3},{3,4},{4,5},{5,6},{6,7},{7,8},{8,9},{9,10},{10,1... | collective-permute-start | bytes 552968 | tf_op jit(solution)/shard_map/ppermute | solution.py:48
  29.8 12.4 %collective-permute-start.5 = (bf16[9,80,128]{2,1,0:T(8,128)(2,1)S(1)}, bf16[9,80,128]{2,1,0:T(8,128)(2,1)S(1)}, u32[]{:S(2)}, u32[]{:S(2)}) collective-permute-start(bf16[9,80,128]{2,1,0:T(8,128)(2,1)S(1)} %get-tuple-element.34), channel_id=1, source_target_pairs={{0,15},{1,0},{2,1},{3,2},{4,3},{5,4},{6,5},{7,6},{8,7},{9,8},{10,9... | collective-permute-start | bytes 552968 | tf_op jit(solution)/shard_map/ppermute | solution.py:48
  48.1 11.3 %collective-permute-start.6 = (f32[9,32,128]{2,1,0:T(8,128)S(1)}, f32[9,32,128]{2,1,0:T(8,128)S(1)}, u32[]{:S(2)}, u32[]{:S(2)}) collective-permute-start(f32[9,32,128]{2,1,0:T(8,128)S(1)} %get-tuple-element.37), channel_id=1, source_target_pairs={{0,64},{64,128},{128,192},{192,256},{256,320},{320,384},{384,448},... | collective-permute-start | bytes 442376 | tf_op jit(solution)/shard_map/ppermute | solution.py:48
  53.5 8.9 %collective-permute-start.7 = (f32[9,32,128]{2,1,0:T(8,128)S(1)}, f32[9,32,128]{2,1,0:T(8,128)S(1)}, u32[]{:S(2)}, u32[]{:S(2)}) collective-permute-start(f32[9,32,128]{2,1,0:T(8,128)S(1)} %get-tuple-element.38), channel_id=1, source_target_pairs={{0,448},{64,0},{128,64},{192,128},{256,192},{320,256},{384,320},{4... | collective-permute-start | bytes 442376 | tf_op jit(solution)/shard_map/ppermute | solution.py:48
  62.7 5.8 %collective-permute-start.8 = (f32[9,48,128]{2,1,0:T(8,128)S(1)}, f32[9,48,128]{2,1,0:T(8,128)S(1)}, u32[]{:S(2)}, u32[]{:S(2)}) collective-permute-start(f32[9,48,128]{2,1,0:T(8,128)S(1)} %get-tuple-element.39), channel_id=1, source_target_pairs={{0,16},{16,32},{32,48},{48,0},{1,17},{17,33},{33,49},{49,1},{2,18}... | collective-permute-start | bytes 663560 | tf_op jit(solution)/shard_map/ppermute | solution.py:48
  65.6 7.3 %collective-permute-start.9 = (f32[9,48,128]{2,1,0:T(8,128)S(1)}, f32[9,48,128]{2,1,0:T(8,128)S(1)}, u32[]{:S(2)}, u32[]{:S(2)}) collective-permute-start(f32[9,48,128]{2,1,0:T(8,128)S(1)} %get-tuple-element.40), channel_id=1, source_target_pairs={{0,48},{16,0},{32,16},{48,32},{1,49},{17,1},{33,17},{49,33},{2,50}... | collective-permute-start | bytes 663560 | tf_op jit(solution)/shard_map/ppermute | solution.py:48
  73.0 12.7 %collective-permute-start.10 = (f32[9,72,128]{2,1,0:T(8,128)S(1)}, f32[9,72,128]{2,1,0:T(8,128)S(1)}, u32[]{:S(2)}, u32[]{:S(2)}) collective-permute-start(f32[9,72,128]{2,1,0:T(8,128)S(1)} %get-tuple-element.41), channel_id=1, source_target_pairs={{0,1},{1,2},{2,3},{3,4},{4,5},{5,6},{6,7},{7,8},{8,9},{9,10},{10,1... | collective-permute-start | bytes 995336 | tf_op jit(solution)/shard_map/ppermute | solution.py:48
  75.0 12.6 %collective-permute-start.11 = (f32[9,72,128]{2,1,0:T(8,128)S(1)}, f32[9,72,128]{2,1,0:T(8,128)S(1)}, u32[]{:S(2)}, u32[]{:S(2)}) collective-permute-start(f32[9,72,128]{2,1,0:T(8,128)S(1)} %get-tuple-element.42), channel_id=1, source_target_pairs={{0,15},{1,0},{2,1},{3,2},{4,3},{5,4},{6,5},{7,6},{8,7},{9,8},{10,9... | collective-permute-start | bytes 995336 | tf_op jit(solution)/shard_map/ppermute | solution.py:48
  94.0 10.9 %collective-permute-start.12 = (f32[9,32,128]{2,1,0:T(8,128)S(1)}, f32[9,32,128]{2,1,0:T(8,128)S(1)}, u32[]{:S(2)}, u32[]{:S(2)}) collective-permute-start(f32[9,32,128]{2,1,0:T(8,128)S(1)} %get-tuple-element.46), channel_id=1, source_target_pairs={{0,64},{64,128},{128,192},{192,256},{256,320},{320,384},{384,448},... | collective-permute-start | bytes 442376 | tf_op jit(solution)/shard_map/ppermute | solution.py:48
  98.3 9.3 %collective-permute-start.13 = (f32[9,32,128]{2,1,0:T(8,128)S(1)}, f32[9,32,128]{2,1,0:T(8,128)S(1)}, u32[]{:S(2)}, u32[]{:S(2)}) collective-permute-start(f32[9,32,128]{2,1,0:T(8,128)S(1)} %get-tuple-element.47), channel_id=1, source_target_pairs={{0,448},{64,0},{128,64},{192,128},{256,192},{320,256},{384,320},{4... | collective-permute-start | bytes 442376 | tf_op jit(solution)/shard_map/ppermute | solution.py:48
  107.8 5.5 %collective-permute-start.14 = (f32[9,48,128]{2,1,0:T(8,128)S(1)}, f32[9,48,128]{2,1,0:T(8,128)S(1)}, u32[]{:S(2)}, u32[]{:S(2)}) collective-permute-start(f32[9,48,128]{2,1,0:T(8,128)S(1)} %get-tuple-element.48), channel_id=1, source_target_pairs={{0,16},{16,32},{32,48},{48,0},{1,17},{17,33},{33,49},{49,1},{2,18}... | collective-permute-start | bytes 663560 | tf_op jit(solution)/shard_map/ppermute | solution.py:48
  110.5 7.3 %collective-permute-start.15 = (f32[9,48,128]{2,1,0:T(8,128)S(1)}, f32[9,48,128]{2,1,0:T(8,128)S(1)}, u32[]{:S(2)}, u32[]{:S(2)}) collective-permute-start(f32[9,48,128]{2,1,0:T(8,128)S(1)} %get-tuple-element.49), channel_id=1, source_target_pairs={{0,48},{16,0},{32,16},{48,32},{1,49},{17,1},{33,17},{49,33},{2,50}... | collective-permute-start | bytes 663560 | tf_op jit(solution)/shard_map/ppermute | solution.py:48
  117.9 12.9 %collective-permute-start.16 = (f32[9,72,128]{2,1,0:T(8,128)S(1)}, f32[9,72,128]{2,1,0:T(8,128)S(1)}, u32[]{:S(2)}, u32[]{:S(2)}) collective-permute-start(f32[9,72,128]{2,1,0:T(8,128)S(1)} %get-tuple-element.50), channel_id=1, source_target_pairs={{0,1},{1,2},{2,3},{3,4},{4,5},{5,6},{6,7},{7,8},{8,9},{9,10},{10,1... | collective-permute-start | bytes 995336 | tf_op jit(solution)/shard_map/ppermute | solution.py:48
  119.8 12.6 %collective-permute-start.17 = (f32[9,72,128]{2,1,0:T(8,128)S(1)}, f32[9,72,128]{2,1,0:T(8,128)S(1)}, u32[]{:S(2)}, u32[]{:S(2)}) collective-permute-start(f32[9,72,128]{2,1,0:T(8,128)S(1)} %get-tuple-element.51), channel_id=1, source_target_pairs={{0,15},{1,0},{2,1},{3,2},{4,3},{5,4},{6,5},{7,6},{8,7},{9,8},{10,9... | collective-permute-start | bytes 995336 | tf_op jit(solution)/shard_map/ppermute | solution.py:48
  145.1 7.2 %collective-permute-start.19 = (f32[8,128]{1,0:T(8,128)S(1)}, f32[8,128]{1,0:T(8,128)S(1)}, u32[]{:S(2)}, u32[]{:S(2)}) collective-permute-start(f32[8,128]{1,0:T(8,128)S(1)} %get-tuple-element.65), channel_id=1, source_target_pairs={{0,1},{1,2},{2,3},{3,4},{4,5},{5,6},{6,7},{7,8},{8,9},{9,10},{10,1... | collective-permute-start | bytes 12296 | tf_op jit(solution)/shard_map/ppermute | solution.py:48
  147.2 5.9 %collective-permute-start.18 = (f32[8,128]{1,0:T(8,128)S(1)}, f32[8,128]{1,0:T(8,128)S(1)}, u32[]{:S(2)}, u32[]{:S(2)}) collective-permute-start(f32[8,128]{1,0:T(8,128)S(1)} %get-tuple-element.66), channel_id=1, source_target_pairs={{0,15},{1,0},{2,1},{3,2},{4,3},{5,4},{6,5},{7,6},{8,7},{9,8},{10,9... | collective-permute-start | bytes 12296 | tf_op jit(solution)/shard_map/ppermute | solution.py:48
  153.4 5.6 %collective-permute-start.20 = (f32[8,128]{1,0:T(8,128)S(1)}, f32[8,128]{1,0:T(8,128)S(1)}, u32[]{:S(2)}, u32[]{:S(2)}) collective-permute-start(f32[8,128]{1,0:T(8,128)S(1)} %get-tuple-element.55), channel_id=1, source_target_pairs={{0,48},{16,0},{32,16},{48,32},{1,49},{17,1},{33,17},{49,33},{2,50}... | collective-permute-start | bytes 12296 | tf_op jit(solution)/shard_map/ppermute | solution.py:48
  156.6 3.1 %collective-permute-start.21 = (f32[8,128]{1,0:T(8,128)S(1)}, f32[8,128]{1,0:T(8,128)S(1)}, u32[]{:S(2)}, u32[]{:S(2)}) collective-permute-start(f32[8,128]{1,0:T(8,128)S(1)} %get-tuple-element.56), channel_id=1, source_target_pairs={{0,16},{16,32},{32,48},{48,0},{1,17},{17,33},{33,49},{49,1},{2,18}... | collective-permute-start | bytes 12296 | tf_op jit(solution)/shard_map/ppermute | solution.py:48
  160.0 9.2 %collective-permute-start.22 = (f32[8,128]{1,0:T(8,128)S(1)}, f32[8,128]{1,0:T(8,128)S(1)}, u32[]{:S(2)}, u32[]{:S(2)}) collective-permute-start(f32[8,128]{1,0:T(8,128)S(1)} %get-tuple-element.58), channel_id=1, source_target_pairs={{0,448},{64,0},{128,64},{192,128},{256,192},{320,256},{384,320},{4... | collective-permute-start | bytes 12296 | tf_op jit(solution)/shard_map/ppermute | solution.py:48
  167.2 8.0 %collective-permute-start.23 = (f32[8,128]{1,0:T(8,128)S(1)}, f32[8,128]{1,0:T(8,128)S(1)}, u32[]{:S(2)}, u32[]{:S(2)}) collective-permute-start(f32[8,128]{1,0:T(8,128)S(1)} %get-tuple-element.59), channel_id=1, source_target_pairs={{0,64},{64,128},{128,192},{192,256},{256,320},{320,384},{384,448},... | collective-permute-start | bytes 12296 | tf_op jit(solution)/shard_map/ppermute | solution.py:48
  (5 other events, 109.0 us)
where the time goes:
time: 179 us; the launch traced here: 176 us
  starting transfers between devices  94.4 us (53%)
  waiting for transfers between devices  48.4 us (27%)
  Pallas kernels  28.4 us (16%)
  local copies, waits for them, and re-layouts  2.93 us (2%)
    ppermute x24, starting transfers between devices, shifted(): lax.ppermute(value, axis, [(i, (i + steps) % count) for i in range(count)])  94.4 us
    ppermute x24, waiting for transfers between devices, shifted(): lax.ppermute(value, axis, [(i, (i + steps) % count) for i in range(count)])  48.4 us
    pallas_call x13, Pallas kernels, call(): pl.pallas_call(kernel, out_shape=shapes, in_specs=in_specs, out_specs=[VM...  28.4 us
  transfers between devices with their start and end apart: 24, of which 18 were waited for; matrix products, arithmetic and copies ran while one was open for 0% of the time, Pallas kernels for 1%

commit v1 on v0

v1 whole, which is shorter than its diff:
```python
import functools

import jax
import jax.numpy as jnp
from jax import lax
from jax.experimental import pallas as pl
from jax.experimental.pallas import tpu as pltpu
from jax.sharding import PartitionSpec as P

CX = 4
CY = 4
CZ = 4
ORB = 9
NEIGH = 15
ATOMS = 2 * CX * CY * CZ
VECS = 128
NX = 2 * CY * CZ
NY = 2 * (CX + 2) * CZ
NZ = 2 * (CX + 2) * (CY + 2)
ROWS_X = ORB * NX + 16
ROWS_Y = ORB * NY + 16
ROWS_Z = ORB * NZ + 8
BEFORE_Y = ATOMS + 2 * NX
BEFORE_Z = BEFORE_Y + 2 * NY
SLOTS = BEFORE_Z + 2 * NZ
LANES_Z = 384
LANES = 640
F32 = jnp.float32
BF16 = jnp.bfloat16
VMEM = pl.BlockSpec(memory_space=pltpu.VMEM)
SMEM = pl.BlockSpec(memory_space=pltpu.SMEM)


def call(kernel, outs, in_specs, args, scratch=(), flops=0, mib=16):
    shapes = [jax.ShapeDtypeStruct(shape, dtype) for shape, dtype in outs]
    moved = sum(a.size * a.dtype.itemsize for a in args) + sum(s.size * s.dtype.itemsize for s in shapes)
    return pl.pallas_call(
        kernel,
        out_shape=shapes,
        in_specs=in_specs,
        out_specs=[VMEM] * len(shapes),
        scratch_shapes=list(scratch),
        compiler_params=pltpu.CompilerParams(vmem_limit_bytes=mib << 20),
        cost_estimate=pl.CostEstimate(flops=flops, bytes_accessed=moved, transcendentals=0),
    )(*args)


def swapped(value, axis, second):
    count = lax.axis_size(axis)
    pairs = [((k + second) % count, (k + 1 + second) % count) for k in range(0, count, 2)]
    return lax.ppermute(value, axis, pairs + [(b, a) for a, b in pairs])


def prep_kernel(ham, rows, turned, wide):
    turned[...] = jnp.zeros_like(turned)
    wide[...] = jnp.zeros_like(wide)
    for a in range(ORB):
        for b in range(ORB):
            turned[pl.ds(b, NEIGH, stride=16), :] = ham[a, b].astype(F32)
        flat = turned[...].T
        wide[0, pl.ds(a, ATOMS, stride=16), :] = flat[:, 0:128]
        wide[1, pl.ds(a, ATOMS, stride=16), :] = flat[:, 128:256]

    def pack(i, carry):
        at = pl.ds(pl.multiple_of(i * 16, 16), 16)
        rows[i, :, 0:128] = wide[0, at, :].astype(BF16)
        rows[i, :, 128:256] = wide[1, at, :].astype(BF16)
        return carry

    lax.fori_loop(0, ATOMS, pack, 0, unroll=8)


def scale_of(level):
    return jnp.exp2(level * 0.25) * (1.0 / 32767.0)


def packed_of(level):
    return jnp.exp2(level * -0.25) * 32767.0


def level_of(message):
    rows = message.shape[0]
    return message[rows - 16 : rows, :].astype(jnp.int32).astype(F32)[8:16]


def pack(plain, message, level):
    fixed = message.dtype == jnp.int16
    rows = message.shape[0]
    if fixed:
        factor = jnp.concatenate([packed_of(level)] * 2, axis=0)
    for t in range(0, rows, 16):
        value = plain[t : t + 16, :]
        if fixed:
            value = jnp.round(value * factor)
            if t == rows - 16:
                value = jnp.concatenate([value[0:8], level], axis=0)
            message[t : t + 16, :] = value.astype(jnp.int32).astype(jnp.int16)
        else:
            message[t : t + 16, :] = value.astype(BF16)


def unpack(message, plain):
    if message.dtype != jnp.int16:
        for t in range(0, message.shape[0], 16):
            plain[t : t + 16, :] = message[t : t + 16, :].astype(F32)
        return
    factor = jnp.concatenate([scale_of(level_of(message))] * 2, axis=0)
    for t in range(0, message.shape[0], 16):
        plain[t : t + 16, :] = message[t : t + 16, :].astype(jnp.int32).astype(F32) * factor


def highest(levels):
    return functools.reduce(jnp.maximum, levels)


def faces_y_kernel(parity, level, own, x1, x2, out1, out2, held, u1, u2, p1, p2):
    fixed = out1.dtype == jnp.int16
    unpack(x1, u1)
    unpack(x2, u2)
    even = parity[1] == 0
    p1[ROWS_Y - 16 :] = jnp.zeros((16, VECS), F32)
    p2[ROWS_Y - 16 :] = jnp.zeros((16, VECS), F32)
    for b in range(ORB):
        if fixed:
            take = [own[b, 16 * q : 16 * q + 16] for q in range(2 * CX)]
        else:
            held[...] = own[b].astype(F32)
            take = [held[16 * q : 16 * q + 16] for q in range(2 * CX)]
        take += [u[b * NX + 16 * q : b * NX + 16 * q + 16] for u in (u1, u2) for q in range(2)]
        for q, rows in enumerate(take):
            at = b * NY + 4 * q
            low, high = rows[0:4], rows[12:16]
            p1[at : at + 4] = jnp.where(even, high, low)
            p2[at : at + 4] = jnp.where(even, low, high)
    if fixed:
        level = highest([level[...], level_of(x1), level_of(x2)])
    pack(p1, out1, level)
    pack(p2, out2, level)


def faces_z_kernel(parity, level, own, x1, x2, y1, y2, out1, out2, held, u1, u2, v1, v2, p1, p2):
    fixed = out1.dtype == jnp.int16
    for message, plain in ((x1, u1), (x2, u2), (y1, v1), (y2, v2)):
        unpack(message, plain)
    even = parity[2] == 0
    p1[ROWS_Z - 8 :] = jnp.zeros((8, VECS), F32)
    p2[ROWS_Z - 8 :] = jnp.zeros((8, VECS), F32)
    ghosts = ((u1, NX), (u2, NX), (v1, NY), (v2, NY))
    for b in range(ORB):
        faces = []
        if not fixed:
            held[...] = own[b].astype(F32)
        for z in (0, CZ - 1):
            at = pl.ds(z, ATOMS // CZ, stride=CZ)
            faces.append([own[b, at, :] if fixed else held[at, :]])
            faces[-1] += [ref[pl.ds(b * rows + z, rows // CZ, stride=CZ), :] for ref, rows in ghosts]
        at = b * NZ
        for low, high in zip(*faces):
            rows = low.shape[0]
            p1[at : at + rows] = jnp.where(even, high, low)
            p2[at : at + rows] = jnp.where(even, low, high)
            at += rows
    if fixed:
        level = highest([level[...]] + [level_of(m) for m in (x1, x2, y1, y2)])
    pack(p1, out1, level)
    pack(p2, out2, level)


def load_tiles(own, ghosts, plains, loose):
    zero = jnp.zeros((8, VECS), F32)

    def clear(j, carry):
        loose[pl.ds(pl.multiple_of(j * 16 + 8, 8), 8), :] = zero
        return carry

    lax.fori_loop(0, SLOTS, clear, 0, unroll=16)
    for message, plain in zip(ghosts, plains):
        unpack(message, plain)
    counts = (NX, NX, NY, NY, NZ, NZ)
    for b in range(ORB):
        loose[pl.ds(b, ATOMS, stride=16), :] = own[b].astype(F32)
        base = ATOMS
        for plain, count in zip(plains, counts):
            loose[pl.ds(base * 16 + b, count, stride=16), :] = plain[b * count : b * count + count]
            base += count


def split_tiles(loose, tiles):
    def split(j, carry):
        value = loose[pl.ds(pl.multiple_of(j * 16, 16), 16), :]
        high = value.astype(BF16)
        tiles[j, :, 0:128] = high
        if tiles.shape[2] == 256:
            tiles[j, :, 128:256] = (value - high.astype(F32)).astype(BF16)
        return carry

    lax.fori_loop(0, SLOTS, split, 0, unroll=16)


def gather(slots, tiles, i):
    taken = [tiles[slots[m, i]] for m in range(NEIGH)]
    return jnp.concatenate(taken + taken[:1], axis=0)


def apply_atoms(slots, rows, tiles, applied):
    def atom(i, carry):
        product = jnp.dot(rows[i], gather(slots, tiles, i), preferred_element_type=F32)
        if tiles.shape[2] == 256:
            product = product[:, 0:128] + product[:, 128:256]
        applied[pl.ds(pl.multiple_of(i * 16, 16), 16), :] = product
        return carry

    lax.fori_loop(0, ATOMS, atom, 0, unroll=16)


def put_faces(parity, now, out1, out2, level, p1, p2):
    even = parity[0] == 0
    p1[ROWS_X - 16 :] = jnp.zeros((16, VECS), F32)
    p2[ROWS_X - 16 :] = jnp.zeros((16, VECS), F32)
    most = jnp.zeros((8, VECS), F32)
    for b in range(ORB):
        value = now[b]
        for row in range(0, ATOMS, 8):
            most = jnp.maximum(most, jnp.abs(value[row : row + 8]))
        for p in range(2):
            low, high = value[64 * p : 64 * p + 16], value[64 * p + 48 : 64 * p + 64]
            at = b * NX + 16 * p
            p1[at : at + 16] = jnp.where(even, high, low)
            p2[at : at + 16] = jnp.where(even, low, high)
    most = jnp.maximum(jnp.max(most, axis=0, keepdims=True), 1e-30)
    steps = jnp.ceil(jnp.log2(most) * 4.0 + 0.01)
    level[...] = jnp.broadcast_to(steps, (8, VECS))
    pack(p1, out1, level[...])
    pack(p2, out2, level[...])


def first_kernel(parity, coef, slots, rows, own, x1, x2, y1, y2, z1, z2, now, total, out1, out2, level, tiles,
                 loose, applied, p1, p2, *plains):
    load_tiles(own, (x1, x2, y1, y2, z1, z2), plains, loose)
    split_tiles(loose, tiles)
    apply_atoms(slots, rows, tiles, applied)
    for a in range(ORB):
        value = applied[pl.ds(a, ATOMS, stride=16), :]
        now[a] = value
        total[a] = coef[0] * own[a].astype(F32) + coef[1] * value
    put_faces(parity, now, out1, out2, level, p1, p2)


def second_kernel(parity, coef, slots, rows, prev, sum_in, own, x1, x2, y1, y2, z1, z2, now, total, out1, out2, level,
                  loose, tiles, applied, p1, p2, *plains):
    load_tiles(own, (x1, x2, y1, y2, z1, z2), plains, loose)
    split_tiles(loose, tiles)
    apply_atoms(slots, rows, tiles, applied)
    for a in range(ORB):
        value = 2.0 * applied[pl.ds(a, ATOMS, stride=16), :] - prev[a].astype(F32)
        now[a] = value
        total[a] = sum_in[a] + coef[2] * value
    put_faces(parity, now, out1, out2, level, p1, p2)


def third_kernel(coef, slots, lanes, rows, prev, sum_in, noise_tiles, deriv, own, x1, x2, y1, y2, z1, z2,
                 total, forces, loose, tiles, applied, dense, turned, stacked, *plains):
    load_tiles(own, (x1, x2, y1, y2, z1, z2), plains, loose)
    split_tiles(loose, tiles)
    apply_atoms(slots, rows, tiles, applied)
    for a in range(ORB):
        at = pl.ds(a, ATOMS, stride=16)
        value = sum_in[a] + coef[3] * (2.0 * applied[at, :] - prev[a])
        total[a] = value
        applied[at, :] = value

    def atom(i, carry):
        at = pl.ds(pl.multiple_of(i * 16, 16), 16)
        value = applied[at, :]
        high = value.astype(BF16)
        low = (value - high.astype(F32)).astype(BF16)
        product = lax.dot_general(
            jnp.concatenate([high, low], axis=0),
            gather(slots, noise_tiles, i),
            (((1,), (1,)), ((), ())),
            preferred_element_type=F32,
        )
        product = product[0:16] + product[16:32]
        dense[0, at, :] = product[:, 0:128]
        dense[1, at, :] = product[:, 128:256]
        return carry

    lax.fori_loop(0, ATOMS, atom, 0, unroll=16)
    pair = [jnp.zeros((NEIGH, ATOMS), F32) for _ in range(3)]
    for a in range(ORB):
        at = pl.ds(a, ATOMS, stride=16)
        turned[0:128] = dense[0, at, :].T
        turned[128:256] = dense[1, at, :].T
        for b in range(ORB):
            density = turned[pl.ds(b, NEIGH, stride=16), :]
            for c in range(3):
                pair[c] = pair[c] + deriv[c, a, b].astype(F32) * density
    others = lax.broadcasted_iota(jnp.int32, (NEIGH, ATOMS), 0) > 0
    stacked[...] = jnp.zeros_like(stacked)
    own_rows = []
    for c in range(3):
        value = jnp.where(others, pair[c] * (1.0 / VECS), 0.0)
        high = value.astype(BF16).astype(F32)
        stacked[pl.ds(c, NEIGH, stride=16), :] = high
        stacked[pl.ds(8 + c, NEIGH, stride=16), :] = value - high
        own_rows.append(jnp.sum(value, axis=0, keepdims=True))
    lane = lax.broadcasted_iota(jnp.int32, (LANES, ATOMS), 0)
    summed = jnp.zeros((16, LANES), F32)
    for m in range(1, NEIGH):
        hit = jnp.where(lane == lanes[m : m + 1, :], 1.0, 0.0).astype(BF16)
        summed = summed + lax.dot_general(
            stacked[16 * m : 16 * m + 16].astype(BF16), hit, (((1,), (1,)), ((), ())), preferred_element_type=F32
        )
    forces[...] = summed[0:8] + summed[8:16]
    for c in range(3):
        forces[c : c + 1, 0:ATOMS] = forces[c : c + 1, 0:ATOMS] - own_rows[c]


def spread(value, place, width):
    row = lax.broadcasted_iota(jnp.int32, (VECS, width), 0)
    lane = lax.broadcasted_iota(jnp.int32, (VECS, width), 1)
    hit = jnp.where((lane == place(row)), 1.0, 0.0)
    return jnp.dot(value, hit, precision=lax.Precision.HIGHEST, preferred_element_type=F32)


def place_z(z):
    return lambda r: jnp.where(r < NZ, 4 * r + z, -1)


def place_y(y):
    return lambda r: jnp.where(r < NY, (r >> 2) * 16 + 4 * y + (r & 3), -1)


def place_x(x):
    return lambda r: jnp.where(r < NX, (r >> 4) * 64 + 16 * x + (r & 15), -1)


def merged(held, from1, from2, place, top, parity, width):
    plane1 = jnp.where(parity == 0, top, 0)
    return held[:, 0:width] + spread(from1[...], place(plane1), width) + spread(from2[...], place(top - plane1), width)


def merge_z_kernel(parity, held, from1, from2, out, out1, out2):
    out[...] = merged(held, from1, from2, place_z, CZ - 1, parity[2], LANES_Z)
    out1[...] = jnp.zeros_like(out1)
    out2[...] = jnp.zeros_like(out2)
    out1[:, 0:NY] = out[:, BEFORE_Y : BEFORE_Y + NY]
    out2[:, 0:NY] = out[:, BEFORE_Y + NY : BEFORE_Z]


def merge_y_kernel(parity, held, from1, from2, out, out1, out2):
    out[...] = merged(held, from1, from2, place_y, CY - 1, parity[1], 256)
    out1[...] = jnp.zeros_like(out1)
    out2[...] = jnp.zeros_like(out2)
    out1[:, 0:NX] = out[:, ATOMS : ATOMS + NX]
    out2[:, 0:NX] = out[:, ATOMS + NX : BEFORE_Y]


def merge_x_kernel(parity, held, from1, from2, out):
    out[...] = merged(held, from1, from2, place_x, CX - 1, parity[0], ATOMS)[0:3]


def slots_of(neighbours, parity):
    cells = CX * CY * CZ
    size_x, size_y, size_z = (lax.axis_size(axis) for axis in ("gx", "gy", "gz"))
    partner = neighbours.T
    domain = partner // ATOMS
    within = partner % ATOMS
    basis = within // cells
    remain = within % cells
    ex = domain // (size_y * size_z) * CX + remain // (CY * CZ) - lax.axis_index("gx") * CX + 1
    ey = domain // size_z % size_y * CY + remain // CZ % CY - lax.axis_index("gy") * CY + 1
    ez = domain % size_z * CZ + remain % CZ - lax.axis_index("gz") * CZ + 1
    ex = jnp.remainder(ex, CX * size_x)
    ey = jnp.remainder(ey, CY * size_y)
    ez = jnp.remainder(ez, CZ * size_z)
    x_out = (ex == 0) | (ex == CX + 1)
    y_out = (ey == 0) | (ey == CY + 1)
    z_out = (ez == 0) | (ez == CZ + 1)
    x_trade = ((ex == 0) == (parity[0] == 0)).astype(jnp.int32)
    y_trade = ((ey == 0) == (parity[1] == 0)).astype(jnp.int32)
    z_trade = ((ez == 0) == (parity[2] == 0)).astype(jnp.int32)
    q = jnp.where(x_out, 2 * CX + 2 * x_trade + basis, basis * CX + ex - 1)
    r_in = q * CY + ey - 1
    r_out = 2 * (CX + 2) * CY + y_trade * (2 * (CX + 2)) + q
    r = jnp.where(y_out, r_out, r_in)
    slots = jnp.where(z_out, BEFORE_Z + z_trade * NZ + r, r * CZ + ez - 1)
    lanes = jnp.where(z_out, LANES_Z + z_trade * 128 + r, r * CZ + ez - 1)
    return slots.astype(jnp.int32), lanes.astype(jnp.int32)


def plain(rows):
    return pltpu.VMEM((rows, VECS), F32)


GHOST_PLAINS = [plain(r) for r in (ROWS_X, ROWS_X, ROWS_Y, ROWS_Y, ROWS_Z, ROWS_Z)]


def exchange(parity, level, own, out1, out2):
    dtype = out1.dtype
    x1, x2 = swapped(out1, "gx", 0), swapped(out2, "gx", 1)
    out1, out2 = call(
        faces_y_kernel, [((ROWS_Y, VECS), dtype)] * 2, [SMEM] + [VMEM] * 4, (parity, level, own, x1, x2),
        [plain(ATOMS), plain(ROWS_X), plain(ROWS_X), plain(ROWS_Y), plain(ROWS_Y)],
    )
    y1, y2 = swapped(out1, "gy", 0), swapped(out2, "gy", 1)
    out1, out2 = call(
        faces_z_kernel, [((ROWS_Z, VECS), dtype)] * 2, [SMEM] + [VMEM] * 6, (parity, level, own, x1, x2, y1, y2),
        [plain(ATOMS)] + GHOST_PLAINS,
    )
    z1, z2 = swapped(out1, "gz", 0), swapped(out2, "gz", 1)
    return x1, x2, y1, y2, z1, z2


def shards(noise_vectors, hamiltonian, derivative, neighbours, coefficients):
    parity = jnp.stack([lax.axis_index(axis) % 2 for axis in ("gx", "gy", "gz")]).astype(jnp.int32)
    slots, lanes = slots_of(neighbours, parity)
    lattice = noise_vectors.reshape(ORB, 2, CX, CY * CZ, VECS)
    low = lattice[:, :, 0].reshape(ORB * NX, VECS)
    high = lattice[:, :, CX - 1].reshape(ORB * NX, VECS)
    room = jnp.zeros((16, VECS), BF16)
    even = parity[0] == 0
    out1 = jnp.concatenate([jnp.where(even, high, low), room])
    out2 = jnp.concatenate([jnp.where(even, low, high), room])
    (rows,) = call(
        prep_kernel, [((ATOMS, 16, 256), BF16)], [VMEM], (hamiltonian.transpose(1, 2, 0, 3),),
        [plain(256), pltpu.VMEM((2, ATOMS * 16, 128), F32)], flops=1 << 22,
    )
    whole = ((ORB, ATOMS, VECS), F32)
    plane = ((ROWS_X, VECS), jnp.int16)
    tile = ((8, 128), F32)
    loose = plain(SLOTS * 16)
    applied = plain(ATOMS * 16)
    split = pltpu.VMEM((SLOTS, 16, 256), BF16)
    ghosts = exchange(parity, jnp.zeros((8, VECS), F32), noise_vectors, out1, out2)
    first, total, out1, out2, level, noise_tiles = call(
        first_kernel, [whole, whole, plane, plane, tile, ((SLOTS, 16, VECS), BF16)], [SMEM] * 3 + [VMEM] * 8,
        (parity, coefficients, slots, rows, noise_vectors) + ghosts,
        [loose, applied, plain(ROWS_X), plain(ROWS_X)] + GHOST_PLAINS, flops=1 << 30, mib=24,
    )
    ghosts = exchange(parity, level, first, out1, out2)
    second, total, out1, out2, level = call(
        second_kernel, [whole, whole, plane, plane, tile], [SMEM] * 3 + [VMEM] * 10,
        (parity, coefficients, slots, rows, noise_vectors, total, first) + ghosts,
        [loose, split, applied, plain(ROWS_X), plain(ROWS_X)] + GHOST_PLAINS, flops=1 << 30, mib=24,
    )
    ghosts = exchange(parity, level, second, out1, out2)
    weighted, held = call(
        third_kernel, [whole, ((8, LANES), F32)], [SMEM] * 2 + [VMEM] * 13,
        (coefficients, slots, lanes, rows, first, total, noise_tiles, derivative.transpose(0, 2, 3, 1, 4), second) + ghosts,
        [loose, split, applied, pltpu.VMEM((2, ATOMS * 16, 128), F32), plain(256), plain(NEIGH * 16)] + GHOST_PLAINS,
        flops=1 << 31, mib=32,
    )
    out1, out2 = held[:, LANES_Z : LANES_Z + 128], held[:, LANES_Z + 128 :]
    from1, from2 = swapped(out1, "gz", 0), swapped(out2, "gz", 1)
    held, out1, out2 = call(
        merge_z_kernel, [((8, LANES_Z), F32), tile, tile], [SMEM] + [VMEM] * 3, (parity, held, from1, from2)
    )
    from1, from2 = swapped(out1, "gy", 0), swapped(out2, "gy", 1)
    held, out1, out2 = call(
        merge_y_kernel, [((8, 256), F32), tile, tile], [SMEM] + [VMEM] * 3, (parity, held, from1, from2)
    )
    from1, from2 = swapped(out1, "gx", 0), swapped(out2, "gx", 1)
    (forces,) = call(merge_x_kernel, [((3, ATOMS), F32)], [SMEM] + [VMEM] * 3, (parity, held, from1, from2))
    return weighted, forces


def solution(mesh):
    in_specs = (
        P(None, ("gx", "gy", "gz"), None),
        P(None, None, None, ("gx", "gy", "gz")),
        P(None, None, None, None, ("gx", "gy", "gz")),
        P(("gx", "gy", "gz"), None),
        P(),
    )
    out_specs = (P(None, ("gx", "gy", "gz"), None), P(None, ("gx", "gy", "gz")))
    return jax.shard_map(shards, mesh=mesh, in_specs=in_specs, out_specs=out_specs, check_vma=False)
```

time: 179 us -> 173 us (0.966); the launches traced: 176 us -> 172 us
  Pallas kernels: 28.4 us -> 33.5 us
  starting transfers between devices: 94.4 us -> 89.5 us
  waiting for transfers between devices: 48.4 us -> 46.2 us
  local copies, waits for them, and re-layouts: 2.93 us -> 1 us
    pallas_call x13, Pallas kernels: 28.4 us -> 33.5 us  [call(): pl.pallas_call(kernel, out_shape=shapes, in_specs=in_specs, out_specs=[VM...]
    ppermute x24, starting transfers between devices: 94.4 us -> 89.5 us  [swapped(): return lax.ppermute(value, axis, pairs + [(b, a) for a, b in pairs])]
    ppermute x24, waiting for transfers between devices: 48.4 us -> 46.2 us  [swapped(): return lax.ppermute(value, axis, pairs + [(b, a) for a, b in pairs])]
  transfers between devices with their start and end apart: 24 -> 24, of which waited for: 18 -> 14; matrix products, arithmetic and copies ran while one was open for 0% -> 0% of each run, Pallas kernels for 1% -> 1%
where the time goes in v1:
time: 173 us; the launch traced here: 172 us
  starting transfers between devices  89.5 us (52%)
  waiting for transfers between devices  46.2 us (27%)
  Pallas kernels  33.5 us (19%)
    ppermute x24, starting transfers between devices, swapped(): return lax.ppermute(value, axis, pairs + [(b, a) for a, b in pairs])  89.5 us
    ppermute x24, waiting for transfers between devices, swapped(): return lax.ppermute(value, axis, pairs + [(b, a) for a, b in pairs])  46.2 us
    pallas_call x13, Pallas kernels, call(): pl.pallas_call(kernel, out_shape=shapes, in_specs=in_specs, out_specs=[VM...  33.5 us
  transfers between devices with their start and end apart: 24, of which 14 were waited for; matrix products, arithmetic and copies ran while one was open for 0% of the time, Pallas kernels for 1%

profile of v1, /device:TPU:1, one launch (start us, length us, event | category | flops | bytes accessed | tf_op | source)
XLA Modules:
  0.0 172.5 jit_solution(11995473777456838399)
XLA Ops:
  1.7 7.9 %collective-permute-start.1 = (bf16[304,128]{1,0:T(8,128)(2,1)S(1)}, bf16[304,128]{1,0:T(8,128)(2,1)S(1)}, u32[]{:S(2)}, u32[]{:S(2)}) collective-permute-start(bf16[304,128]{1,0:T(8,128)(2,1)S(1)} %concatenate.7), channel_id=1, source_target_pairs={{64,128},{192,256},{320,384},{448,0},{128,64},{256,192},{384,320},... | collective-permute-start | bytes 233480 | tf_op jit(solution)/shard_map/ppermute | solution.py:51
  17.0 4.1 %collective-permute-start.2 = (bf16[448,128]{1,0:T(8,128)(2,1)S(1)}, bf16[448,128]{1,0:T(8,128)(2,1)S(1)}, u32[]{:S(2)}, u32[]{:S(2)}) collective-permute-start(bf16[448,128]{1,0:T(8,128)(2,1)S(1)} %get-tuple-element.33), channel_id=1, source_target_pairs={{0,16},{32,48},{16,0},{48,32},{1,17},{33,49},{17,1},{49,33},{2,18}... | collective-permute-start | bytes 344072 | tf_op jit(solution)/shard_map/ppermute | solution.py:51
  23.2 4.5 %collective-permute-done.3.y2 = bf16[448,128]{1,0:T(8,128)(2,1)S(1)} collective-permute-done((bf16[448,128]{1,0:T(8,128)(2,1)S(1)}, bf16[448,128]{1,0:T(8,128)(2,1)S(1)}, u32[]{:S(2)}, u32[]{:S(2)}) %collective-permute-start.3) | collective-permute-done | bytes 114720 | tf_op jit(solution)/shard_map/ppermute | solution.py:51
  28.4 3.5 %collective-permute-start.4 = (bf16[656,128]{1,0:T(8,128)(2,1)S(1)}, bf16[656,128]{1,0:T(8,128)(2,1)S(1)}, u32[]{:S(2)}, u32[]{:S(2)}) collective-permute-start(bf16[656,128]{1,0:T(8,128)(2,1)S(1)} %get-tuple-element.35), channel_id=1, source_target_pairs={{0,1},{2,3},{4,5},{6,7},{8,9},{10,11},{12,13},{14,15},{1,0},{3,2},... | collective-permute-start | bytes 503816 | tf_op jit(solution)/shard_map/ppermute | solution.py:51
  31.9 10.2 %collective-permute-start.5 = (bf16[656,128]{1,0:T(8,128)(2,1)S(1)}, bf16[656,128]{1,0:T(8,128)(2,1)S(1)}, u32[]{:S(2)}, u32[]{:S(2)}) collective-permute-start(bf16[656,128]{1,0:T(8,128)(2,1)S(1)} %get-tuple-element.36), channel_id=1, source_target_pairs={{1,2},{3,4},{5,6},{7,8},{9,10},{11,12},{13,14},{15,0},{2,1},{4,3},... | collective-permute-start | bytes 503816 | tf_op jit(solution)/shard_map/ppermute | solution.py:51
  42.2 4.4 %collective-permute-done.5.z2 = bf16[656,128]{1,0:T(8,128)(2,1)S(1)} collective-permute-done((bf16[656,128]{1,0:T(8,128)(2,1)S(1)}, bf16[656,128]{1,0:T(8,128)(2,1)S(1)}, u32[]{:S(2)}, u32[]{:S(2)}) %collective-permute-start.5) | collective-permute-done | bytes 167968 | tf_op jit(solution)/shard_map/ppermute | solution.py:51
  46.5 6.2 %shard_map.71 = (f32[9,128,128]{2,1,0:T(8,128)S(1)}, f32[9,128,128]{2,1,0:T(8,128)S(1)}, s16[304,128]{1,0:T(8,128)(2,1)S(1)}, s16[304,128]{1,0:T(8,128)(2,1)S(1)...) custom-call(s32[3]{0:T(128)S(1)} %pad_add_fusion.parity, f32[4]{0:T(128)S(1)} %copy-done.3, ...), custom_call_target="tpu_custom_call" | custom-call | flops 1073741824 | bytes 5180956 | tf_op jit(solution)/shard_map/pallas_call | solution.py:37
  54.6 5.0 %collective-permute-start.7 = (s16[304,128]{1,0:T(8,128)(2,1)S(1)}, s16[304,128]{1,0:T(8,128)(2,1)S(1)}, u32[]{:S(2)}, u32[]{:S(2)}) collective-permute-start(s16[304,128]{1,0:T(8,128)(2,1)S(1)} %get-tuple-element.40), channel_id=1, source_target_pairs={{64,128},{192,256},{320,384},{448,0},{128,64},{256,192},{384,320},... | collective-permute-start | bytes 233480 | tf_op jit(solution)/shard_map/ppermute | solution.py:51
  59.7 3.7 %collective-permute-done.7.x2 = s16[304,128]{1,0:T(8,128)(2,1)S(1)} collective-permute-done((s16[304,128]{1,0:T(8,128)(2,1)S(1)}, s16[304,128]{1,0:T(8,128)(2,1)S(1)}, u32[]{:S(2)}, u32[]{:S(2)}) %collective-permute-start.7) | collective-permute-done | bytes 77856 | tf_op jit(solution)/shard_map/ppermute | solution.py:51
  64.1 3.9 %collective-permute-start.8 = (s16[448,128]{1,0:T(8,128)(2,1)S(1)}, s16[448,128]{1,0:T(8,128)(2,1)S(1)}, u32[]{:S(2)}, u32[]{:S(2)}) collective-permute-start(s16[448,128]{1,0:T(8,128)(2,1)S(1)} %get-tuple-element.42), channel_id=1, source_target_pairs={{0,16},{32,48},{16,0},{48,32},{1,17},{33,49},{17,1},{49,33},{2,18}... | collective-permute-start | bytes 344072 | tf_op jit(solution)/shard_map/ppermute | solution.py:51
  70.1 4.5 %collective-permute-done.9.y2 = s16[448,128]{1,0:T(8,128)(2,1)S(1)} collective-permute-done((s16[448,128]{1,0:T(8,128)(2,1)S(1)}, s16[448,128]{1,0:T(8,128)(2,1)S(1)}, u32[]{:S(2)}, u32[]{:S(2)}) %collective-permute-start.9) | collective-permute-done | bytes 114720 | tf_op jit(solution)/shard_map/ppermute | solution.py:51
  77.4 4.6 %collective-permute-start.11 = (s16[656,128]{1,0:T(8,128)(2,1)S(1)}, s16[656,128]{1,0:T(8,128)(2,1)S(1)}, u32[]{:S(2)}, u32[]{:S(2)}) collective-permute-start(s16[656,128]{1,0:T(8,128)(2,1)S(1)} %get-tuple-element.45), channel_id=1, source_target_pairs={{1,2},{3,4},{5,6},{7,8},{9,10},{11,12},{13,14},{15,0},{2,1},{4,3},... | collective-permute-start | bytes 503816 | tf_op jit(solution)/shard_map/ppermute | solution.py:51
  83.2 3.1 %collective-permute-done.11.z2 = s16[656,128]{1,0:T(8,128)(2,1)S(1)} collective-permute-done((s16[656,128]{1,0:T(8,128)(2,1)S(1)}, s16[656,128]{1,0:T(8,128)(2,1)S(1)}, u32[]{:S(2)}, u32[]{:S(2)}) %collective-permute-start.11) | collective-permute-done | bytes 167968 | tf_op jit(solution)/shard_map/ppermute | solution.py:51
  86.3 6.6 %shard_map.74 = (f32[9,128,128]{2,1,0:T(8,128)S(1)}, f32[9,128,128]{2,1,0:T(8,128)S(1)}, s16[304,128]{1,0:T(8,128)(2,1)S(1)}, s16[304,128]{1,0:T(8,128)(2,1)S(1)}, f32[8,128]{1,0:T(8,128)S(1)}) custom-call(s32[3]{0:T(128)S(1)} %pad_add_fusion.parity, f32[4]{0:T(128)S(1)} %copy-done.3, s32[15,128]{1,0:T(8,128)S(1)} %add_select_fusion.16.slots, ...), custom_call_target="tpu_custom_call" | custom-call | flops 1073741824 | bytes 4591132 | tf_op jit(solution)/shard_map/pallas_call | solution.py:37
  92.9 3.9 %collective-permute-start.12 = (s16[304,128]{1,0:T(8,128)(2,1)S(1)}, s16[304,128]{1,0:T(8,128)(2,1)S(1)}, u32[]{:S(2)}, u32[]{:S(2)}) collective-permute-start(s16[304,128]{1,0:T(8,128)(2,1)S(1)} %get-tuple-element.49), channel_id=1, source_target_pairs={{0,64},{128,192},{256,320},{384,448},{64,0},{192,128},{320,256},{4... | collective-permute-start | bytes 233480 | tf_op jit(solution)/shard_map/ppermute | solution.py:51
  96.8 3.3 %collective-permute-start.13 = (s16[304,128]{1,0:T(8,128)(2,1)S(1)}, s16[304,128]{1,0:T(8,128)(2,1)S(1)}, u32[]{:S(2)}, u32[]{:S(2)}) collective-permute-start(s16[304,128]{1,0:T(8,128)(2,1)S(1)} %get-tuple-element.50), channel_id=1, source_target_pairs={{64,128},{192,256},{320,384},{448,0},{128,64},{256,192},{384,320},... | collective-permute-start | bytes 233480 | tf_op jit(solution)/shard_map/ppermute | solution.py:51
  100.2 5.4 %collective-permute-done.13.x2 = s16[304,128]{1,0:T(8,128)(2,1)S(1)} collective-permute-done((s16[304,128]{1,0:T(8,128)(2,1)S(1)}, s16[304,128]{1,0:T(8,128)(2,1)S(1)}, u32[]{:S(2)}, u32[]{:S(2)}) %collective-permute-start.13) | collective-permute-done | bytes 77856 | tf_op jit(solution)/shard_map/ppermute | solution.py:51
  106.3 4.2 %collective-permute-start.14 = (s16[448,128]{1,0:T(8,128)(2,1)S(1)}, s16[448,128]{1,0:T(8,128)(2,1)S(1)}, u32[]{:S(2)}, u32[]{:S(2)}) collective-permute-start(s16[448,128]{1,0:T(8,128)(2,1)S(1)} %get-tuple-element.52), channel_id=1, source_target_pairs={{0,16},{32,48},{16,0},{48,32},{1,17},{33,49},{17,1},{49,33},{2,18}... | collective-permute-start | bytes 344072 | tf_op jit(solution)/shard_map/ppermute | solution.py:51
  112.6 4.5 %collective-permute-done.15.y2 = s16[448,128]{1,0:T(8,128)(2,1)S(1)} collective-permute-done((s16[448,128]{1,0:T(8,128)(2,1)S(1)}, s16[448,128]{1,0:T(8,128)(2,1)S(1)}, u32[]{:S(2)}, u32[]{:S(2)}) %collective-permute-start.15) | collective-permute-done | bytes 114720 | tf_op jit(solution)/shard_map/ppermute | solution.py:51
  120.1 4.6 %collective-permute-start.17 = (s16[656,128]{1,0:T(8,128)(2,1)S(1)}, s16[656,128]{1,0:T(8,128)(2,1)S(1)}, u32[]{:S(2)}, u32[]{:S(2)}) collective-permute-start(s16[656,128]{1,0:T(8,128)(2,1)S(1)} %get-tuple-element.55), channel_id=1, source_target_pairs={{1,2},{3,4},{5,6},{7,8},{9,10},{11,12},{13,14},{15,0},{2,1},{4,3},... | collective-permute-start | bytes 503816 | tf_op jit(solution)/shard_map/ppermute | solution.py:51
  128.7 12.6 %shard_map.77 = (f32[9,128,128]{2,1,0:T(8,128)}, f32[8,640]{1,0:T(8,128)S(1)}) custom-call(f32[4]{0:T(128)S(1)} %copy-done.3, s32[15,128]{1,0:T(8,128)S(1)} %add_select_fusion.16.slots, s32[15,128]{1,0:T(8,128)S(1)} %get-tuple-element.64.lanes, bf16[128,16,256]{2,1,0:T(8,128)(2,1)S(1)} %shard_map.68.rows, f32[9,128,128]{2,1,0:T(8,128)S(1)} %get-tuple-element.37.own.prev, ...), custom_call_target="tpu_custom_call" | custom-call | flops 2147483648 | bytes 6867216 | tf_op jit(solution)/shard_map/pallas_call | solution.py:37
  141.3 4.6 %collective-permute-start.19 = (f32[8,128]{1,0:T(8,128)S(1)}, f32[8,128]{1,0:T(8,128)S(1)}, u32[]{:S(2)}, u32[]{:S(2)}) collective-permute-start(f32[8,128]{1,0:T(8,128)S(1)} %get-tuple-element.69), channel_id=1, source_target_pairs={{1,2},{3,4},{5,6},{7,8},{9,10},{11,12},{13,14},{15,0},{2,1},{4,3},... | collective-permute-start | bytes 12296 | tf_op jit(solution)/shard_map/ppermute | solution.py:51
  151.1 4.5 %collective-permute-start.20 = (f32[8,128]{1,0:T(8,128)S(1)}, f32[8,128]{1,0:T(8,128)S(1)}, u32[]{:S(2)}, u32[]{:S(2)}) collective-permute-start(f32[8,128]{1,0:T(8,128)S(1)} %get-tuple-element.59), channel_id=1, source_target_pairs={{0,16},{32,48},{16,0},{48,32},{1,17},{33,49},{17,1},{49,33},{2,18}... | collective-permute-start | bytes 12296 | tf_op jit(solution)/shard_map/ppermute | solution.py:51
  163.2 5.0 %collective-permute-start.23 = (f32[8,128]{1,0:T(8,128)S(1)}, f32[8,128]{1,0:T(8,128)S(1)}, u32[]{:S(2)}, u32[]{:S(2)}) collective-permute-start(f32[8,128]{1,0:T(8,128)S(1)} %get-tuple-element.63), channel_id=1, source_target_pairs={{64,128},{192,256},{320,384},{448,0},{128,64},{256,192},{384,320},... | collective-permute-start | bytes 12296 | tf_op jit(solution)/shard_map/ppermute | solution.py:51
  (55 shorter events, 46.6 us)
Async XLA Ops:
  1.7 12.0 %collective-permute-start.1 = (bf16[304,128]{1,0:T(8,128)(2,1)S(1)}, bf16[304,128]{1,0:T(8,128)(2,1)S(1)}, u32[]{:S(2)}, u32[]{:S(2)}) collective-permute-start(bf16[304,128]{1,0:T(8,128)(2,1)S(1)} %concatenate.7), channel_id=1, source_target_pairs={{64,128},{192,256},{320,384},{448,0},{128,64},{256,192},{384,320},... | collective-permute-start | bytes 233480 | tf_op jit(solution)/shard_map/ppermute | solution.py:51
  9.6 6.6 %collective-permute-start = (bf16[304,128]{1,0:T(8,128)(2,1)S(1)}, bf16[304,128]{1,0:T(8,128)(2,1)S(1)}, u32[]{:S(2)}, u32[]{:S(2)}) collective-permute-start(bf16[304,128]{1,0:T(8,128)(2,1)S(1)} %concatenate.6), channel_id=1, source_target_pairs={{0,64},{128,192},{256,320},{384,448},{64,0},{192,128},{320,256},{4... | collective-permute-start | bytes 233480 | tf_op jit(solution)/shard_map/ppermute | solution.py:51
  17.0 6.2 %collective-permute-start.2 = (bf16[448,128]{1,0:T(8,128)(2,1)S(1)}, bf16[448,128]{1,0:T(8,128)(2,1)S(1)}, u32[]{:S(2)}, u32[]{:S(2)}) collective-permute-start(bf16[448,128]{1,0:T(8,128)(2,1)S(1)} %get-tuple-element.33), channel_id=1, source_target_pairs={{0,16},{32,48},{16,0},{48,32},{1,17},{33,49},{17,1},{49,33},{2,18}... | collective-permute-start | bytes 344072 | tf_op jit(solution)/shard_map/ppermute | solution.py:51
  21.1 6.7 %collective-permute-start.3 = (bf16[448,128]{1,0:T(8,128)(2,1)S(1)}, bf16[448,128]{1,0:T(8,128)(2,1)S(1)}, u32[]{:S(2)}, u32[]{:S(2)}) collective-permute-start(bf16[448,128]{1,0:T(8,128)(2,1)S(1)} %get-tuple-element.34), channel_id=1, source_target_pairs={{16,32},{48,0},{32,16},{0,48},{17,33},{49,1},{33,17},{1,49},{18,34... | collective-permute-start | bytes 344072 | tf_op jit(solution)/shard_map/ppermute | solution.py:51
  28.4 13.7 %collective-permute-start.4 = (bf16[656,128]{1,0:T(8,128)(2,1)S(1)}, bf16[656,128]{1,0:T(8,128)(2,1)S(1)}, u32[]{:S(2)}, u32[]{:S(2)}) collective-permute-start(bf16[656,128]{1,0:T(8,128)(2,1)S(1)} %get-tuple-element.35), channel_id=1, source_target_pairs={{0,1},{2,3},{4,5},{6,7},{8,9},{10,11},{12,13},{14,15},{1,0},{3,2},... | collective-permute-start | bytes 503816 | tf_op jit(solution)/shard_map/ppermute | solution.py:51
  31.9 14.6 %collective-permute-start.5 = (bf16[656,128]{1,0:T(8,128)(2,1)S(1)}, bf16[656,128]{1,0:T(8,128)(2,1)S(1)}, u32[]{:S(2)}, u32[]{:S(2)}) collective-permute-start(bf16[656,128]{1,0:T(8,128)(2,1)S(1)} %get-tuple-element.36), channel_id=1, source_target_pairs={{1,2},{3,4},{5,6},{7,8},{9,10},{11,12},{13,14},{15,0},{2,1},{4,3},... | collective-permute-start | bytes 503816 | tf_op jit(solution)/shard_map/ppermute | solution.py:51
  52.7 7.0 %collective-permute-start.6 = (s16[304,128]{1,0:T(8,128)(2,1)S(1)}, s16[304,128]{1,0:T(8,128)(2,1)S(1)}, u32[]{:S(2)}, u32[]{:S(2)}) collective-permute-start(s16[304,128]{1,0:T(8,128)(2,1)S(1)} %get-tuple-element.39), channel_id=1, source_target_pairs={{0,64},{128,192},{256,320},{384,448},{64,0},{192,128},{320,256},{4... | collective-permute-start | bytes 233480 | tf_op jit(solution)/shard_map/ppermute | solution.py:51
  54.6 8.8 %collective-permute-start.7 = (s16[304,128]{1,0:T(8,128)(2,1)S(1)}, s16[304,128]{1,0:T(8,128)(2,1)S(1)}, u32[]{:S(2)}, u32[]{:S(2)}) collective-permute-start(s16[304,128]{1,0:T(8,128)(2,1)S(1)} %get-tuple-element.40), channel_id=1, source_target_pairs={{64,128},{192,256},{320,384},{448,0},{128,64},{256,192},{384,320},... | collective-permute-start | bytes 233480 | tf_op jit(solution)/shard_map/ppermute | solution.py:51
  64.1 6.0 %collective-permute-start.8 = (s16[448,128]{1,0:T(8,128)(2,1)S(1)}, s16[448,128]{1,0:T(8,128)(2,1)S(1)}, u32[]{:S(2)}, u32[]{:S(2)}) collective-permute-start(s16[448,128]{1,0:T(8,128)(2,1)S(1)} %get-tuple-element.42), channel_id=1, source_target_pairs={{0,16},{32,48},{16,0},{48,32},{1,17},{33,49},{17,1},{49,33},{2,18}... | collective-permute-start | bytes 344072 | tf_op jit(solution)/shard_map/ppermute | solution.py:51
  68.0 6.7 %collective-permute-start.9 = (s16[448,128]{1,0:T(8,128)(2,1)S(1)}, s16[448,128]{1,0:T(8,128)(2,1)S(1)}, u32[]{:S(2)}, u32[]{:S(2)}) collective-permute-start(s16[448,128]{1,0:T(8,128)(2,1)S(1)} %get-tuple-element.43), channel_id=1, source_target_pairs={{16,32},{48,0},{32,16},{0,48},{17,33},{49,1},{33,17},{1,49},{18,34... | collective-permute-start | bytes 344072 | tf_op jit(solution)/shard_map/ppermute | solution.py:51
  75.4 7.8 %collective-permute-start.10 = (s16[656,128]{1,0:T(8,128)(2,1)S(1)}, s16[656,128]{1,0:T(8,128)(2,1)S(1)}, u32[]{:S(2)}, u32[]{:S(2)}) collective-permute-start(s16[656,128]{1,0:T(8,128)(2,1)S(1)} %get-tuple-element.44), channel_id=1, source_target_pairs={{0,1},{2,3},{4,5},{6,7},{8,9},{10,11},{12,13},{14,15},{1,0},{3,2},... | collective-permute-start | bytes 503816 | tf_op jit(solution)/shard_map/ppermute | solution.py:51
  77.4 9.0 %collective-permute-start.11 = (s16[656,128]{1,0:T(8,128)(2,1)S(1)}, s16[656,128]{1,0:T(8,128)(2,1)S(1)}, u32[]{:S(2)}, u32[]{:S(2)}) collective-permute-start(s16[656,128]{1,0:T(8,128)(2,1)S(1)} %get-tuple-element.45), channel_id=1, source_target_pairs={{1,2},{3,4},{5,6},{7,8},{9,10},{11,12},{13,14},{15,0},{2,1},{4,3},... | collective-permute-start | bytes 503816 | tf_op jit(solution)/shard_map/ppermute | solution.py:51
  92.9 7.3 %collective-permute-start.12 = (s16[304,128]{1,0:T(8,128)(2,1)S(1)}, s16[304,128]{1,0:T(8,128)(2,1)S(1)}, u32[]{:S(2)}, u32[]{:S(2)}) collective-permute-start(s16[304,128]{1,0:T(8,128)(2,1)S(1)} %get-tuple-element.49), channel_id=1, source_target_pairs={{0,64},{128,192},{256,320},{384,448},{64,0},{192,128},{320,256},{4... | collective-permute-start | bytes 233480 | tf_op jit(solution)/shard_map/ppermute | solution.py:51
  96.8 8.8 %collective-permute-start.13 = (s16[304,128]{1,0:T(8,128)(2,1)S(1)}, s16[304,128]{1,0:T(8,128)(2,1)S(1)}, u32[]{:S(2)}, u32[]{:S(2)}) collective-permute-start(s16[304,128]{1,0:T(8,128)(2,1)S(1)} %get-tuple-element.50), channel_id=1, source_target_pairs={{64,128},{192,256},{320,384},{448,0},{128,64},{256,192},{384,320},... | collective-permute-start | bytes 233480 | tf_op jit(solution)/shard_map/ppermute | solution.py:51
  106.3 6.3 %collective-permute-start.14 = (s16[448,128]{1,0:T(8,128)(2,1)S(1)}, s16[448,128]{1,0:T(8,128)(2,1)S(1)}, u32[]{:S(2)}, u32[]{:S(2)}) collective-permute-start(s16[448,128]{1,0:T(8,128)(2,1)S(1)} %get-tuple-element.52), channel_id=1, source_target_pairs={{0,16},{32,48},{16,0},{48,32},{1,17},{33,49},{17,1},{49,33},{2,18}... | collective-permute-start | bytes 344072 | tf_op jit(solution)/shard_map/ppermute | solution.py:51
  110.5 6.7 %collective-permute-start.15 = (s16[448,128]{1,0:T(8,128)(2,1)S(1)}, s16[448,128]{1,0:T(8,128)(2,1)S(1)}, u32[]{:S(2)}, u32[]{:S(2)}) collective-permute-start(s16[448,128]{1,0:T(8,128)(2,1)S(1)} %get-tuple-element.53), channel_id=1, source_target_pairs={{16,32},{48,0},{32,16},{0,48},{17,33},{49,1},{33,17},{1,49},{18,34... | collective-permute-start | bytes 344072 | tf_op jit(solution)/shard_map/ppermute | solution.py:51
  117.9 7.8 %collective-permute-start.16 = (s16[656,128]{1,0:T(8,128)(2,1)S(1)}, s16[656,128]{1,0:T(8,128)(2,1)S(1)}, u32[]{:S(2)}, u32[]{:S(2)}) collective-permute-start(s16[656,128]{1,0:T(8,128)(2,1)S(1)} %get-tuple-element.54), channel_id=1, source_target_pairs={{0,1},{2,3},{4,5},{6,7},{8,9},{10,11},{12,13},{14,15},{1,0},{3,2},... | collective-permute-start | bytes 503816 | tf_op jit(solution)/shard_map/ppermute | solution.py:51
  120.1 8.6 %collective-permute-start.17 = (s16[656,128]{1,0:T(8,128)(2,1)S(1)}, s16[656,128]{1,0:T(8,128)(2,1)S(1)}, u32[]{:S(2)}, u32[]{:S(2)}) collective-permute-start(s16[656,128]{1,0:T(8,128)(2,1)S(1)} %get-tuple-element.55), channel_id=1, source_target_pairs={{1,2},{3,4},{5,6},{7,8},{9,10},{11,12},{13,14},{15,0},{2,1},{4,3},... | collective-permute-start | bytes 503816 | tf_op jit(solution)/shard_map/ppermute | solution.py:51
  141.3 6.5 %collective-permute-start.19 = (f32[8,128]{1,0:T(8,128)S(1)}, f32[8,128]{1,0:T(8,128)S(1)}, u32[]{:S(2)}, u32[]{:S(2)}) collective-permute-start(f32[8,128]{1,0:T(8,128)S(1)} %get-tuple-element.69), channel_id=1, source_target_pairs={{1,2},{3,4},{5,6},{7,8},{9,10},{11,12},{13,14},{15,0},{2,1},{4,3},... | collective-permute-start | bytes 12296 | tf_op jit(solution)/shard_map/ppermute | solution.py:51
  145.9 4.4 %collective-permute-start.18 = (f32[8,128]{1,0:T(8,128)S(1)}, f32[8,128]{1,0:T(8,128)S(1)}, u32[]{:S(2)}, u32[]{:S(2)}) collective-permute-start(f32[8,128]{1,0:T(8,128)S(1)} %get-tuple-element.70), channel_id=1, source_target_pairs={{0,1},{2,3},{4,5},{6,7},{8,9},{10,11},{12,13},{14,15},{1,0},{3,2},... | collective-permute-start | bytes 12296 | tf_op jit(solution)/shard_map/ppermute | solution.py:51
  151.1 6.6 %collective-permute-start.20 = (f32[8,128]{1,0:T(8,128)S(1)}, f32[8,128]{1,0:T(8,128)S(1)}, u32[]{:S(2)}, u32[]{:S(2)}) collective-permute-start(f32[8,128]{1,0:T(8,128)S(1)} %get-tuple-element.59), channel_id=1, source_target_pairs={{0,16},{32,48},{16,0},{48,32},{1,17},{33,49},{17,1},{49,33},{2,18}... | collective-permute-start | bytes 12296 | tf_op jit(solution)/shard_map/ppermute | solution.py:51
  155.6 4.9 %collective-permute-start.21 = (f32[8,128]{1,0:T(8,128)S(1)}, f32[8,128]{1,0:T(8,128)S(1)}, u32[]{:S(2)}, u32[]{:S(2)}) collective-permute-start(f32[8,128]{1,0:T(8,128)S(1)} %get-tuple-element.60), channel_id=1, source_target_pairs={{16,32},{48,0},{32,16},{0,48},{17,33},{49,1},{33,17},{1,49},{18,34... | collective-permute-start | bytes 12296 | tf_op jit(solution)/shard_map/ppermute | solution.py:51
  161.3 7.0 %collective-permute-start.22 = (f32[8,128]{1,0:T(8,128)S(1)}, f32[8,128]{1,0:T(8,128)S(1)}, u32[]{:S(2)}, u32[]{:S(2)}) collective-permute-start(f32[8,128]{1,0:T(8,128)S(1)} %get-tuple-element.62), channel_id=1, source_target_pairs={{0,64},{128,192},{256,320},{384,448},{64,0},{192,128},{320,256},{4... | collective-permute-start | bytes 12296 | tf_op jit(solution)/shard_map/ppermute | solution.py:51
  163.2 8.0 %collective-permute-start.23 = (f32[8,128]{1,0:T(8,128)S(1)}, f32[8,128]{1,0:T(8,128)S(1)}, u32[]{:S(2)}, u32[]{:S(2)}) collective-permute-start(f32[8,128]{1,0:T(8,128)S(1)} %get-tuple-element.63), channel_id=1, source_target_pairs={{64,128},{192,256},{320,384},{448,0},{128,64},{256,192},{384,320},... | collective-permute-start | bytes 12296 | tf_op jit(solution)/shard_map/ppermute | solution.py:51
  (5 other events, 127.4 us)

commit v2 on v1

--- a/solution.py
+++ b/solution.py
@@ -113,13 +113,12 @@
     return functools.reduce(jnp.maximum, levels)
 
 
-def faces_y_kernel(parity, level, own, x1, x2, out1, out2, held, u1, u2, p1, p2):
-    fixed = out1.dtype == jnp.int16
+def faces_y_kernel(trade, parity, level, own, x1, x2, out, held, u1, u2, picked):
+    fixed = out.dtype == jnp.int16
     unpack(x1, u1)
     unpack(x2, u2)
-    even = parity[1] == 0
-    p1[ROWS_Y - 16 :] = jnp.zeros((16, VECS), F32)
-    p2[ROWS_Y - 16 :] = jnp.zeros((16, VECS), F32)
+    upper = parity[1] == trade
+    picked[ROWS_Y - 16 :] = jnp.zeros((16, VECS), F32)
     for b in range(ORB):
         if fixed:
             take = [own[b, 16 * q : 16 * q + 16] for q in range(2 * CX)]
@@ -128,14 +127,10 @@
             take = [held[16 * q : 16 * q + 16] for q in range(2 * CX)]
         take += [u[b * NX + 16 * q : b * NX + 16 * q + 16] for u in (u1, u2) for q in range(2)]
         for q, rows in enumerate(take):
-            at = b * NY + 4 * q
-            low, high = rows[0:4], rows[12:16]
-            p1[at : at + 4] = jnp.where(even, high, low)
-            p2[at : at + 4] = jnp.where(even, low, high)
+            picked[b * NY + 4 * q : b * NY + 4 * q + 4] = jnp.where(upper, rows[12:16], rows[0:4])
     if fixed:
         level = highest([level[...], level_of(x1), level_of(x2)])
-    pack(p1, out1, level)
-    pack(p2, out2, level)
+    pack(picked, out, level)
 
 
 def faces_z_kernel(parity, level, own, x1, x2, y1, y2, out1, out2, held, u1, u2, v1, v2, p1, p2):
@@ -166,35 +161,68 @@
     pack(p2, out2, level)
 
 
-def load_tiles(own, ghosts, plains, loose):
+def loop(count, body, unroll):
+    def step(k, carry):
+        body(k)
+        return carry
+
+    lax.fori_loop(0, count, step, 0, unroll=unroll)
+
+
+def aligned(row, count=16):
+    return pl.ds(pl.multiple_of(row, count), count)
+
+
+def make_tiles(pieces, loose, tiles, base):
+    slots = sum(count for _, count in pieces)
     zero = jnp.zeros((8, VECS), F32)
 
-    def clear(j, carry):
-        loose[pl.ds(pl.multiple_of(j * 16 + 8, 8), 8), :] = zero
-        return carry
-
-    lax.fori_loop(0, SLOTS, clear, 0, unroll=16)
-    for message, plain in zip(ghosts, plains):
+    def clear(j):
+        loose[aligned(j * 16 + 8, 8), :] = zero
+
+    loop(slots, clear, 16)
+    for b in range(ORB):
+        at = 0
+        for rows_of, count in pieces:
+            loose[pl.ds(at * 16 + b, count, stride=16), :] = rows_of(b)
+            at += count
+
+    def split(j):
+        value = loose[aligned(j * 16), :]
+        high = value.astype(BF16)
+        tiles[base + j, :, 0:128] = high
+        if tiles.shape[2] == 256:
+            tiles[base + j, :, 128:256] = (value - high.astype(F32)).astype(BF16)
+
+    loop(slots, split, 16)
+
+
+def front_tiles(own, messages, plains, loose, tiles):
+    pieces = [(lambda b: own[b].astype(F32), ATOMS)]
+    for message, plain, count in zip(messages, plains, (NX, NX, NY, NY)):
         unpack(message, plain)
-    counts = (NX, NX, NY, NY, NZ, NZ)
-    for b in range(ORB):
-        loose[pl.ds(b, ATOMS, stride=16), :] = own[b].astype(F32)
-        base = ATOMS
-        for plain, count in zip(plains, counts):
-            loose[pl.ds(base * 16 + b, count, stride=16), :] = plain[b * count : b * count + count]
-            base += count
-
-
-def split_tiles(loose, tiles):
-    def split(j, carry):
-        value = loose[pl.ds(pl.multiple_of(j * 16, 16), 16), :]
-        high = value.astype(BF16)
-        tiles[j, :, 0:128] = high
-        if tiles.shape[2] == 256:
-            tiles[j, :, 128:256] = (value - high.astype(F32)).astype(BF16)
-        return carry
-
-    lax.fori_loop(0, SLOTS, split, 0, unroll=16)
+        pieces.append((lambda b, plain=plain, count=count: plain[b * count : b * count + count], count))
+    make_tiles(pieces, loose, tiles, 0)
+
+
+def back_tiles(front, messages, plains, loose, tiles):
+    def copy(j):
+        tiles[j] = front[j]
+
+    loop(BEFORE_Z, copy, 16)
+    pieces = []
+    for message, plain in zip(messages, plains):
+        unpack(message, plain)
+        pieces.append((lambda b, plain=plain: plain[b * NZ : b * NZ + NZ], NZ))
+    make_tiles(pieces, loose, tiles, BEFORE_Z)
+
+
+def middle(k):
+    return 4 * (k >> 1) + 1 + (k & 1)
+
+
+def outer(k):
+    return 4 * (k >> 1) + 3 * (k & 1)
 
 
 def gather(slots, tiles, i):
@@ -202,15 +230,58 @@
     return jnp.concatenate(taken + taken[:1], axis=0)
 
 
-def apply_atoms(slots, rows, tiles, applied):
-    def atom(i, carry):
+def apply_atoms(slots, rows, tiles, applied, which, place):
+    def atom(k):
+        i = which(k)
         product = jnp.dot(rows[i], gather(slots, tiles, i), preferred_element_type=F32)
         if tiles.shape[2] == 256:
             product = product[:, 0:128] + product[:, 128:256]
-        applied[pl.ds(pl.multiple_of(i * 16, 16), 16), :] = product
-        return carry
-
-    lax.fori_loop(0, ATOMS, atom, 0, unroll=16)
+        applied[aligned(place(k) * 16), :] = product
+
+    loop(ATOMS // 2, atom, 16)
+
+
+def densities(slots, noise_tiles, values, dense, which, place):
+    def atom(k):
+        i = which(k)
+        value = values[aligned(i * 16), :]
+        high = value.astype(BF16)
+        low = (value - high.astype(F32)).astype(BF16)
+        product = lax.dot_general(
+            jnp.concatenate([high, low], axis=0),
+            gather(slots, noise_tiles, i),
+            (((1,), (1,)), ((), ())),
+            preferred_element_type=F32,
+        )
+        product = product[0:16] + product[16:32]
+        dense[0, aligned(place(k) * 16), :] = product[:, 0:128]
+        dense[1, aligned(place(k) * 16), :] = product[:, 128:256]
+
+    loop(ATOMS // 2, atom, 16)
+
+
+def spread_middle(half, applied):
+    def put(k):
+        applied[aligned(middle(k) * 16), :] = half[aligned(k * 16), :]
+
+    loop(ATOMS // 2, put, 16)
+
+
+def front_kernel(slots, rows, own, x1, x2, y1, y2, front, half, loose, *plains):
+    front_tiles(own, (x1, x2, y1, y2), plains, loose, front)
+    apply_atoms(slots, rows, front, half, middle, lambda k: k)
+
+
+def front_third_kernel(coef, slots, rows, prev, sum_in, noise_tiles, own, x1, x2, y1, y2, front, half, dense,
+                       loose, applied, *plains):
+    front_tiles(own, (x1, x2, y1, y2), plains, loose, front)
+    apply_atoms(slots, rows, front, half, middle, lambda k: k)
+    applied[...] = jnp.zeros_like(applied)
+    spread_middle(half, applied)
+    for a in range(ORB):
+        at = pl.ds(a, ATOMS, stride=16)
+        applied[at, :] = sum_in[a] + coef[3] * (2.0 * applied[at, :] - prev[a])
+    densities(slots, noise_tiles, applied, dense, middle, lambda k: k)
 
 
 def put_faces(parity, now, out1, out2, level, p1, p2):
@@ -234,11 +305,15 @@
     pack(p2, out2, level[...])
 
 
-def first_kernel(parity, coef, slots, rows, own, x1, x2, y1, y2, z1, z2, now, total, out1, out2, level, tiles,
+def rest(slots, rows, front, half, messages, plains, loose, tiles, applied):
+    back_tiles(front, messages, plains, loose, tiles)
+    apply_atoms(slots, rows, tiles, applied, outer, outer)
+    spread_middle(half, applied)
+
+
+def first_kernel(parity, coef, slots, rows, own, front, half, z1, z2, now, total, out1, out2, level, tiles,
                  loose, applied, p1, p2, *plains):
-    load_tiles(own, (x1, x2, y1, y2, z1, z2), plains, loose)
-    split_tiles(loose, tiles)
-    apply_atoms(slots, rows, tiles, applied)
+    rest(slots, rows, front, half, (z1, z2), plains, loose, tiles, applied)
     for a in range(ORB):
         value = applied[pl.ds(a, ATOMS, stride=16), :]
         now[a] = value
@@ -246,11 +321,9 @@
     put_faces(parity, now, out1, out2, level, p1, p2)
 
 
-def second_kernel(parity, coef, slots, rows, prev, sum_in, own, x1, x2, y1, y2, z1, z2, now, total, out1, out2, level,
-                  loose, tiles, applied, p1, p2, *plains):
-    load_tiles(own, (x1, x2, y1, y2, z1, z2), plains, loose)
-    split_tiles(loose, tiles)
-    apply_atoms(slots, rows, tiles, applied)
+def second_kernel(parity, coef, slots, rows, prev, sum_in, front, half, z1, z2, now, total, out1, out2, level,
+                  tiles, loose, applied, p1, p2, *plains):
+    rest(slots, rows, front, half, (z1, z2), plains, loose, tiles, applied)
     for a in range(ORB):
         value = 2.0 * applied[pl.ds(a, ATOMS, stride=16), :] - prev[a].astype(F32)
         now[a] = value
@@ -258,34 +331,17 @@
     put_faces(parity, now, out1, out2, level, p1, p2)
 
 
-def third_kernel(coef, slots, lanes, rows, prev, sum_in, noise_tiles, deriv, own, x1, x2, y1, y2, z1, z2,
-                 total, forces, loose, tiles, applied, dense, turned, stacked, *plains):
-    load_tiles(own, (x1, x2, y1, y2, z1, z2), plains, loose)
-    split_tiles(loose, tiles)
-    apply_atoms(slots, rows, tiles, applied)
+def third_kernel(coef, slots, lanes, rows, prev, sum_in, noise_tiles, deriv, front, half, dense_half, z1, z2,
+                 total, forces, tiles, loose, applied, dense, turned, stacked, *plains):
+    rest(slots, rows, front, half, (z1, z2), plains, loose, tiles, applied)
     for a in range(ORB):
         at = pl.ds(a, ATOMS, stride=16)
         value = sum_in[a] + coef[3] * (2.0 * applied[at, :] - prev[a])
         total[a] = value
         applied[at, :] = value
-
-    def atom(i, carry):
-        at = pl.ds(pl.multiple_of(i * 16, 16), 16)
-        value = applied[at, :]
-        high = value.astype(BF16)
-        low = (value - high.astype(F32)).astype(BF16)
-        product = lax.dot_general(
-            jnp.concatenate([high, low], axis=0),
-            gather(slots, noise_tiles, i),
-            (((1,), (1,)), ((), ())),
-            preferred_element_type=F32,
-        )
-        product = product[0:16] + product[16:32]
-        dense[0, at, :] = product[:, 0:128]
-        dense[1, at, :] = product[:, 128:256]
-        return carry
-
-    lax.fori_loop(0, ATOMS, atom, 0, unroll=16)
+    densities(slots, noise_tiles, applied, dense, outer, outer)
+    for side in range(2):
+        spread_middle(dense_half.at[side], dense.at[side])
     pair = [jnp.zeros((NEIGH, ATOMS), F32) for _ in range(3)]
     for a in range(ORB):
         at = pl.ds(a, ATOMS, stride=16)
@@ -393,23 +449,27 @@
     return pltpu.VMEM((rows, VECS), F32)
 
 
-GHOST_PLAINS = [plain(r) for r in (ROWS_X, ROWS_X, ROWS_Y, ROWS_Y, ROWS_Z, ROWS_Z)]
-
-
-def exchange(parity, level, own, out1, out2):
+FRONT_PLAINS = [plain(r) for r in (ROWS_X, ROWS_X, ROWS_Y, ROWS_Y)]
+BACK_PLAINS = [plain(ROWS_Z), plain(ROWS_Z)]
+
+
+def exchange(parity, level, own, out1, out2, work):
     dtype = out1.dtype
-    x1, x2 = swapped(out1, "gx", 0), swapped(out2, "gx", 1)
-    out1, out2 = call(
-        faces_y_kernel, [((ROWS_Y, VECS), dtype)] * 2, [SMEM] + [VMEM] * 4, (parity, level, own, x1, x2),
-        [plain(ATOMS), plain(ROWS_X), plain(ROWS_X), plain(ROWS_Y), plain(ROWS_Y)],
-    )
-    y1, y2 = swapped(out1, "gy", 0), swapped(out2, "gy", 1)
+    x2, x1 = swapped(out2, "gx", 1), swapped(out1, "gx", 0)
+    outs = []
+    for trade in (1, 0):
+        (out,) = call(
+            functools.partial(faces_y_kernel, trade), [((ROWS_Y, VECS), dtype)], [SMEM] + [VMEM] * 4,
+            (parity, level, own, x1, x2), [plain(ATOMS), plain(ROWS_X), plain(ROWS_X), plain(ROWS_Y)],
+        )
+        outs.append(swapped(out, "gy", trade))
+    y2, y1 = outs
     out1, out2 = call(
         faces_z_kernel, [((ROWS_Z, VECS), dtype)] * 2, [SMEM] + [VMEM] * 6, (parity, level, own, x1, x2, y1, y2),
-        [plain(ATOMS)] + GHOST_PLAINS,
+        [plain(ATOMS)] + FRONT_PLAINS + BACK_PLAINS,
     )
     z1, z2 = swapped(out1, "gz", 0), swapped(out2, "gz", 1)
-    return x1, x2, y1, y2, z1, z2
+    return work(own, x1, x2, y1, y2), (z1, z2)
 
 
 def shards(noise_vectors, hamiltonian, derivative, neighbours, coefficients):
@@ -429,27 +489,44 @@
     whole = ((ORB, ATOMS, VECS), F32)
     plane = ((ROWS_X, VECS), jnp.int16)
     tile = ((8, 128), F32)
-    loose = plain(SLOTS * 16)
-    applied = plain(ATOMS * 16)
-    split = pltpu.VMEM((SLOTS, 16, 256), BF16)
-    ghosts = exchange(parity, jnp.zeros((8, VECS), F32), noise_vectors, out1, out2)
+    half = ((ATOMS // 2 * 16, VECS), F32)
+    front_loose, loose, applied = plain(BEFORE_Z * 16), plain((SLOTS - BEFORE_Z) * 16), plain(ATOMS * 16)
+    faces = [plain(ROWS_X), plain(ROWS_X)]
+
+    def work(*vectors):
+        width = 128 if vectors[0].dtype == BF16 else 256
+        return call(
+            front_kernel, [((BEFORE_Z, 16, width), BF16), half], [SMEM] + [VMEM] * 6, (slots, rows) + vectors,
+            [front_loose] + FRONT_PLAINS, flops=1 << 29,
+        )
+
+    fronts, ghosts = exchange(parity, jnp.zeros((8, VECS), F32), noise_vectors, out1, out2, work)
     first, total, out1, out2, level, noise_tiles = call(
-        first_kernel, [whole, whole, plane, plane, tile, ((SLOTS, 16, VECS), BF16)], [SMEM] * 3 + [VMEM] * 8,
-        (parity, coefficients, slots, rows, noise_vectors) + ghosts,
-        [loose, applied, plain(ROWS_X), plain(ROWS_X)] + GHOST_PLAINS, flops=1 << 30, mib=24,
-    )
-    ghosts = exchange(parity, level, first, out1, out2)
+        first_kernel, [whole, whole, plane, plane, tile, ((SLOTS, 16, VECS), BF16)], [SMEM] * 3 + [VMEM] * 6,
+        (parity, coefficients, slots, rows, noise_vectors, *fronts, *ghosts),
+        [loose, applied] + faces + BACK_PLAINS, flops=1 << 29, mib=24,
+    )
+    fronts, ghosts = exchange(parity, level, first, out1, out2, work)
     second, total, out1, out2, level = call(
-        second_kernel, [whole, whole, plane, plane, tile], [SMEM] * 3 + [VMEM] * 10,
-        (parity, coefficients, slots, rows, noise_vectors, total, first) + ghosts,
-        [loose, split, applied, plain(ROWS_X), plain(ROWS_X)] + GHOST_PLAINS, flops=1 << 30, mib=24,
-    )
-    ghosts = exchange(parity, level, second, out1, out2)
+        second_kernel, [whole, whole, plane, plane, tile], [SMEM] * 3 + [VMEM] * 7,
+        (parity, coefficients, slots, rows, noise_vectors, total, *fronts, *ghosts),
+        [pltpu.VMEM((SLOTS, 16, 256), BF16), loose, applied] + faces + BACK_PLAINS, flops=1 << 29, mib=24,
+    )
+
+    def last_work(*vectors):
+        return call(
+            front_third_kernel, [((BEFORE_Z, 16, 256), BF16), half, ((2,) + half[0], F32)], [SMEM] * 2 + [VMEM] * 9,
+            (coefficients, slots, rows, first, total, noise_tiles) + vectors,
+            [front_loose, applied] + FRONT_PLAINS, flops=1 << 30, mib=24,
+        )
+
+    fronts, ghosts = exchange(parity, level, second, out1, out2, last_work)
     weighted, held = call(
-        third_kernel, [whole, ((8, LANES), F32)], [SMEM] * 2 + [VMEM] * 13,
-        (coefficients, slots, lanes, rows, first, total, noise_tiles, derivative.transpose(0, 2, 3, 1, 4), second) + ghosts,
-        [loose, split, applied, pltpu.VMEM((2, ATOMS * 16, 128), F32), plain(256), plain(NEIGH * 16)] + GHOST_PLAINS,
-        flops=1 << 31, mib=32,
+        third_kernel, [whole, ((8, LANES), F32)], [SMEM] * 2 + [VMEM] * 11,
+        (coefficients, slots, lanes, rows, first, total, noise_tiles, derivative.transpose(0, 2, 3, 1, 4), *fronts, *ghosts),
+        [pltpu.VMEM((SLOTS, 16, 256), BF16), loose, applied, pltpu.VMEM((2, ATOMS * 16, 128), F32), plain(256),
+         plain(NEIGH * 16)] + BACK_PLAINS,
+        flops=1 << 30, mib=32,
     )
     out1, out2 = held[:, LANES_Z : LANES_Z + 128], held[:, LANES_Z + 128 :]
     from1, from2 = swapped(out1, "gz", 0), swapped(out2, "gz", 1)

time: 173 us -> 167 us (0.965)
  waiting for transfers between devices: 46.2 us -> 35 us
  Pallas kernels: 33.5 us -> 40.5 us
  starting transfers between devices: 89.5 us -> 86.7 us
    ppermute x24, waiting for transfers between devices: 46.2 us -> 35 us  [swapped(): return lax.ppermute(value, axis, pairs + [(b, a) for a, b in pairs])]
    pallas_call x13 -> x19, Pallas kernels: 33.5 us -> 40.5 us  [call(): pl.pallas_call(kernel, out_shape=shapes, in_specs=in_specs, out_specs=[VM...]
    ppermute x24, starting transfers between devices: 89.5 us -> 86.7 us  [swapped(): return lax.ppermute(value, axis, pairs + [(b, a) for a, b in pairs])]
  transfers between devices with their start and end apart: 24 -> 24, of which waited for: 14 -> 12; matrix products, arithmetic and copies ran while one was open for 0% -> 0% of each run, Pallas kernels for 1% -> 10%
where the time goes in v2:
time: 167 us; the launch traced here: 166 us
  starting transfers between devices  86.7 us (52%)
  Pallas kernels  40.5 us (24%)
  waiting for transfers between devices  35 us (21%)
  local copies, waits for them, and re-layouts  1.97 us (1%)
    ppermute x24, starting transfers between devices, swapped(): return lax.ppermute(value, axis, pairs + [(b, a) for a, b in pairs])  86.7 us
    pallas_call x19, Pallas kernels, call(): pl.pallas_call(kernel, out_shape=shapes, in_specs=in_specs, out_specs=[VM...  40.5 us
    ppermute x24, waiting for transfers between devices, swapped(): return lax.ppermute(value, axis, pairs + [(b, a) for a, b in pairs])  35 us
  transfers between devices with their start and end apart: 24, of which 12 were waited for; matrix products, arithmetic and copies ran while one was open for 0% of the time, Pallas kernels for 10%

profile of v2, /device:TPU:1, one launch (start us, length us, event | category | flops | bytes accessed | tf_op | source)
XLA Modules:
  0.0 166.4 jit_solution(6356992859721800800)
XLA Ops:
  1.6 7.9 %collective-permute-start.1 = (bf16[304,128]{1,0:T(8,128)(2,1)S(1)}, bf16[304,128]{1,0:T(8,128)(2,1)S(1)}, u32[]{:S(2)}, u32[]{:S(2)}) collective-permute-start(bf16[304,128]{1,0:T(8,128)(2,1)S(1)} %concatenate.7), channel_id=1, source_target_pairs={{64,128},{192,256},{320,384},{448,0},{128,64},{256,192},{384,320},... | collective-permute-start | bytes 233480 | tf_op jit(solution)/shard_map/ppermute | solution.py:51
  17.8 4.1 %collective-permute-start.2 = (bf16[448,128]{1,0:T(8,128)(2,1)S(1)}, bf16[448,128]{1,0:T(8,128)(2,1)S(1)}, u32[]{:S(2)}, u32[]{:S(2)}) collective-permute-start(bf16[448,128]{1,0:T(8,128)(2,1)S(1)} %shard_map.69), channel_id=1, source_target_pairs={{0,16},{32,48},{16,0},{48,32},{1,17},{33,49},{17,1},{49,33},{2,18}... | collective-permute-start | bytes 344072 | tf_op jit(solution)/shard_map/ppermute | solution.py:51
  24.7 4.5 %collective-permute-done.3.y2 = bf16[448,128]{1,0:T(8,128)(2,1)S(1)} collective-permute-done((bf16[448,128]{1,0:T(8,128)(2,1)S(1)}, bf16[448,128]{1,0:T(8,128)(2,1)S(1)}, u32[]{:S(2)}, u32[]{:S(2)}) %collective-permute-start.3) | collective-permute-done | bytes 114720 | tf_op jit(solution)/shard_map/ppermute | solution.py:51
  29.9 3.5 %collective-permute-start.4 = (bf16[656,128]{1,0:T(8,128)(2,1)S(1)}, bf16[656,128]{1,0:T(8,128)(2,1)S(1)}, u32[]{:S(2)}, u32[]{:S(2)}) collective-permute-start(bf16[656,128]{1,0:T(8,128)(2,1)S(1)} %get-tuple-element.36), channel_id=1, source_target_pairs={{0,1},{2,3},{4,5},{6,7},{8,9},{10,11},{12,13},{14,15},{1,0},{3,2},... | collective-permute-start | bytes 503816 | tf_op jit(solution)/shard_map/ppermute | solution.py:51
  33.4 10.2 %collective-permute-start.5 = (bf16[656,128]{1,0:T(8,128)(2,1)S(1)}, bf16[656,128]{1,0:T(8,128)(2,1)S(1)}, u32[]{:S(2)}, u32[]{:S(2)}) collective-permute-start(bf16[656,128]{1,0:T(8,128)(2,1)S(1)} %get-tuple-element.37), channel_id=1, source_target_pairs={{1,2},{3,4},{5,6},{7,8},{9,10},{11,12},{13,14},{15,0},{2,1},{4,3},... | collective-permute-start | bytes 503816 | tf_op jit(solution)/shard_map/ppermute | solution.py:51
  43.6 3.6 %shard_map.71 = (bf16[288,16,128]{2,1,0:T(8,128)(2,1)S(1)}, f32[1024,128]{1,0:T(8,128)S(1)}) custom-call(s32[15,128]{1,0:T(8,128)S(1)} %add_select_fusion.16.slots, bf16[128,16,256]{2,1,0:T(8,128)(2,1)S(1)} %shard_map.68.rows, bf16[9,128,128]{2,1,0:T(8,128)(2,1)S(1)} %copy-done, bf16[304,128]{1,0:T(8,128)(2,1)S(1)} %collective-permute-done.x1, ...), custom_call_target="tpu_custom_call" | custom-call | flops 536870912 | bytes 3440128 | tf_op jit(solution)/shard_map/pallas_call | solution.py:37
  48.0 3.9 %shard_map.73 = (f32[9,128,128]{2,1,0:T(8,128)S(1)}, f32[9,128,128]{2,1,0:T(8,128)S(1)}, s16[304,128]{1,0:T(8,128)(2,1)S(1)}, s16[304,128]{1,0:T(8,128)(2,1)S(1)...) custom-call(s32[3]{0:T(128)S(1)} %pad_add_fusion.parity, f32[4]{0:T(128)S(1)} %copy-done.4, ...), custom_call_target="tpu_custom_call" | custom-call | flops 536870912 | bytes 6499868 | tf_op jit(solution)/shard_map/pallas_call | solution.py:37
  53.8 5.0 %collective-permute-start.7 = (s16[304,128]{1,0:T(8,128)(2,1)S(1)}, s16[304,128]{1,0:T(8,128)(2,1)S(1)}, u32[]{:S(2)}, u32[]{:S(2)}) collective-permute-start(s16[304,128]{1,0:T(8,128)(2,1)S(1)} %get-tuple-element.41), channel_id=1, source_target_pairs={{64,128},{192,256},{320,384},{448,0},{128,64},{256,192},{384,320},... | collective-permute-start | bytes 233480 | tf_op jit(solution)/shard_map/ppermute | solution.py:51
  58.9 3.7 %collective-permute-done.7.x2 = s16[304,128]{1,0:T(8,128)(2,1)S(1)} collective-permute-done((s16[304,128]{1,0:T(8,128)(2,1)S(1)}, s16[304,128]{1,0:T(8,128)(2,1)S(1)}, u32[]{:S(2)}, u32[]{:S(2)}) %collective-permute-start.7) | collective-permute-done | bytes 77856 | tf_op jit(solution)/shard_map/ppermute | solution.py:51
  63.2 3.9 %collective-permute-start.8 = (s16[448,128]{1,0:T(8,128)(2,1)S(1)}, s16[448,128]{1,0:T(8,128)(2,1)S(1)}, u32[]{:S(2)}, u32[]{:S(2)}) collective-permute-start(s16[448,128]{1,0:T(8,128)(2,1)S(1)} %shard_map.74), channel_id=1, source_target_pairs={{0,16},{32,48},{16,0},{48,32},{1,17},{33,49},{17,1},{49,33},{2,18}... | collective-permute-start | bytes 344072 | tf_op jit(solution)/shard_map/ppermute | solution.py:51
  69.9 4.5 %collective-permute-done.9.y2 = s16[448,128]{1,0:T(8,128)(2,1)S(1)} collective-permute-done((s16[448,128]{1,0:T(8,128)(2,1)S(1)}, s16[448,128]{1,0:T(8,128)(2,1)S(1)}, u32[]{:S(2)}, u32[]{:S(2)}) %collective-permute-start.9) | collective-permute-done | bytes 114720 | tf_op jit(solution)/shard_map/ppermute | solution.py:51
  77.1 4.6 %collective-permute-start.11 = (s16[656,128]{1,0:T(8,128)(2,1)S(1)}, s16[656,128]{1,0:T(8,128)(2,1)S(1)}, u32[]{:S(2)}, u32[]{:S(2)}) collective-permute-start(s16[656,128]{1,0:T(8,128)(2,1)S(1)} %get-tuple-element.46), channel_id=1, source_target_pairs={{1,2},{3,4},{5,6},{7,8},{9,10},{11,12},{13,14},{15,0},{2,1},{4,3},... | collective-permute-start | bytes 503816 | tf_op jit(solution)/shard_map/ppermute | solution.py:51
  81.7 3.9 %shard_map.76 = (bf16[288,16,256]{2,1,0:T(8,128)(2,1)S(1)}, f32[1024,128]{1,0:T(8,128)S(1)}) custom-call(s32[15,128]{1,0:T(8,128)S(1)} %add_select_fusion.16.slots, bf16[128,16,256]{2,1,0:T(8,128)(2,1)S(1)} %shard_map.68.rows, f32[9,128,128]{2,1,0:T(8,128)S(1)} %get-tuple-element.38.own.prev, s16[304,128]{1,0:T(8,128)(2,1)S(1)} %collective-permute-done.6.x1, ...), custom_call_target="tpu_custom_call" | custom-call | flops 536870912 | bytes 4914688 | tf_op jit(solution)/shard_map/pallas_call | solution.py:37
  86.1 4.1 %shard_map.78 = (f32[9,128,128]{2,1,0:T(8,128)S(1)}, f32[9,128,128]{2,1,0:T(8,128)S(1)}, s16[304,128]{1,0:T(8,128)(2,1)S(1)}, s16[304,128]{1,0:T(8,128)(2,1)S(1)}, f32[8,128]{1,0:T(8,128)S(1)}) custom-call(s32[3]{0:T(128)S(1)} %pad_add_fusion.parity, f32[4]{0:T(128)S(1)} %copy-done.4, s32[15,128]{1,0:T(8,128)S(1)} %add_select_fusion.16.slots, ...), custom_call_target="tpu_custom_call" | custom-call | flops 536870912 | bytes 6499868 | tf_op jit(solution)/shard_map/pallas_call | solution.py:37
  90.2 3.9 %collective-permute-start.12 = (s16[304,128]{1,0:T(8,128)(2,1)S(1)}, s16[304,128]{1,0:T(8,128)(2,1)S(1)}, u32[]{:S(2)}, u32[]{:S(2)}) collective-permute-start(s16[304,128]{1,0:T(8,128)(2,1)S(1)} %get-tuple-element.50), channel_id=1, source_target_pairs={{0,64},{128,192},{256,320},{384,448},{64,0},{192,128},{320,256},{4... | collective-permute-start | bytes 233480 | tf_op jit(solution)/shard_map/ppermute | solution.py:51
  94.2 3.3 %collective-permute-start.13 = (s16[304,128]{1,0:T(8,128)(2,1)S(1)}, s16[304,128]{1,0:T(8,128)(2,1)S(1)}, u32[]{:S(2)}, u32[]{:S(2)}) collective-permute-start(s16[304,128]{1,0:T(8,128)(2,1)S(1)} %get-tuple-element.51), channel_id=1, source_target_pairs={{64,128},{192,256},{320,384},{448,0},{128,64},{256,192},{384,320},... | collective-permute-start | bytes 233480 | tf_op jit(solution)/shard_map/ppermute | solution.py:51
  97.5 5.4 %collective-permute-done.13.x2 = s16[304,128]{1,0:T(8,128)(2,1)S(1)} collective-permute-done((s16[304,128]{1,0:T(8,128)(2,1)S(1)}, s16[304,128]{1,0:T(8,128)(2,1)S(1)}, u32[]{:S(2)}, u32[]{:S(2)}) %collective-permute-start.13) | collective-permute-done | bytes 77856 | tf_op jit(solution)/shard_map/ppermute | solution.py:51
  103.6 4.2 %collective-permute-start.14 = (s16[448,128]{1,0:T(8,128)(2,1)S(1)}, s16[448,128]{1,0:T(8,128)(2,1)S(1)}, u32[]{:S(2)}, u32[]{:S(2)}) collective-permute-start(s16[448,128]{1,0:T(8,128)(2,1)S(1)} %shard_map.79), channel_id=1, source_target_pairs={{0,16},{32,48},{16,0},{48,32},{1,17},{33,49},{17,1},{49,33},{2,18}... | collective-permute-start | bytes 344072 | tf_op jit(solution)/shard_map/ppermute | solution.py:51
  110.6 4.5 %collective-permute-done.15.y2 = s16[448,128]{1,0:T(8,128)(2,1)S(1)} collective-permute-done((s16[448,128]{1,0:T(8,128)(2,1)S(1)}, s16[448,128]{1,0:T(8,128)(2,1)S(1)}, u32[]{:S(2)}, u32[]{:S(2)}) %collective-permute-start.15) | collective-permute-done | bytes 114720 | tf_op jit(solution)/shard_map/ppermute | solution.py:51
  118.0 4.8 %collective-permute-start.17 = (s16[656,128]{1,0:T(8,128)(2,1)S(1)}, s16[656,128]{1,0:T(8,128)(2,1)S(1)}, u32[]{:S(2)}, u32[]{:S(2)}) collective-permute-start(s16[656,128]{1,0:T(8,128)(2,1)S(1)} %get-tuple-element.57), channel_id=1, source_target_pairs={{1,2},{3,4},{5,6},{7,8},{9,10},{11,12},{13,14},{15,0},{2,1},{4,3},... | collective-permute-start | bytes 503816 | tf_op jit(solution)/shard_map/ppermute | solution.py:51
  122.8 6.5 %shard_map.81 = (bf16[288,16,256]{2,1,0:T(8,128)(2,1)S(1)}, f32[1024,128]{1,0:T(8,128)S(1)}, f32[2,1024,128]{2,1,0:T(8,128)S(1)}) custom-call(f32[4]{0:T(128)S(1)} %copy-done.4, s32[15,128]{1,0:T(8,128)S(1)} %add_select_fusion.16.slots, bf16[128,16,256]{2,1,0:T(8,128)(2,1)S(1)} %shard_map.68.rows, f32[9,128,128]{2,1,0:T(8,128)S(1)} %get-tuple-element.38.own.prev, ...), custom_call_target="tpu_custom_call" | custom-call | flops 1073741824 | bytes 8912400 | tf_op jit(solution)/shard_map/pallas_call | solution.py:37
  129.3 8.6 %shard_map.83 = (f32[9,128,128]{2,1,0:T(8,128)}, f32[8,640]{1,0:T(8,128)S(1)}) custom-call(f32[4]{0:T(128)S(1)} %copy-done.4, s32[15,128]{1,0:T(8,128)S(1)} %add_select_fusion.16.slots, s32[15,128]{1,0:T(8,128)S(1)} %get-tuple-element.66.lanes, bf16[128,16,256]{2,1,0:T(8,128)(2,1)S(1)} %shard_map.68.rows, f32[9,128,128]{2,1,0:T(8,128)S(1)} %get-tuple-element.38.own.prev, ...), custom_call_target="tpu_custom_call" | custom-call | flops 1073741824 | bytes 9824528 | tf_op jit(solution)/shard_map/pallas_call | solution.py:37
  145.3 4.2 %collective-permute-start.20 = (f32[8,128]{1,0:T(8,128)S(1)}, f32[8,128]{1,0:T(8,128)S(1)}, u32[]{:S(2)}, u32[]{:S(2)}) collective-permute-start(f32[8,128]{1,0:T(8,128)S(1)} %get-tuple-element.61), channel_id=1, source_target_pairs={{0,16},{32,48},{16,0},{48,32},{1,17},{33,49},{17,1},{49,33},{2,18}... | collective-permute-start | bytes 12296 | tf_op jit(solution)/shard_map/ppermute | solution.py:51
  157.2 5.0 %collective-permute-start.23 = (f32[8,128]{1,0:T(8,128)S(1)}, f32[8,128]{1,0:T(8,128)S(1)}, u32[]{:S(2)}, u32[]{:S(2)}) collective-permute-start(f32[8,128]{1,0:T(8,128)S(1)} %get-tuple-element.65), channel_id=1, source_target_pairs={{64,128},{192,256},{320,384},{448,0},{128,64},{256,192},{384,320},... | collective-permute-start | bytes 12296 | tf_op jit(solution)/shard_map/ppermute | solution.py:51
  (63 shorter events, 47.4 us)
Async XLA Ops:
  1.6 12.0 %collective-permute-start.1 = (bf16[304,128]{1,0:T(8,128)(2,1)S(1)}, bf16[304,128]{1,0:T(8,128)(2,1)S(1)}, u32[]{:S(2)}, u32[]{:S(2)}) collective-permute-start(bf16[304,128]{1,0:T(8,128)(2,1)S(1)} %concatenate.7), channel_id=1, source_target_pairs={{64,128},{192,256},{320,384},{448,0},{128,64},{256,192},{384,320},... | collective-permute-start | bytes 233480 | tf_op jit(solution)/shard_map/ppermute | solution.py:51
  9.6 6.6 %collective-permute-start = (bf16[304,128]{1,0:T(8,128)(2,1)S(1)}, bf16[304,128]{1,0:T(8,128)(2,1)S(1)}, u32[]{:S(2)}, u32[]{:S(2)}) collective-permute-start(bf16[304,128]{1,0:T(8,128)(2,1)S(1)} %concatenate.6), channel_id=1, source_target_pairs={{0,64},{128,192},{256,320},{384,448},{64,0},{192,128},{320,256},{4... | collective-permute-start | bytes 233480 | tf_op jit(solution)/shard_map/ppermute | solution.py:51
  17.8 6.9 %collective-permute-start.2 = (bf16[448,128]{1,0:T(8,128)(2,1)S(1)}, bf16[448,128]{1,0:T(8,128)(2,1)S(1)}, u32[]{:S(2)}, u32[]{:S(2)}) collective-permute-start(bf16[448,128]{1,0:T(8,128)(2,1)S(1)} %shard_map.69), channel_id=1, source_target_pairs={{0,16},{32,48},{16,0},{48,32},{1,17},{33,49},{17,1},{49,33},{2,18}... | collective-permute-start | bytes 344072 | tf_op jit(solution)/shard_map/ppermute | solution.py:51
  22.5 6.7 %collective-permute-start.3 = (bf16[448,128]{1,0:T(8,128)(2,1)S(1)}, bf16[448,128]{1,0:T(8,128)(2,1)S(1)}, u32[]{:S(2)}, u32[]{:S(2)}) collective-permute-start(bf16[448,128]{1,0:T(8,128)(2,1)S(1)} %shard_map.70), channel_id=1, source_target_pairs={{16,32},{48,0},{32,16},{0,48},{17,33},{49,1},{33,17},{1,49},{18,34... | collective-permute-start | bytes 344072 | tf_op jit(solution)/shard_map/ppermute | solution.py:51
  29.9 17.3 %collective-permute-start.4 = (bf16[656,128]{1,0:T(8,128)(2,1)S(1)}, bf16[656,128]{1,0:T(8,128)(2,1)S(1)}, u32[]{:S(2)}, u32[]{:S(2)}) collective-permute-start(bf16[656,128]{1,0:T(8,128)(2,1)S(1)} %get-tuple-element.36), channel_id=1, source_target_pairs={{0,1},{2,3},{4,5},{6,7},{8,9},{10,11},{12,13},{14,15},{1,0},{3,2},... | collective-permute-start | bytes 503816 | tf_op jit(solution)/shard_map/ppermute | solution.py:51
  33.4 14.6 %collective-permute-start.5 = (bf16[656,128]{1,0:T(8,128)(2,1)S(1)}, bf16[656,128]{1,0:T(8,128)(2,1)S(1)}, u32[]{:S(2)}, u32[]{:S(2)}) collective-permute-start(bf16[656,128]{1,0:T(8,128)(2,1)S(1)} %get-tuple-element.37), channel_id=1, source_target_pairs={{1,2},{3,4},{5,6},{7,8},{9,10},{11,12},{13,14},{15,0},{2,1},{4,3},... | collective-permute-start | bytes 503816 | tf_op jit(solution)/shard_map/ppermute | solution.py:51
  51.9 7.0 %collective-permute-start.6 = (s16[304,128]{1,0:T(8,128)(2,1)S(1)}, s16[304,128]{1,0:T(8,128)(2,1)S(1)}, u32[]{:S(2)}, u32[]{:S(2)}) collective-permute-start(s16[304,128]{1,0:T(8,128)(2,1)S(1)} %get-tuple-element.40), channel_id=1, source_target_pairs={{0,64},{128,192},{256,320},{384,448},{64,0},{192,128},{320,256},{4... | collective-permute-start | bytes 233480 | tf_op jit(solution)/shard_map/ppermute | solution.py:51
  53.8 8.8 %collective-permute-start.7 = (s16[304,128]{1,0:T(8,128)(2,1)S(1)}, s16[304,128]{1,0:T(8,128)(2,1)S(1)}, u32[]{:S(2)}, u32[]{:S(2)}) collective-permute-start(s16[304,128]{1,0:T(8,128)(2,1)S(1)} %get-tuple-element.41), channel_id=1, source_target_pairs={{64,128},{192,256},{320,384},{448,0},{128,64},{256,192},{384,320},... | collective-permute-start | bytes 233480 | tf_op jit(solution)/shard_map/ppermute | solution.py:51
  63.2 6.7 %collective-permute-start.8 = (s16[448,128]{1,0:T(8,128)(2,1)S(1)}, s16[448,128]{1,0:T(8,128)(2,1)S(1)}, u32[]{:S(2)}, u32[]{:S(2)}) collective-permute-start(s16[448,128]{1,0:T(8,128)(2,1)S(1)} %shard_map.74), channel_id=1, source_target_pairs={{0,16},{32,48},{16,0},{48,32},{1,17},{33,49},{17,1},{49,33},{2,18}... | collective-permute-start | bytes 344072 | tf_op jit(solution)/shard_map/ppermute | solution.py:51
  67.8 6.7 %collective-permute-start.9 = (s16[448,128]{1,0:T(8,128)(2,1)S(1)}, s16[448,128]{1,0:T(8,128)(2,1)S(1)}, u32[]{:S(2)}, u32[]{:S(2)}) collective-permute-start(s16[448,128]{1,0:T(8,128)(2,1)S(1)} %shard_map.75), channel_id=1, source_target_pairs={{16,32},{48,0},{32,16},{0,48},{17,33},{49,1},{33,17},{1,49},{18,34... | collective-permute-start | bytes 344072 | tf_op jit(solution)/shard_map/ppermute | solution.py:51
  75.2 10.4 %collective-permute-start.10 = (s16[656,128]{1,0:T(8,128)(2,1)S(1)}, s16[656,128]{1,0:T(8,128)(2,1)S(1)}, u32[]{:S(2)}, u32[]{:S(2)}) collective-permute-start(s16[656,128]{1,0:T(8,128)(2,1)S(1)} %get-tuple-element.45), channel_id=1, source_target_pairs={{0,1},{2,3},{4,5},{6,7},{8,9},{10,11},{12,13},{14,15},{1,0},{3,2},... | collective-permute-start | bytes 503816 | tf_op jit(solution)/shard_map/ppermute | solution.py:51
  77.1 9.0 %collective-permute-start.11 = (s16[656,128]{1,0:T(8,128)(2,1)S(1)}, s16[656,128]{1,0:T(8,128)(2,1)S(1)}, u32[]{:S(2)}, u32[]{:S(2)}) collective-permute-start(s16[656,128]{1,0:T(8,128)(2,1)S(1)} %get-tuple-element.46), channel_id=1, source_target_pairs={{1,2},{3,4},{5,6},{7,8},{9,10},{11,12},{13,14},{15,0},{2,1},{4,3},... | collective-permute-start | bytes 503816 | tf_op jit(solution)/shard_map/ppermute | solution.py:51
  90.2 7.3 %collective-permute-start.12 = (s16[304,128]{1,0:T(8,128)(2,1)S(1)}, s16[304,128]{1,0:T(8,128)(2,1)S(1)}, u32[]{:S(2)}, u32[]{:S(2)}) collective-permute-start(s16[304,128]{1,0:T(8,128)(2,1)S(1)} %get-tuple-element.50), channel_id=1, source_target_pairs={{0,64},{128,192},{256,320},{384,448},{64,0},{192,128},{320,256},{4... | collective-permute-start | bytes 233480 | tf_op jit(solution)/shard_map/ppermute | solution.py:51
  94.2 8.8 %collective-permute-start.13 = (s16[304,128]{1,0:T(8,128)(2,1)S(1)}, s16[304,128]{1,0:T(8,128)(2,1)S(1)}, u32[]{:S(2)}, u32[]{:S(2)}) collective-permute-start(s16[304,128]{1,0:T(8,128)(2,1)S(1)} %get-tuple-element.51), channel_id=1, source_target_pairs={{64,128},{192,256},{320,384},{448,0},{128,64},{256,192},{384,320},... | collective-permute-start | bytes 233480 | tf_op jit(solution)/shard_map/ppermute | solution.py:51
  103.6 7.0 %collective-permute-start.14 = (s16[448,128]{1,0:T(8,128)(2,1)S(1)}, s16[448,128]{1,0:T(8,128)(2,1)S(1)}, u32[]{:S(2)}, u32[]{:S(2)}) collective-permute-start(s16[448,128]{1,0:T(8,128)(2,1)S(1)} %shard_map.79), channel_id=1, source_target_pairs={{0,16},{32,48},{16,0},{48,32},{1,17},{33,49},{17,1},{49,33},{2,18}... | collective-permute-start | bytes 344072 | tf_op jit(solution)/shard_map/ppermute | solution.py:51
  108.4 6.7 %collective-permute-start.15 = (s16[448,128]{1,0:T(8,128)(2,1)S(1)}, s16[448,128]{1,0:T(8,128)(2,1)S(1)}, u32[]{:S(2)}, u32[]{:S(2)}) collective-permute-start(s16[448,128]{1,0:T(8,128)(2,1)S(1)} %shard_map.80), channel_id=1, source_target_pairs={{16,32},{48,0},{32,16},{0,48},{17,33},{49,1},{33,17},{1,49},{18,34... | collective-permute-start | bytes 344072 | tf_op jit(solution)/shard_map/ppermute | solution.py:51
  115.8 13.4 %collective-permute-start.16 = (s16[656,128]{1,0:T(8,128)(2,1)S(1)}, s16[656,128]{1,0:T(8,128)(2,1)S(1)}, u32[]{:S(2)}, u32[]{:S(2)}) collective-permute-start(s16[656,128]{1,0:T(8,128)(2,1)S(1)} %get-tuple-element.56), channel_id=1, source_target_pairs={{0,1},{2,3},{4,5},{6,7},{8,9},{10,11},{12,13},{14,15},{1,0},{3,2},... | collective-permute-start | bytes 503816 | tf_op jit(solution)/shard_map/ppermute | solution.py:51
  118.0 11.3 %collective-permute-start.17 = (s16[656,128]{1,0:T(8,128)(2,1)S(1)}, s16[656,128]{1,0:T(8,128)(2,1)S(1)}, u32[]{:S(2)}, u32[]{:S(2)}) collective-permute-start(s16[656,128]{1,0:T(8,128)(2,1)S(1)} %get-tuple-element.57), channel_id=1, source_target_pairs={{1,2},{3,4},{5,6},{7,8},{9,10},{11,12},{13,14},{15,0},{2,1},{4,3},... | collective-permute-start | bytes 503816 | tf_op jit(solution)/shard_map/ppermute | solution.py:51
  137.9 5.5 %collective-permute-start.19 = (f32[8,128]{1,0:T(8,128)S(1)}, f32[8,128]{1,0:T(8,128)S(1)}, u32[]{:S(2)}, u32[]{:S(2)}) collective-permute-start(f32[8,128]{1,0:T(8,128)S(1)} %get-tuple-element.71), channel_id=1, source_target_pairs={{1,2},{3,4},{5,6},{7,8},{9,10},{11,12},{13,14},{15,0},{2,1},{4,3},... | collective-permute-start | bytes 12296 | tf_op jit(solution)/shard_map/ppermute | solution.py:51
  139.8 4.6 %collective-permute-start.18 = (f32[8,128]{1,0:T(8,128)S(1)}, f32[8,128]{1,0:T(8,128)S(1)}, u32[]{:S(2)}, u32[]{:S(2)}) collective-permute-start(f32[8,128]{1,0:T(8,128)S(1)} %get-tuple-element.72), channel_id=1, source_target_pairs={{0,1},{2,3},{4,5},{6,7},{8,9},{10,11},{12,13},{14,15},{1,0},{3,2},... | collective-permute-start | bytes 12296 | tf_op jit(solution)/shard_map/ppermute | solution.py:51
  145.3 6.3 %collective-permute-start.20 = (f32[8,128]{1,0:T(8,128)S(1)}, f32[8,128]{1,0:T(8,128)S(1)}, u32[]{:S(2)}, u32[]{:S(2)}) collective-permute-start(f32[8,128]{1,0:T(8,128)S(1)} %get-tuple-element.61), channel_id=1, source_target_pairs={{0,16},{32,48},{16,0},{48,32},{1,17},{33,49},{17,1},{49,33},{2,18}... | collective-permute-start | bytes 12296 | tf_op jit(solution)/shard_map/ppermute | solution.py:51
  149.5 4.9 %collective-permute-start.21 = (f32[8,128]{1,0:T(8,128)S(1)}, f32[8,128]{1,0:T(8,128)S(1)}, u32[]{:S(2)}, u32[]{:S(2)}) collective-permute-start(f32[8,128]{1,0:T(8,128)S(1)} %get-tuple-element.62), channel_id=1, source_target_pairs={{16,32},{48,0},{32,16},{0,48},{17,33},{49,1},{33,17},{1,49},{18,34... | collective-permute-start | bytes 12296 | tf_op jit(solution)/shard_map/ppermute | solution.py:51
  155.2 7.0 %collective-permute-start.22 = (f32[8,128]{1,0:T(8,128)S(1)}, f32[8,128]{1,0:T(8,128)S(1)}, u32[]{:S(2)}, u32[]{:S(2)}) collective-permute-start(f32[8,128]{1,0:T(8,128)S(1)} %get-tuple-element.64), channel_id=1, source_target_pairs={{0,64},{128,192},{256,320},{384,448},{64,0},{192,128},{320,256},{4... | collective-permute-start | bytes 12296 | tf_op jit(solution)/shard_map/ppermute | solution.py:51
  157.2 8.0 %collective-permute-start.23 = (f32[8,128]{1,0:T(8,128)S(1)}, f32[8,128]{1,0:T(8,128)S(1)}, u32[]{:S(2)}, u32[]{:S(2)}) collective-permute-start(f32[8,128]{1,0:T(8,128)S(1)} %get-tuple-element.65), channel_id=1, source_target_pairs={{64,128},{192,256},{320,384},{448,0},{128,64},{256,192},{384,320},... | collective-permute-start | bytes 12296 | tf_op jit(solution)/shard_map/ppermute | solution.py:51
  (6 other events, 103.4 us)

commit v3 on v2

--- a/solution.py
+++ b/solution.py
@@ -17,14 +17,16 @@
 NX = 2 * CY * CZ
 NY = 2 * (CX + 2) * CZ
 NZ = 2 * (CX + 2) * (CY + 2)
+BEFORE_Y = ATOMS + 2 * NX
+BEFORE_Z = BEFORE_Y + 2 * NY
+SLOTS = BEFORE_Z + 2 * NZ
 ROWS_X = ORB * NX + 16
 ROWS_Y = ORB * NY + 16
 ROWS_Z = ORB * NZ + 8
-BEFORE_Y = ATOMS + 2 * NX
-BEFORE_Z = BEFORE_Y + 2 * NY
-SLOTS = BEFORE_Z + 2 * NZ
-LANES_Z = 384
-LANES = 640
+SECOND = ATOMS
+FIRST = SECOND + 8 * 32
+LANES = FIRST + 8 * 64
+AXES = ("gx", "gy", "gz")
 F32 = jnp.float32
 BF16 = jnp.bfloat16
 VMEM = pl.BlockSpec(memory_space=pltpu.VMEM)
@@ -113,14 +115,10 @@
     return functools.reduce(jnp.maximum, levels)
 
 
-def faces_y_kernel(trade, parity, level, own, x1, x2, out, held, u1, u2, picked):
-    fixed = out.dtype == jnp.int16
-    unpack(x1, u1)
-    unpack(x2, u2)
-    upper = parity[1] == trade
+def pick_y(upper, own, u1, u2, held, picked):
     picked[ROWS_Y - 16 :] = jnp.zeros((16, VECS), F32)
     for b in range(ORB):
-        if fixed:
+        if own.dtype == F32:
             take = [own[b, 16 * q : 16 * q + 16] for q in range(2 * CX)]
         else:
             held[...] = own[b].astype(F32)
@@ -128,15 +126,27 @@
         take += [u[b * NX + 16 * q : b * NX + 16 * q + 16] for u in (u1, u2) for q in range(2)]
         for q, rows in enumerate(take):
             picked[b * NY + 4 * q : b * NY + 4 * q + 4] = jnp.where(upper, rows[12:16], rows[0:4])
-    if fixed:
-        level = highest([level[...], level_of(x1), level_of(x2)])
-    pack(picked, out, level)
-
-
-def faces_z_kernel(parity, level, own, x1, x2, y1, y2, out1, out2, held, u1, u2, v1, v2, p1, p2):
+
+
+def second_y_kernel(parity, x2, x1, level, own, out, u1, u2, tall, held, picked):
+    unpack(x1, u1)
+    unpack(x2, u2)
+    tall[...] = level[...]
+    if out.dtype == jnp.int16:
+        tall[...] = highest([level[...], level_of(x1), level_of(x2)])
+    pick_y(parity[1] == 1, own, u1, u2, held, picked)
+    pack(picked, out, tall[...])
+
+
+def first_y_kernel(parity, tall, own, u1, u2, out, held, picked):
+    pick_y(parity[1] == 0, own, u1, u2, held, picked)
+    pack(picked, out, tall[...])
+
+
+def faces_z_kernel(parity, y2, y1, level, own, u1, u2, out1, out2, v1, v2, held, p1, p2):
     fixed = out1.dtype == jnp.int16
-    for message, plain in ((x1, u1), (x2, u2), (y1, v1), (y2, v2)):
-        unpack(message, plain)
+    unpack(y1, v1)
+    unpack(y2, v2)
     even = parity[2] == 0
     p1[ROWS_Z - 8 :] = jnp.zeros((8, VECS), F32)
     p2[ROWS_Z - 8 :] = jnp.zeros((8, VECS), F32)
@@ -155,8 +165,7 @@
             p1[at : at + rows] = jnp.where(even, high, low)
             p2[at : at + rows] = jnp.where(even, low, high)
             at += rows
-    if fixed:
-        level = highest([level[...]] + [level_of(m) for m in (x1, x2, y1, y2)])
+    level = highest([level[...], level_of(y1), level_of(y2)]) if fixed else level[...]
     pack(p1, out1, level)
     pack(p2, out2, level)
 
@@ -197,10 +206,9 @@
     loop(slots, split, 16)
 
 
-def front_tiles(own, messages, plains, loose, tiles):
+def front_tiles(own, plains, loose, tiles):
     pieces = [(lambda b: own[b].astype(F32), ATOMS)]
-    for message, plain, count in zip(messages, plains, (NX, NX, NY, NY)):
-        unpack(message, plain)
+    for plain, count in zip(plains, (NX, NX, NY, NY)):
         pieces.append((lambda b, plain=plain, count=count: plain[b * count : b * count + count], count))
     make_tiles(pieces, loose, tiles, 0)
 
@@ -267,14 +275,14 @@
     loop(ATOMS // 2, put, 16)
 
 
-def front_kernel(slots, rows, own, x1, x2, y1, y2, front, half, loose, *plains):
-    front_tiles(own, (x1, x2, y1, y2), plains, loose, front)
+def front_kernel(slots, rows, own, u1, u2, v1, v2, front, half, loose):
+    front_tiles(own, (u1, u2, v1, v2), loose, front)
     apply_atoms(slots, rows, front, half, middle, lambda k: k)
 
 
-def front_third_kernel(coef, slots, rows, prev, sum_in, noise_tiles, own, x1, x2, y1, y2, front, half, dense,
-                       loose, applied, *plains):
-    front_tiles(own, (x1, x2, y1, y2), plains, loose, front)
+def front_third_kernel(coef, slots, rows, prev, sum_in, noise_tiles, own, u1, u2, v1, v2, front, half, dense,
+                       loose, applied):
+    front_tiles(own, (u1, u2, v1, v2), loose, front)
     apply_atoms(slots, rows, front, half, middle, lambda k: k)
     applied[...] = jnp.zeros_like(applied)
     spread_middle(half, applied)
@@ -331,8 +339,8 @@
     put_faces(parity, now, out1, out2, level, p1, p2)
 
 
-def third_kernel(coef, slots, lanes, rows, prev, sum_in, noise_tiles, deriv, front, half, dense_half, z1, z2,
-                 total, forces, tiles, loose, applied, dense, turned, stacked, *plains):
+def third_kernel(parity, coef, slots, lanes, rows, prev, sum_in, noise_tiles, deriv, front, half, dense_half, z1, z2,
+                 total, forces, sent, tiles, loose, applied, dense, turned, stacked, *plains):
     rest(slots, rows, front, half, (z1, z2), plains, loose, tiles, applied)
     for a in range(ORB):
         at = pl.ds(a, ATOMS, stride=16)
@@ -367,53 +375,93 @@
         summed = summed + lax.dot_general(
             stacked[16 * m : 16 * m + 16].astype(BF16), hit, (((1,), (1,)), ((), ())), preferred_element_type=F32
         )
-    forces[...] = summed[0:8] + summed[8:16]
+    summed = summed[0:8] + summed[8:16]
+    forces[...] = summed[:, 0:FIRST]
     for c in range(3):
         forces[c : c + 1, 0:ATOMS] = forces[c : c + 1, 0:ATOMS] - own_rows[c]
-
-
-def spread(value, place, width):
-    row = lax.broadcasted_iota(jnp.int32, (VECS, width), 0)
-    lane = lax.broadcasted_iota(jnp.int32, (VECS, width), 1)
-    hit = jnp.where((lane == place(row)), 1.0, 0.0)
-    return jnp.dot(value, hit, precision=lax.Precision.HIGHEST, preferred_element_type=F32)
-
-
-def place_z(z):
-    return lambda r: jnp.where(r < NZ, 4 * r + z, -1)
-
-
-def place_y(y):
-    return lambda r: jnp.where(r < NY, (r >> 2) * 16 + 4 * y + (r & 3), -1)
-
-
-def place_x(x):
-    return lambda r: jnp.where(r < NX, (r >> 4) * 64 + 16 * x + (r & 15), -1)
-
-
-def merged(held, from1, from2, place, top, parity, width):
-    plane1 = jnp.where(parity == 0, top, 0)
-    return held[:, 0:width] + spread(from1[...], place(plane1), width) + spread(from2[...], place(top - plane1), width)
-
-
-def merge_z_kernel(parity, held, from1, from2, out, out1, out2):
-    out[...] = merged(held, from1, from2, place_z, CZ - 1, parity[2], LANES_Z)
-    out1[...] = jnp.zeros_like(out1)
-    out2[...] = jnp.zeros_like(out2)
-    out1[:, 0:NY] = out[:, BEFORE_Y : BEFORE_Y + NY]
-    out2[:, 0:NY] = out[:, BEFORE_Y + NY : BEFORE_Z]
-
-
-def merge_y_kernel(parity, held, from1, from2, out, out1, out2):
-    out[...] = merged(held, from1, from2, place_y, CY - 1, parity[1], 256)
-    out1[...] = jnp.zeros_like(out1)
-    out2[...] = jnp.zeros_like(out2)
-    out1[:, 0:NX] = out[:, ATOMS : ATOMS + NX]
-    out2[:, 0:NX] = out[:, ATOMS + NX : BEFORE_Y]
-
-
-def merge_x_kernel(parity, held, from1, from2, out):
-    out[...] = merged(held, from1, from2, place_x, CX - 1, parity[0], ATOMS)[0:3]
+    send(sent, summed[:, FIRST:], 64, place_of(parity))
+
+
+def place_of(parity):
+    return 4 * parity[0] + 2 * parity[1] + parity[2]
+
+
+def send(sent, value, width, place):
+    sent[...] = jnp.zeros_like(sent)
+    for kind in range(1, 8):
+        sent[place ^ kind, :, 0:width] = value[:, width * kind : width * kind + width]
+
+
+def spread(got, lanes, place, width):
+    lane = lax.broadcasted_iota(jnp.int32, (width, VECS), 0)
+    summed = jnp.zeros((24, width), F32)
+    for kind in range(1, 8):
+        value = got[place ^ kind]
+        terms = []
+        for _ in range(3):
+            terms.append(value.astype(BF16))
+            value = value - terms[-1].astype(F32)
+        hit = jnp.where(lane == lanes[kind : kind + 1, :], 1.0, 0.0).astype(BF16)
+        summed = summed + lax.dot_general(
+            jnp.concatenate([t.astype(F32) for t in terms], axis=0).astype(BF16), hit,
+            (((1,), (1,)), ((), ())), preferred_element_type=F32,
+        )
+    return summed[0:8] + summed[8:16] + summed[16:24]
+
+
+def merge_kernel(parity, held, lanes, got, out, sent):
+    value = held[...] + spread(got, lanes, place_of(parity), FIRST)
+    out[...] = value[:, 0:ATOMS]
+    send(sent, value[:, SECOND:], 32, 7 - place_of(parity))
+
+
+def finish_kernel(parity, held, lanes, got, out):
+    value = held[...] + spread(got, lanes, 7 - place_of(parity), ATOMS)
+    out[...] = value[0:3]
+
+
+def blocks(second):
+    sizes = [lax.axis_size(axis) for axis in AXES]
+    pairs = [[((k + second) % n, (k + 1 + second) % n) for k in range(0, n, 2)] for n in sizes]
+    return [
+        [(x * sizes[1] + y) * sizes[2] + z for x in px for y in py for z in pz]
+        for px in pairs[0] for py in pairs[1] for pz in pairs[2]
+    ]
+
+
+def trade_all(sent, second):
+    return lax.all_to_all(sent, AXES, 0, 0, tiled=True, axis_index_groups=blocks(second))
+
+
+def number(basis, digits, bases):
+    for digit, base in zip(digits, bases):
+        basis = basis * base + digit
+    return basis
+
+
+def second_lane(basis, cells, kinds):
+    inner = number(basis, [jnp.where(k, 0, c) for c, k in zip(cells, kinds)], [jnp.where(k, 1, 4) for k in kinds])
+    kind = 4 * kinds[0] + 2 * kinds[1] + kinds[2]
+    return jnp.where(kind > 0, SECOND + 32 * kind + inner, number(basis, cells, (CX, CY, CZ)))
+
+
+def landing_lanes(parity):
+    tables = []
+    for second in (0, 1):
+        base = 4 if second else 5
+        kind = lax.broadcasted_iota(jnp.int32, (8, VECS), 0)
+        rest = lax.broadcasted_iota(jnp.int32, (8, VECS), 1)
+        cells = [None] * 3
+        for d in (2, 1, 0):
+            traded = (kind >> (2 - d)) % 2 == 1
+            radix = jnp.where(traded, 1, base)
+            near = jnp.where((parity[d] == 0) != (second == 1), CX - 1, 0)
+            cells[d] = jnp.where(traded, near, rest % radix)
+            rest = rest // radix
+        ghost = [(c == CX).astype(jnp.int32) for c in cells]
+        lane = second_lane(rest, cells, ghost)
+        tables.append(jnp.where((rest < 2) & (kind > 0), lane, -1).astype(jnp.int32))
+    return tables
 
 
 def slots_of(neighbours, parity):
@@ -441,7 +489,16 @@
     r_out = 2 * (CX + 2) * CY + y_trade * (2 * (CX + 2)) + q
     r = jnp.where(y_out, r_out, r_in)
     slots = jnp.where(z_out, BEFORE_Z + z_trade * NZ + r, r * CZ + ez - 1)
-    lanes = jnp.where(z_out, LANES_Z + z_trade * 128 + r, r * CZ + ez - 1)
+    cells = [e - 1 for e in (ex, ey, ez)]
+    outside = (x_out, y_out, z_out)
+    trades = (x_trade, y_trade, z_trade)
+    firsts = [o & (t == 0) for o, t in zip(outside, trades)]
+    seconds = [o & (t == 1) for o, t in zip(outside, trades)]
+    kind = 4 * firsts[0] + 2 * firsts[1] + firsts[2]
+    digits = [jnp.where(f, 0, jnp.where(s, 4, c)) for f, s, c in zip(firsts, seconds, cells)]
+    inner = number(basis, digits, [jnp.where(f, 1, 5) for f in firsts])
+    lanes = second_lane(basis, cells, [s.astype(jnp.int32) for s in seconds])
+    lanes = jnp.where(kind > 0, FIRST + 64 * kind + inner, lanes)
     return slots.astype(jnp.int32), lanes.astype(jnp.int32)
 
 
@@ -449,31 +506,33 @@
     return pltpu.VMEM((rows, VECS), F32)
 
 
-FRONT_PLAINS = [plain(r) for r in (ROWS_X, ROWS_X, ROWS_Y, ROWS_Y)]
 BACK_PLAINS = [plain(ROWS_Z), plain(ROWS_Z)]
 
 
 def exchange(parity, level, own, out1, out2, work):
     dtype = out1.dtype
+    rows_x, rows_y = ((ROWS_X, VECS), F32), ((ROWS_Y, VECS), F32)
     x2, x1 = swapped(out2, "gx", 1), swapped(out1, "gx", 0)
-    outs = []
-    for trade in (1, 0):
-        (out,) = call(
-            functools.partial(faces_y_kernel, trade), [((ROWS_Y, VECS), dtype)], [SMEM] + [VMEM] * 4,
-            (parity, level, own, x1, x2), [plain(ATOMS), plain(ROWS_X), plain(ROWS_X), plain(ROWS_Y)],
-        )
-        outs.append(swapped(out, "gy", trade))
-    y2, y1 = outs
-    out1, out2 = call(
-        faces_z_kernel, [((ROWS_Z, VECS), dtype)] * 2, [SMEM] + [VMEM] * 6, (parity, level, own, x1, x2, y1, y2),
-        [plain(ATOMS)] + FRONT_PLAINS + BACK_PLAINS,
+    out2, u1, u2, level = call(
+        second_y_kernel, [((ROWS_Y, VECS), dtype), rows_x, rows_x, ((8, VECS), F32)], [SMEM] + [VMEM] * 4,
+        (parity, x2, x1, level, own), [plain(ATOMS), plain(ROWS_Y)],
+    )
+    y2 = swapped(out2, "gy", 1)
+    (out1,) = call(
+        first_y_kernel, [((ROWS_Y, VECS), dtype)], [SMEM] + [VMEM] * 4, (parity, level, own, u1, u2),
+        [plain(ATOMS), plain(ROWS_Y)],
+    )
+    y1 = swapped(out1, "gy", 0)
+    out1, out2, v1, v2 = call(
+        faces_z_kernel, [((ROWS_Z, VECS), dtype)] * 2 + [rows_y] * 2, [SMEM] + [VMEM] * 6,
+        (parity, y2, y1, level, own, u1, u2), [plain(ATOMS)] + BACK_PLAINS,
     )
     z1, z2 = swapped(out1, "gz", 0), swapped(out2, "gz", 1)
-    return work(own, x1, x2, y1, y2), (z1, z2)
+    return work(own, u1, u2, v1, v2), (z1, z2)
 
 
 def shards(noise_vectors, hamiltonian, derivative, neighbours, coefficients):
-    parity = jnp.stack([lax.axis_index(axis) % 2 for axis in ("gx", "gy", "gz")]).astype(jnp.int32)
+    parity = jnp.stack([lax.axis_index(axis) % 2 for axis in AXES]).astype(jnp.int32)
     slots, lanes = slots_of(neighbours, parity)
     lattice = noise_vectors.reshape(ORB, 2, CX, CY * CZ, VECS)
     low = lattice[:, :, 0].reshape(ORB * NX, VECS)
@@ -497,7 +556,7 @@
         width = 128 if vectors[0].dtype == BF16 else 256
         return call(
             front_kernel, [((BEFORE_Z, 16, width), BF16), half], [SMEM] + [VMEM] * 6, (slots, rows) + vectors,
-            [front_loose] + FRONT_PLAINS, flops=1 << 29,
+            [front_loose], flops=1 << 29,
         )
 
     fronts, ghosts = exchange(parity, jnp.zeros((8, VECS), F32), noise_vectors, out1, out2, work)
@@ -517,28 +576,21 @@
         return call(
             front_third_kernel, [((BEFORE_Z, 16, 256), BF16), half, ((2,) + half[0], F32)], [SMEM] * 2 + [VMEM] * 9,
             (coefficients, slots, rows, first, total, noise_tiles) + vectors,
-            [front_loose, applied] + FRONT_PLAINS, flops=1 << 30, mib=24,
+            [front_loose, applied], flops=1 << 30, mib=24,
         )
 
     fronts, ghosts = exchange(parity, level, second, out1, out2, last_work)
-    weighted, held = call(
-        third_kernel, [whole, ((8, LANES), F32)], [SMEM] * 2 + [VMEM] * 11,
-        (coefficients, slots, lanes, rows, first, total, noise_tiles, derivative.transpose(0, 2, 3, 1, 4), *fronts, *ghosts),
+    eight = ((8, 8, 128), F32)
+    lanes1, lanes2 = landing_lanes(parity)
+    weighted, held, sent = call(
+        third_kernel, [whole, ((8, FIRST), F32), eight], [SMEM] * 3 + [VMEM] * 11,
+        (parity, coefficients, slots, lanes, rows, first, total, noise_tiles, derivative.transpose(0, 2, 3, 1, 4), *fronts, *ghosts),
         [pltpu.VMEM((SLOTS, 16, 256), BF16), loose, applied, pltpu.VMEM((2, ATOMS * 16, 128), F32), plain(256),
          plain(NEIGH * 16)] + BACK_PLAINS,
         flops=1 << 30, mib=32,
     )
-    out1, out2 = held[:, LANES_Z : LANES_Z + 128], held[:, LANES_Z + 128 :]
-    from1, from2 = swapped(out1, "gz", 0), swapped(out2, "gz", 1)
-    held, out1, out2 = call(
-        merge_z_kernel, [((8, LANES_Z), F32), tile, tile], [SMEM] + [VMEM] * 3, (parity, held, from1, from2)
-    )
-    from1, from2 = swapped(out1, "gy", 0), swapped(out2, "gy", 1)
-    held, out1, out2 = call(
-        merge_y_kernel, [((8, 256), F32), tile, tile], [SMEM] + [VMEM] * 3, (parity, held, from1, from2)
-    )
-    from1, from2 = swapped(out1, "gx", 0), swapped(out2, "gx", 1)
-    (forces,) = call(merge_x_kernel, [((3, ATOMS), F32)], [SMEM] + [VMEM] * 3, (parity, held, from1, from2))
+    held, sent = call(merge_kernel, [tile, eight], [SMEM] + [VMEM] * 3, (parity, held, lanes1, trade_all(sent, 0)))
+    (forces,) = call(finish_kernel, [((3, ATOMS), F32)], [SMEM] + [VMEM] * 3, (parity, held, lanes2, trade_all(sent, 1)))
     return weighted, forces
 
 

time: 167 us -> 155 us (0.928)
  waiting for transfers between devices: 35 us -> 21.3 us
  starting transfers between devices: 86.7 us -> 75.2 us
  blocking collectives: 0 us -> 10.7 us
    ppermute x24 -> x18, waiting for transfers between devices: 35 us -> 16 us  [swapped(): return lax.ppermute(value, axis, pairs + [(b, a) for a, b in pairs])]
    ppermute x24 -> x18, starting transfers between devices: 86.7 us -> 70.5 us  [swapped(): return lax.ppermute(value, axis, pairs + [(b, a) for a, b in pairs])]
    all_to_all x0 -> x1, blocking collectives: none -> 10.7 us  [trade_all(): lax.all_to_all(sent, AXES, 0, 0, tiled=True, axis_index_groups=blocks(sec...]
    all_to_all x0 -> x1, waiting for transfers between devices: none -> 5.26 us  [trade_all(): lax.all_to_all(sent, AXES, 0, 0, tiled=True, axis_index_groups=blocks(sec...]
    all_to_all x0 -> x1, starting transfers between devices: none -> 4.71 us  [trade_all(): lax.all_to_all(sent, AXES, 0, 0, tiled=True, axis_index_groups=blocks(sec...]
    unnamed x12 -> x18, local copies, waits for them, and re-layouts: 1.95 us -> 3.43 us
    pallas_call x19 -> x18, Pallas kernels: 40.5 us -> 40.5 us  [call(): pl.pallas_call(kernel, out_shape=shapes, in_specs=in_specs, out_specs=[VM...]
  transfers between devices with their start and end apart: 24 -> 19, of which waited for: 12 -> 12; matrix products, arithmetic and copies ran while one was open for 0% -> 1% of each run, Pallas kernels for 10% -> 11%
where the time goes in v3:
time: 155 us; the launch traced here: 154 us
  starting transfers between devices  75.2 us (49%)
  Pallas kernels  40.5 us (26%)
  waiting for transfers between devices  21.3 us (14%)
  blocking collectives  10.7 us (7%)
  local copies, waits for them, and re-layouts  3.45 us (2%)
  other arithmetic  1.89 us (1%)
    ppermute x18, starting transfers between devices, swapped(): return lax.ppermute(value, axis, pairs + [(b, a) for a, b in pairs])  70.5 us
    pallas_call x18, Pallas kernels, call(): pl.pallas_call(kernel, out_shape=shapes, in_specs=in_specs, out_specs=[VM...  40.5 us
    ppermute x18, waiting for transfers between devices, swapped(): return lax.ppermute(value, axis, pairs + [(b, a) for a, b in pairs])  16 us
    all_to_all x1, blocking collectives, trade_all(): lax.all_to_all(sent, AXES, 0, 0, tiled=True, axis_index_groups=blocks(sec...  10.7 us
    all_to_all x1, waiting for transfers between devices, trade_all(): lax.all_to_all(sent, AXES, 0, 0, tiled=True, axis_index_groups=blocks(sec...  5.26 us
    all_to_all x1, starting transfers between devices, trade_all(): lax.all_to_all(sent, AXES, 0, 0, tiled=True, axis_index_groups=blocks(sec...  4.71 us
    unnamed x18, local copies, waits for them, and re-layouts  3.43 us
  transfers between devices with their start and end apart: 19, of which 12 were waited for; matrix products, arithmetic and copies ran while one was open for 1% of the time, Pallas kernels for 11%

profile of v3, /device:TPU:1, one launch (start us, length us, event | category | flops | bytes accessed | tf_op | source)
XLA Modules:
  0.0 154.1 jit_solution(16157524718626134573)
XLA Ops:
  1.7 7.9 %collective-permute-start = (bf16[304,128]{1,0:T(8,128)(2,1)S(1)}, bf16[304,128]{1,0:T(8,128)(2,1)S(1)}, u32[]{:S(2)}, u32[]{:S(2)}) collective-permute-start(bf16[304,128]{1,0:T(8,128)(2,1)S(1)} %concatenate.6), channel_id=1, source_target_pairs={{64,128},{192,256},{320,384},{448,0},{128,64},{256,192},{384,320},... | collective-permute-start | bytes 233480 | tf_op jit(solution)/shard_map/ppermute | solution.py:53
  13.7 2.6 %collective-permute-done.1.x1 = bf16[304,128]{1,0:T(8,128)(2,1)S(1)} collective-permute-done((bf16[304,128]{1,0:T(8,128)(2,1)S(1)}, bf16[304,128]{1,0:T(8,128)(2,1)S(1)}, u32[]{:S(2)}, u32[]{:S(2)}) %collective-permute-start.1) | collective-permute-done | bytes 77856 | tf_op jit(solution)/shard_map/ppermute | solution.py:53
  17.9 4.2 %collective-permute-start.2 = (bf16[448,128]{1,0:T(8,128)(2,1)S(1)}, bf16[448,128]{1,0:T(8,128)(2,1)S(1)}, u32[]{:S(2)}, u32[]{:S(2)}) collective-permute-start(bf16[448,128]{1,0:T(8,128)(2,1)S(1)} %get-tuple-element.51), channel_id=1, source_target_pairs={{16,32},{48,0},{32,16},{0,48},{17,33},{49,1},{33,17},{1,49},{18,34... | collective-permute-start | bytes 344072 | tf_op jit(solution)/shard_map/ppermute | solution.py:53
  26.6 3.5 %collective-permute-start.4 = (bf16[656,128]{1,0:T(8,128)(2,1)S(1)}, bf16[656,128]{1,0:T(8,128)(2,1)S(1)}, u32[]{:S(2)}, u32[]{:S(2)}) collective-permute-start(bf16[656,128]{1,0:T(8,128)(2,1)S(1)} %get-tuple-element.57), channel_id=1, source_target_pairs={{0,1},{2,3},{4,5},{6,7},{8,9},{10,11},{12,13},{14,15},{1,0},{3,2},... | collective-permute-start | bytes 503816 | tf_op jit(solution)/shard_map/ppermute | solution.py:53
  30.2 10.2 %collective-permute-start.5 = (bf16[656,128]{1,0:T(8,128)(2,1)S(1)}, bf16[656,128]{1,0:T(8,128)(2,1)S(1)}, u32[]{:S(2)}, u32[]{:S(2)}) collective-permute-start(bf16[656,128]{1,0:T(8,128)(2,1)S(1)} %get-tuple-element.58), channel_id=1, source_target_pairs={{1,2},{3,4},{5,6},{7,8},{9,10},{11,12},{13,14},{15,0},{2,1},{4,3},... | collective-permute-start | bytes 503816 | tf_op jit(solution)/shard_map/ppermute | solution.py:53
  40.5 3.5 %shard_map.72 = (bf16[288,16,128]{2,1,0:T(8,128)(2,1)S(1)}, f32[1024,128]{1,0:T(8,128)S(1)}) custom-call(s32[15,128]{1,0:T(8,128)S(1)} %add_select_fusion.15.slots, bf16[128,16,256]{2,1,0:T(8,128)(2,1)S(1)} %shard_map.68.rows, bf16[9,128,128]{2,1,0:T(8,128)(2,1)S(1)} %copy-done.1, f32[304,128]{1,0:T(8,128)S(1)} %get-tuple-element.49.u1, ...), custom_call_target="tpu_custom_call" | custom-call | flops 536870912 | bytes 3825152 | tf_op jit(solution)/shard_map/pallas_call | solution.py:39
  44.2 3.9 %shard_map.73 = (f32[9,128,128]{2,1,0:T(8,128)S(1)}, f32[9,128,128]{2,1,0:T(8,128)S(1)}, s16[304,128]{1,0:T(8,128)(2,1)S(1)}, s16[304,128]{1,0:T(8,128)(2,1)S(1)...) custom-call(s32[3]{0:T(128)S(1)} %pad_add_fusion.parity, f32[4]{0:T(128)S(1)} %copy-done.7, ...), custom_call_target="tpu_custom_call" | custom-call | flops 536870912 | bytes 6499868 | tf_op jit(solution)/shard_map/pallas_call | solution.py:39
  48.1 3.7 %collective-permute-start.6 = (s16[304,128]{1,0:T(8,128)(2,1)S(1)}, s16[304,128]{1,0:T(8,128)(2,1)S(1)}, u32[]{:S(2)}, u32[]{:S(2)}) collective-permute-start(s16[304,128]{1,0:T(8,128)(2,1)S(1)} %get-tuple-element.61), channel_id=1, source_target_pairs={{64,128},{192,256},{320,384},{448,0},{128,64},{256,192},{384,320},... | collective-permute-start | bytes 233480 | tf_op jit(solution)/shard_map/ppermute | solution.py:53
  53.8 3.1 %collective-permute-done.6.x2 = s16[304,128]{1,0:T(8,128)(2,1)S(1)} collective-permute-done((s16[304,128]{1,0:T(8,128)(2,1)S(1)}, s16[304,128]{1,0:T(8,128)(2,1)S(1)}, u32[]{:S(2)}, u32[]{:S(2)}) %collective-permute-start.6) | collective-permute-done | bytes 77856 | tf_op jit(solution)/shard_map/ppermute | solution.py:53
  59.5 4.3 %collective-permute-start.8 = (s16[448,128]{1,0:T(8,128)(2,1)S(1)}, s16[448,128]{1,0:T(8,128)(2,1)S(1)}, u32[]{:S(2)}, u32[]{:S(2)}) collective-permute-start(s16[448,128]{1,0:T(8,128)(2,1)S(1)} %get-tuple-element.66), channel_id=1, source_target_pairs={{16,32},{48,0},{32,16},{0,48},{17,33},{49,1},{33,17},{1,49},{18,34... | collective-permute-start | bytes 344072 | tf_op jit(solution)/shard_map/ppermute | solution.py:53
  70.3 4.7 %collective-permute-start.11 = (s16[656,128]{1,0:T(8,128)(2,1)S(1)}, s16[656,128]{1,0:T(8,128)(2,1)S(1)}, u32[]{:S(2)}, u32[]{:S(2)}) collective-permute-start(s16[656,128]{1,0:T(8,128)(2,1)S(1)} %get-tuple-element.73), channel_id=1, source_target_pairs={{1,2},{3,4},{5,6},{7,8},{9,10},{11,12},{13,14},{15,0},{2,1},{4,3},... | collective-permute-start | bytes 503816 | tf_op jit(solution)/shard_map/ppermute | solution.py:53
  75.0 3.8 %shard_map.77 = (bf16[288,16,256]{2,1,0:T(8,128)(2,1)S(1)}, f32[1024,128]{1,0:T(8,128)S(1)}) custom-call(s32[15,128]{1,0:T(8,128)S(1)} %add_select_fusion.15.slots, bf16[128,16,256]{2,1,0:T(8,128)(2,1)S(1)} %shard_map.68.rows, f32[9,128,128]{2,1,0:T(8,128)S(1)} %get-tuple-element.59.own.prev, f32[304,128]{1,0:T(8,128)S(1)} %get-tuple-element.64.u1, ...), custom_call_target="tpu_custom_call" | custom-call | flops 536870912 | bytes 5299712 | tf_op jit(solution)/shard_map/pallas_call | solution.py:39
  79.0 4.1 %shard_map.78 = (f32[9,128,128]{2,1,0:T(8,128)S(1)}, f32[9,128,128]{2,1,0:T(8,128)S(1)}, s16[304,128]{1,0:T(8,128)(2,1)S(1)}, s16[304,128]{1,0:T(8,128)(2,1)S(1)}, f32[8,128]{1,0:T(8,128)S(1)}) custom-call(s32[3]{0:T(128)S(1)} %pad_add_fusion.parity, f32[4]{0:T(128)S(1)} %copy-done.7, s32[15,128]{1,0:T(8,128)S(1)} %add_select_fusion.15.slots, ...), custom_call_target="tpu_custom_call" | custom-call | flops 536870912 | bytes 6499868 | tf_op jit(solution)/shard_map/pallas_call | solution.py:39
  83.2 7.2 %collective-permute-start.12 = (s16[304,128]{1,0:T(8,128)(2,1)S(1)}, s16[304,128]{1,0:T(8,128)(2,1)S(1)}, u32[]{:S(2)}, u32[]{:S(2)}) collective-permute-start(s16[304,128]{1,0:T(8,128)(2,1)S(1)} %get-tuple-element.77), channel_id=1, source_target_pairs={{64,128},{192,256},{320,384},{448,0},{128,64},{256,192},{384,320},... | collective-permute-start | bytes 233480 | tf_op jit(solution)/shard_map/ppermute | solution.py:53
  92.3 4.7 %collective-permute-done.13.x1 = s16[304,128]{1,0:T(8,128)(2,1)S(1)} collective-permute-done((s16[304,128]{1,0:T(8,128)(2,1)S(1)}, s16[304,128]{1,0:T(8,128)(2,1)S(1)}, u32[]{:S(2)}, u32[]{:S(2)}) %collective-permute-start.13) | collective-permute-done | bytes 77856 | tf_op jit(solution)/shard_map/ppermute | solution.py:53
  98.3 3.3 %collective-permute-start.14 = (s16[448,128]{1,0:T(8,128)(2,1)}, s16[448,128]{1,0:T(8,128)(2,1)S(1)}, u32[]{:S(2)}, u32[]{:S(2)}) collective-permute-start(s16[448,128]{1,0:T(8,128)(2,1)} %get-tuple-element.82), channel_id=1, source_target_pairs={{16,32},{48,0},{32,16},{0,48},{17,33},{49,1},{33,17},{1,49},{18,34... | collective-permute-start | bytes 344072 | tf_op jit(solution)/shard_map/ppermute | solution.py:53
  102.3 2.9 %collective-permute-start.15 = (s16[448,128]{1,0:T(8,128)(2,1)S(1)}, s16[448,128]{1,0:T(8,128)(2,1)S(1)}, u32[]{:S(2)}, u32[]{:S(2)}) collective-permute-start(s16[448,128]{1,0:T(8,128)(2,1)S(1)} %shard_map.80), channel_id=1, source_target_pairs={{0,16},{32,48},{16,0},{48,32},{1,17},{33,49},{17,1},{49,33},{2,18}... | collective-permute-start | bytes 344072 | tf_op jit(solution)/shard_map/ppermute | solution.py:53
  106.8 2.2 %collective-permute-start.16 = (s16[656,128]{1,0:T(8,128)(2,1)S(1)}, s16[656,128]{1,0:T(8,128)(2,1)S(1)}, u32[]{:S(2)}, u32[]{:S(2)}) collective-permute-start(s16[656,128]{1,0:T(8,128)(2,1)S(1)} %get-tuple-element.89), channel_id=1, source_target_pairs={{0,1},{2,3},{4,5},{6,7},{8,9},{10,11},{12,13},{14,15},{1,0},{3,2},... | collective-permute-start | bytes 503816 | tf_op jit(solution)/shard_map/ppermute | solution.py:53
  109.0 4.8 %collective-permute-start.17 = (s16[656,128]{1,0:T(8,128)(2,1)S(1)}, s16[656,128]{1,0:T(8,128)(2,1)S(1)}, u32[]{:S(2)}, u32[]{:S(2)}) collective-permute-start(s16[656,128]{1,0:T(8,128)(2,1)S(1)} %get-tuple-element.90), channel_id=1, source_target_pairs={{1,2},{3,4},{5,6},{7,8},{9,10},{11,12},{13,14},{15,0},{2,1},{4,3},... | collective-permute-start | bytes 503816 | tf_op jit(solution)/shard_map/ppermute | solution.py:53
  115.2 6.4 %shard_map.82 = (bf16[288,16,256]{2,1,0:T(8,128)(2,1)S(1)}, f32[1024,128]{1,0:T(8,128)S(1)}, f32[2,1024,128]{2,1,0:T(8,128)S(1)}) custom-call(f32[4]{0:T(128)S(1)} %copy-done.7, s32[15,128]{1,0:T(8,128)S(1)} %add_select_fusion.15.slots, bf16[128,16,256]{2,1,0:T(8,128)(2,1)S(1)} %shard_map.68.rows, f32[9,128,128]{2,1,0:T(8,128)S(1)} %get-tuple-element.59.own.prev, ...), custom_call_target="tpu_custom_call" | custom-call | flops 1073741824 | bytes 9297424 | tf_op jit(solution)/shard_map/pallas_call | solution.py:39
  121.6 8.9 %shard_map.83 = (f32[9,128,128]{2,1,0:T(8,128)}, f32[8,384]{1,0:T(8,128)S(1)}, f32[8,8,128]{2,1,0:T(8,128)}) custom-call(s32[3]{0:T(128)S(1)} %pad_add_fusion.parity, f32[4]{0:T(128)S(1)} %copy-done.7, s32[15,128]{1,0:T(8,128)S(1)} %add_select_fusion.15.slots, s32[15,128]{1,0:T(8,128)S(1)} %get-tuple-element.96.lanes, ...), custom_call_target="tpu_custom_call" | custom-call | flops 1073741824 | bytes 9849116 | tf_op jit(solution)/shard_map/pallas_call | solution.py:39
  130.5 4.7 %all-to-all-start = ((f32[8,8,128]{2,1,0:T(8,128)}), f32[8,8,128]{2,1,0:T(8,128)S(1)}, u32[]{:S(2)}, u32[]{:S(2)}) async-start(f32[8,8,128]{2,1,0:T(8,128)} %get-tuple-element.93), calls=%async_computation | async-start | bytes 65536 | tf_op jit(solution)/shard_map/all_to_all | solution.py:433
  135.8 5.3 %all-to-all-done.got = f32[8,8,128]{2,1,0:T(8,128)S(1)} async-done(((f32[8,8,128]{2,1,0:T(8,128)}), f32[8,8,128]{2,1,0:T(8,128)S(1)}, u32[]{:S(2)}, u32[]{:S(2)}) %all-to-all-start) | async-done | bytes 32800 | tf_op jit(solution)/shard_map/all_to_all | solution.py:433
  142.0 10.7 %all_to_all.10.got = f32[8,8,128]{2,1,0:T(8,128)S(1)} all-to-all(f32[8,8,128]{2,1,0:T(8,128)S(1)} %get-tuple-element.95), channel_id=1, replica_groups={{81,82,97,98,145,146,161,162},{83,84,99,100,147,148,163,164},{85,86,101..., dimensions={0} | all-to-all | bytes 65536 | tf_op jit(solution)/shard_map/all_to_all | solution.py:433
  (65 shorter events, 32.4 us)
Async XLA Ops:
  0.6 21.5 %copy-start.1 = (bf16[9,128,128]{2,1,0:T(8,128)(2,1)S(1)}, bf16[9,128,128]{2,1,0:T(8,128)(2,1)}, u32[]{:S(2)}) copy-start(bf16[9,128,128]{2,1,0:T(8,128)(2,1)} %prev.1) | copy-start | bytes 884740
  0.6 24.0 %copy-start.8 = (s32[128,15]{0,1:T(8,128)S(1)}, s32[128,15]{0,1:T(8,128)}, u32[]{:S(2)}) copy-start(s32[128,15]{0,1:T(8,128)} %param.8) | copy-start | bytes 23044
  1.7 12.0 %collective-permute-start = (bf16[304,128]{1,0:T(8,128)(2,1)S(1)}, bf16[304,128]{1,0:T(8,128)(2,1)S(1)}, u32[]{:S(2)}, u32[]{:S(2)}) collective-permute-start(bf16[304,128]{1,0:T(8,128)(2,1)S(1)} %concatenate.6), channel_id=1, source_target_pairs={{64,128},{192,256},{320,384},{448,0},{128,64},{256,192},{384,320},... | collective-permute-start | bytes 233480 | tf_op jit(solution)/shard_map/ppermute | solution.py:53
  9.6 6.6 %collective-permute-start.1 = (bf16[304,128]{1,0:T(8,128)(2,1)S(1)}, bf16[304,128]{1,0:T(8,128)(2,1)S(1)}, u32[]{:S(2)}, u32[]{:S(2)}) collective-permute-start(bf16[304,128]{1,0:T(8,128)(2,1)S(1)} %concatenate.7), channel_id=1, source_target_pairs={{0,64},{128,192},{256,320},{384,448},{64,0},{192,128},{320,256},{4... | collective-permute-start | bytes 233480 | tf_op jit(solution)/shard_map/ppermute | solution.py:53
  13.6 30.7 %copy-start.7 = (f32[4]{0:T(128)S(1)}, f32[4]{0:T(128)}, u32[]{:S(2)}) copy-start(f32[4]{0:T(128)} %coef.7) | copy-start | bytes 52
  17.9 7.3 %collective-permute-start.2 = (bf16[448,128]{1,0:T(8,128)(2,1)S(1)}, bf16[448,128]{1,0:T(8,128)(2,1)S(1)}, u32[]{:S(2)}, u32[]{:S(2)}) collective-permute-start(bf16[448,128]{1,0:T(8,128)(2,1)S(1)} %get-tuple-element.51), channel_id=1, source_target_pairs={{16,32},{48,0},{32,16},{0,48},{17,33},{49,1},{33,17},{1,49},{18,34... | collective-permute-start | bytes 344072 | tf_op jit(solution)/shard_map/ppermute | solution.py:53
  22.7 3.2 %collective-permute-start.3 = (bf16[448,128]{1,0:T(8,128)(2,1)S(1)}, bf16[448,128]{1,0:T(8,128)(2,1)S(1)}, u32[]{:S(2)}, u32[]{:S(2)}) collective-permute-start(bf16[448,128]{1,0:T(8,128)(2,1)S(1)} %shard_map.70), channel_id=1, source_target_pairs={{0,16},{32,48},{16,0},{48,32},{1,17},{33,49},{17,1},{49,33},{2,18}... | collective-permute-start | bytes 344072 | tf_op jit(solution)/shard_map/ppermute | solution.py:53
  26.6 17.4 %collective-permute-start.4 = (bf16[656,128]{1,0:T(8,128)(2,1)S(1)}, bf16[656,128]{1,0:T(8,128)(2,1)S(1)}, u32[]{:S(2)}, u32[]{:S(2)}) collective-permute-start(bf16[656,128]{1,0:T(8,128)(2,1)S(1)} %get-tuple-element.57), channel_id=1, source_target_pairs={{0,1},{2,3},{4,5},{6,7},{8,9},{10,11},{12,13},{14,15},{1,0},{3,2},... | collective-permute-start | bytes 503816 | tf_op jit(solution)/shard_map/ppermute | solution.py:53
  30.2 14.0 %collective-permute-start.5 = (bf16[656,128]{1,0:T(8,128)(2,1)S(1)}, bf16[656,128]{1,0:T(8,128)(2,1)S(1)}, u32[]{:S(2)}, u32[]{:S(2)}) collective-permute-start(bf16[656,128]{1,0:T(8,128)(2,1)S(1)} %get-tuple-element.58), channel_id=1, source_target_pairs={{1,2},{3,4},{5,6},{7,8},{9,10},{11,12},{13,14},{15,0},{2,1},{4,3},... | collective-permute-start | bytes 503816 | tf_op jit(solution)/shard_map/ppermute | solution.py:53
  48.1 30.8 %copy-start.2 = (bf16[432,16,128]{2,1,0:T(8,128)(2,1)}, bf16[432,16,128]{2,1,0:T(8,128)(2,1)S(1)}, u32[]{:S(2)}) copy-start(bf16[432,16,128]{2,1,0:T(8,128)(2,1)S(1)} %get-tuple-element.75.noise_tiles) | copy-start | bytes 5308420
  48.1 8.8 %collective-permute-start.6 = (s16[304,128]{1,0:T(8,128)(2,1)S(1)}, s16[304,128]{1,0:T(8,128)(2,1)S(1)}, u32[]{:S(2)}, u32[]{:S(2)}) collective-permute-start(s16[304,128]{1,0:T(8,128)(2,1)S(1)} %get-tuple-element.61), channel_id=1, source_target_pairs={{64,128},{192,256},{320,384},{448,0},{128,64},{256,192},{384,320},... | collective-permute-start | bytes 233480 | tf_op jit(solution)/shard_map/ppermute | solution.py:53
  51.9 6.9 %collective-permute-start.7 = (s16[304,128]{1,0:T(8,128)(2,1)S(1)}, s16[304,128]{1,0:T(8,128)(2,1)S(1)}, u32[]{:S(2)}, u32[]{:S(2)}) collective-permute-start(s16[304,128]{1,0:T(8,128)(2,1)S(1)} %get-tuple-element.62), channel_id=1, source_target_pairs={{0,64},{128,192},{256,320},{384,448},{64,0},{192,128},{320,256},{4... | collective-permute-start | bytes 233480 | tf_op jit(solution)/shard_map/ppermute | solution.py:53
  59.5 7.6 %collective-permute-start.8 = (s16[448,128]{1,0:T(8,128)(2,1)S(1)}, s16[448,128]{1,0:T(8,128)(2,1)S(1)}, u32[]{:S(2)}, u32[]{:S(2)}) collective-permute-start(s16[448,128]{1,0:T(8,128)(2,1)S(1)} %get-tuple-element.66), channel_id=1, source_target_pairs={{16,32},{48,0},{32,16},{0,48},{17,33},{49,1},{33,17},{1,49},{18,34... | collective-permute-start | bytes 344072 | tf_op jit(solution)/shard_map/ppermute | solution.py:53
  64.4 3.2 %collective-permute-start.9 = (s16[448,128]{1,0:T(8,128)(2,1)S(1)}, s16[448,128]{1,0:T(8,128)(2,1)S(1)}, u32[]{:S(2)}, u32[]{:S(2)}) collective-permute-start(s16[448,128]{1,0:T(8,128)(2,1)S(1)} %shard_map.75), channel_id=1, source_target_pairs={{0,16},{32,48},{16,0},{48,32},{1,17},{33,49},{17,1},{49,33},{2,18}... | collective-permute-start | bytes 344072 | tf_op jit(solution)/shard_map/ppermute | solution.py:53
  68.4 10.5 %collective-permute-start.10 = (s16[656,128]{1,0:T(8,128)(2,1)S(1)}, s16[656,128]{1,0:T(8,128)(2,1)S(1)}, u32[]{:S(2)}, u32[]{:S(2)}) collective-permute-start(s16[656,128]{1,0:T(8,128)(2,1)S(1)} %get-tuple-element.72), channel_id=1, source_target_pairs={{0,1},{2,3},{4,5},{6,7},{8,9},{10,11},{12,13},{14,15},{1,0},{3,2},... | collective-permute-start | bytes 503816 | tf_op jit(solution)/shard_map/ppermute | solution.py:53
  70.3 8.7 %collective-permute-start.11 = (s16[656,128]{1,0:T(8,128)(2,1)S(1)}, s16[656,128]{1,0:T(8,128)(2,1)S(1)}, u32[]{:S(2)}, u32[]{:S(2)}) collective-permute-start(s16[656,128]{1,0:T(8,128)(2,1)S(1)} %get-tuple-element.73), channel_id=1, source_target_pairs={{1,2},{3,4},{5,6},{7,8},{9,10},{11,12},{13,14},{15,0},{2,1},{4,3},... | collective-permute-start | bytes 503816 | tf_op jit(solution)/shard_map/ppermute | solution.py:53
  83.2 9.1 %collective-permute-start.12 = (s16[304,128]{1,0:T(8,128)(2,1)S(1)}, s16[304,128]{1,0:T(8,128)(2,1)S(1)}, u32[]{:S(2)}, u32[]{:S(2)}) collective-permute-start(s16[304,128]{1,0:T(8,128)(2,1)S(1)} %get-tuple-element.77), channel_id=1, source_target_pairs={{64,128},{192,256},{320,384},{448,0},{128,64},{256,192},{384,320},... | collective-permute-start | bytes 233480 | tf_op jit(solution)/shard_map/ppermute | solution.py:53
  90.3 6.6 %collective-permute-start.13 = (s16[304,128]{1,0:T(8,128)(2,1)S(1)}, s16[304,128]{1,0:T(8,128)(2,1)S(1)}, u32[]{:S(2)}, u32[]{:S(2)}) collective-permute-start(s16[304,128]{1,0:T(8,128)(2,1)S(1)} %get-tuple-element.78), channel_id=1, source_target_pairs={{0,64},{128,192},{256,320},{384,448},{64,0},{192,128},{320,256},{4... | collective-permute-start | bytes 233480 | tf_op jit(solution)/shard_map/ppermute | solution.py:53
  98.3 6.9 %collective-permute-start.14 = (s16[448,128]{1,0:T(8,128)(2,1)}, s16[448,128]{1,0:T(8,128)(2,1)S(1)}, u32[]{:S(2)}, u32[]{:S(2)}) collective-permute-start(s16[448,128]{1,0:T(8,128)(2,1)} %get-tuple-element.82), channel_id=1, source_target_pairs={{16,32},{48,0},{32,16},{0,48},{17,33},{49,1},{33,17},{1,49},{18,34... | collective-permute-start | bytes 344072 | tf_op jit(solution)/shard_map/ppermute | solution.py:53
  102.3 3.8 %collective-permute-start.15 = (s16[448,128]{1,0:T(8,128)(2,1)S(1)}, s16[448,128]{1,0:T(8,128)(2,1)S(1)}, u32[]{:S(2)}, u32[]{:S(2)}) collective-permute-start(s16[448,128]{1,0:T(8,128)(2,1)S(1)} %shard_map.80), channel_id=1, source_target_pairs={{0,16},{32,48},{16,0},{48,32},{1,17},{33,49},{17,1},{49,33},{2,18}... | collective-permute-start | bytes 344072 | tf_op jit(solution)/shard_map/ppermute | solution.py:53
  106.8 14.8 %collective-permute-start.16 = (s16[656,128]{1,0:T(8,128)(2,1)S(1)}, s16[656,128]{1,0:T(8,128)(2,1)S(1)}, u32[]{:S(2)}, u32[]{:S(2)}) collective-permute-start(s16[656,128]{1,0:T(8,128)(2,1)S(1)} %get-tuple-element.89), channel_id=1, source_target_pairs={{0,1},{2,3},{4,5},{6,7},{8,9},{10,11},{12,13},{14,15},{1,0},{3,2},... | collective-permute-start | bytes 503816 | tf_op jit(solution)/shard_map/ppermute | solution.py:53
  109.0 12.6 %collective-permute-start.17 = (s16[656,128]{1,0:T(8,128)(2,1)S(1)}, s16[656,128]{1,0:T(8,128)(2,1)S(1)}, u32[]{:S(2)}, u32[]{:S(2)}) collective-permute-start(s16[656,128]{1,0:T(8,128)(2,1)S(1)} %get-tuple-element.90), channel_id=1, source_target_pairs={{1,2},{3,4},{5,6},{7,8},{9,10},{11,12},{13,14},{15,0},{2,1},{4,3},... | collective-permute-start | bytes 503816 | tf_op jit(solution)/shard_map/ppermute | solution.py:53
  115.2 6.4 %copy-start.5 = (bf16[3,15,9,9,128]{4,1,3,2,0:T(8,128)(2,1)S(1)}, bf16[3,15,9,9,128]{4,1,3,2,0:T(8,128)(2,1)}, u32[]{:S(2)}) copy-start(bf16[3,15,9,9,128]{4,1,3,2,0:T(8,128)(2,1)} %param.7) | copy-start | bytes 2799364
  130.5 10.6 %all-to-all-start = ((f32[8,8,128]{2,1,0:T(8,128)}), f32[8,8,128]{2,1,0:T(8,128)S(1)}, u32[]{:S(2)}, u32[]{:S(2)}) async-start(f32[8,8,128]{2,1,0:T(8,128)} %get-tuple-element.93), calls=%async_computation | async-start | bytes 65536 | tf_op jit(solution)/shard_map/all_to_all | solution.py:433
  (4 other events, 9.8 us)

commit v4 on v3

--- a/solution.py
+++ b/solution.py
@@ -23,28 +23,36 @@
 ROWS_X = ORB * NX + 16
 ROWS_Y = ORB * NY + 16
 ROWS_Z = ORB * NZ + 8
-SECOND = ATOMS
-FIRST = SECOND + 8 * 32
-LANES = FIRST + 8 * 64
+KINDS = (1, 2, 4, 3, 5, 6, 7)
+SECOND_SIZE = {kind: 2 * 4 ** (3 - kind.bit_count()) for kind in KINDS}
+FIRST_SIZE = {kind: 2 * 5 ** (3 - kind.bit_count()) for kind in KINDS}
+SECOND_AT = {kind: ATOMS + sum(SECOND_SIZE[k] for k in KINDS[:n]) for n, kind in enumerate(KINDS)}
+FIRST = 256
+FIRST_AT = {kind: FIRST + sum(FIRST_SIZE[k] for k in KINDS[:n]) for n, kind in enumerate(KINDS)}
+LANES = 448
 AXES = ("gx", "gy", "gz")
 F32 = jnp.float32
 BF16 = jnp.bfloat16
 VMEM = pl.BlockSpec(memory_space=pltpu.VMEM)
-SMEM = pl.BlockSpec(memory_space=pltpu.SMEM)
-
-
-def call(kernel, outs, in_specs, args, scratch=(), flops=0, mib=16):
+HBM = pl.BlockSpec(memory_space=pltpu.HBM)
+
+
+def call(kernel, outs, args, scratch=(), flops=0, mib=16, in_hbm=()):
     shapes = [jax.ShapeDtypeStruct(shape, dtype) for shape, dtype in outs]
     moved = sum(a.size * a.dtype.itemsize for a in args) + sum(s.size * s.dtype.itemsize for s in shapes)
     return pl.pallas_call(
         kernel,
         out_shape=shapes,
-        in_specs=in_specs,
+        in_specs=[HBM if k in in_hbm else VMEM for k in range(len(args))],
         out_specs=[VMEM] * len(shapes),
         scratch_shapes=list(scratch),
         compiler_params=pltpu.CompilerParams(vmem_limit_bytes=mib << 20),
         cost_estimate=pl.CostEstimate(flops=flops, bytes_accessed=moved, transcendentals=0),
     )(*args)
+
+
+def odd(axis):
+    return lax.axis_index(axis) & 1
 
 
 def swapped(value, axis, second):
@@ -128,26 +136,26 @@
             picked[b * NY + 4 * q : b * NY + 4 * q + 4] = jnp.where(upper, rows[12:16], rows[0:4])
 
 
-def second_y_kernel(parity, x2, x1, level, own, out, u1, u2, tall, held, picked):
+def second_y_kernel(x2, x1, level, own, out, u1, u2, tall, held, picked):
     unpack(x1, u1)
     unpack(x2, u2)
     tall[...] = level[...]
     if out.dtype == jnp.int16:
         tall[...] = highest([level[...], level_of(x1), level_of(x2)])
-    pick_y(parity[1] == 1, own, u1, u2, held, picked)
+    pick_y(odd("gy") == 1, own, u1, u2, held, picked)
     pack(picked, out, tall[...])
 
 
-def first_y_kernel(parity, tall, own, u1, u2, out, held, picked):
-    pick_y(parity[1] == 0, own, u1, u2, held, picked)
+def first_y_kernel(tall, own, u1, u2, out, held, picked):
+    pick_y(odd("gy") == 0, own, u1, u2, held, picked)
     pack(picked, out, tall[...])
 
 
-def faces_z_kernel(parity, y2, y1, level, own, u1, u2, out1, out2, v1, v2, held, p1, p2):
+def faces_z_kernel(y2, y1, level, own, u1, u2, out1, out2, v1, v2, held, p1, p2):
     fixed = out1.dtype == jnp.int16
     unpack(y1, v1)
     unpack(y2, v2)
-    even = parity[2] == 0
+    even = odd("gz") == 0
     p1[ROWS_Z - 8 :] = jnp.zeros((8, VECS), F32)
     p2[ROWS_Z - 8 :] = jnp.zeros((8, VECS), F32)
     ghosts = ((u1, NX), (u2, NX), (v1, NY), (v2, NY))
@@ -233,6 +241,12 @@
     return 4 * (k >> 1) + 3 * (k & 1)
 
 
+def fetch(slots, table, arrived):
+    copy = pltpu.make_async_copy(slots, table, arrived)
+    copy.start()
+    return copy
+
+
 def gather(slots, tiles, i):
     taken = [tiles[slots[m, i]] for m in range(NEIGH)]
     return jnp.concatenate(taken + taken[:1], axis=0)
@@ -246,7 +260,7 @@
             product = product[:, 0:128] + product[:, 128:256]
         applied[aligned(place(k) * 16), :] = product
 
-    loop(ATOMS // 2, atom, 16)
+    loop(ATOMS // 2, atom, ATOMS // 2)
 
 
 def densities(slots, noise_tiles, values, dense, which, place):
@@ -265,7 +279,7 @@
         dense[0, aligned(place(k) * 16), :] = product[:, 0:128]
         dense[1, aligned(place(k) * 16), :] = product[:, 128:256]
 
-    loop(ATOMS // 2, atom, 16)
+    loop(ATOMS // 2, atom, ATOMS // 2)
 
 
 def spread_middle(half, applied):
@@ -275,25 +289,29 @@
     loop(ATOMS // 2, put, 16)
 
 
-def front_kernel(slots, rows, own, u1, u2, v1, v2, front, half, loose):
+def front_kernel(slots, rows, own, u1, u2, v1, v2, front, half, table, arrived, loose):
+    copy = fetch(slots, table, arrived)
     front_tiles(own, (u1, u2, v1, v2), loose, front)
-    apply_atoms(slots, rows, front, half, middle, lambda k: k)
+    copy.wait()
+    apply_atoms(table, rows, front, half, middle, lambda k: k)
 
 
 def front_third_kernel(coef, slots, rows, prev, sum_in, noise_tiles, own, u1, u2, v1, v2, front, half, dense,
-                       loose, applied):
+                       table, arrived, loose, applied):
+    copy = fetch(slots, table, arrived)
     front_tiles(own, (u1, u2, v1, v2), loose, front)
-    apply_atoms(slots, rows, front, half, middle, lambda k: k)
+    copy.wait()
+    apply_atoms(table, rows, front, half, middle, lambda k: k)
     applied[...] = jnp.zeros_like(applied)
     spread_middle(half, applied)
     for a in range(ORB):
         at = pl.ds(a, ATOMS, stride=16)
-        applied[at, :] = sum_in[a] + coef[3] * (2.0 * applied[at, :] - prev[a])
-    densities(slots, noise_tiles, applied, dense, middle, lambda k: k)
-
-
-def put_faces(parity, now, out1, out2, level, p1, p2):
-    even = parity[0] == 0
+        applied[at, :] = sum_in[a] + coef[3 : 4, :] * (2.0 * applied[at, :] - prev[a])
+    densities(table, noise_tiles, applied, dense, middle, lambda k: k)
+
+
+def put_faces(now, out1, out2, level, p1, p2):
+    even = odd("gx") == 0
     p1[ROWS_X - 16 :] = jnp.zeros((16, VECS), F32)
     p2[ROWS_X - 16 :] = jnp.zeros((16, VECS), F32)
     most = jnp.zeros((8, VECS), F32)
@@ -313,43 +331,48 @@
     pack(p2, out2, level[...])
 
 
-def rest(slots, rows, front, half, messages, plains, loose, tiles, applied):
+def rest(slots, table, arrived, rows, front, half, messages, plains, loose, tiles, applied):
+    copy = fetch(slots, table, arrived)
     back_tiles(front, messages, plains, loose, tiles)
-    apply_atoms(slots, rows, tiles, applied, outer, outer)
+    copy.wait()
+    apply_atoms(table, rows, tiles, applied, outer, outer)
     spread_middle(half, applied)
 
 
-def first_kernel(parity, coef, slots, rows, own, front, half, z1, z2, now, total, out1, out2, level, tiles,
-                 loose, applied, p1, p2, *plains):
-    rest(slots, rows, front, half, (z1, z2), plains, loose, tiles, applied)
+def first_kernel(coef, slots, rows, own, front, half, z1, z2, now, total, out1, out2, level, tiles,
+                 table, arrived, loose, applied, p1, p2, *plains):
+    rest(slots, table, arrived, rows, front, half, (z1, z2), plains, loose, tiles, applied)
     for a in range(ORB):
         value = applied[pl.ds(a, ATOMS, stride=16), :]
         now[a] = value
-        total[a] = coef[0] * own[a].astype(F32) + coef[1] * value
-    put_faces(parity, now, out1, out2, level, p1, p2)
-
-
-def second_kernel(parity, coef, slots, rows, prev, sum_in, front, half, z1, z2, now, total, out1, out2, level,
-                  tiles, loose, applied, p1, p2, *plains):
-    rest(slots, rows, front, half, (z1, z2), plains, loose, tiles, applied)
+        total[a] = coef[0 : 1, :] * own[a].astype(F32) + coef[1 : 2, :] * value
+    put_faces(now, out1, out2, level, p1, p2)
+
+
+def second_kernel(coef, slots, rows, prev, sum_in, front, half, z1, z2, now, total, out1, out2, level,
+                  table, arrived, tiles, loose, applied, p1, p2, *plains):
+    rest(slots, table, arrived, rows, front, half, (z1, z2), plains, loose, tiles, applied)
     for a in range(ORB):
         value = 2.0 * applied[pl.ds(a, ATOMS, stride=16), :] - prev[a].astype(F32)
         now[a] = value
-        total[a] = sum_in[a] + coef[2] * value
-    put_faces(parity, now, out1, out2, level, p1, p2)
-
-
-def third_kernel(parity, coef, slots, lanes, rows, prev, sum_in, noise_tiles, deriv, front, half, dense_half, z1, z2,
-                 total, forces, sent, tiles, loose, applied, dense, turned, stacked, *plains):
-    rest(slots, rows, front, half, (z1, z2), plains, loose, tiles, applied)
+        total[a] = sum_in[a] + coef[2 : 3, :] * value
+    put_faces(now, out1, out2, level, p1, p2)
+
+
+def third_kernel(coef, slots, lanes, rows, prev, sum_in, noise_tiles, deriv, front, half, dense_half, z1, z2,
+                 total, forces, sent, table, arrived, tiles, loose, applied, dense, turned, stacked, slopes, loaded, *plains):
+    load = pltpu.make_async_copy(deriv, slopes, loaded)
+    load.start()
+    rest(slots, table, arrived, rows, front, half, (z1, z2), plains, loose, tiles, applied)
     for a in range(ORB):
         at = pl.ds(a, ATOMS, stride=16)
-        value = sum_in[a] + coef[3] * (2.0 * applied[at, :] - prev[a])
+        value = sum_in[a] + coef[3 : 4, :] * (2.0 * applied[at, :] - prev[a])
         total[a] = value
         applied[at, :] = value
-    densities(slots, noise_tiles, applied, dense, outer, outer)
+    densities(table, noise_tiles, applied, dense, outer, outer)
     for side in range(2):
         spread_middle(dense_half.at[side], dense.at[side])
+    load.wait()
     pair = [jnp.zeros((NEIGH, ATOMS), F32) for _ in range(3)]
     for a in range(ORB):
         at = pl.ds(a, ATOMS, stride=16)
@@ -358,7 +381,7 @@
         for b in range(ORB):
             density = turned[pl.ds(b, NEIGH, stride=16), :]
             for c in range(3):
-                pair[c] = pair[c] + deriv[c, a, b].astype(F32) * density
+                pair[c] = pair[c] + slopes[c, a, b].astype(F32) * density
     others = lax.broadcasted_iota(jnp.int32, (NEIGH, ATOMS), 0) > 0
     stacked[...] = jnp.zeros_like(stacked)
     own_rows = []
@@ -379,44 +402,45 @@
     forces[...] = summed[:, 0:FIRST]
     for c in range(3):
         forces[c : c + 1, 0:ATOMS] = forces[c : c + 1, 0:ATOMS] - own_rows[c]
-    send(sent, summed[:, FIRST:], 64, place_of(parity))
-
-
-def place_of(parity):
-    return 4 * parity[0] + 2 * parity[1] + parity[2]
-
-
-def send(sent, value, width, place):
+    send(sent, summed, FIRST_AT, FIRST_SIZE, place_of())
+
+
+def place_of():
+    return 4 * odd("gx") + 2 * odd("gy") + odd("gz")
+
+
+def send(sent, value, starts, sizes, place):
     sent[...] = jnp.zeros_like(sent)
-    for kind in range(1, 8):
-        sent[place ^ kind, :, 0:width] = value[:, width * kind : width * kind + width]
+    for kind in KINDS:
+        sent[place ^ kind, :, 0 : sizes[kind]] = value[:, starts[kind] : starts[kind] + sizes[kind]]
 
 
 def spread(got, lanes, place, width):
     lane = lax.broadcasted_iota(jnp.int32, (width, VECS), 0)
-    summed = jnp.zeros((24, width), F32)
-    for kind in range(1, 8):
+    hits, terms = [], []
+    for kind in KINDS:
         value = got[place ^ kind]
-        terms = []
+        parts = []
         for _ in range(3):
-            terms.append(value.astype(BF16))
-            value = value - terms[-1].astype(F32)
-        hit = jnp.where(lane == lanes[kind : kind + 1, :], 1.0, 0.0).astype(BF16)
-        summed = summed + lax.dot_general(
-            jnp.concatenate([t.astype(F32) for t in terms], axis=0).astype(BF16), hit,
-            (((1,), (1,)), ((), ())), preferred_element_type=F32,
-        )
+            parts.append(value.astype(BF16).astype(F32))
+            value = value - parts[-1]
+        terms.append(jnp.concatenate(parts, axis=0).astype(BF16))
+        hits.append(jnp.where(lane == lanes[kind : kind + 1, :], 1.0, 0.0).astype(BF16))
+    summed = lax.dot_general(
+        jnp.concatenate(terms, axis=1), jnp.concatenate(hits, axis=1), (((1,), (1,)), ((), ())),
+        preferred_element_type=F32,
+    )
     return summed[0:8] + summed[8:16] + summed[16:24]
 
 
-def merge_kernel(parity, held, lanes, got, out, sent):
-    value = held[...] + spread(got, lanes, place_of(parity), FIRST)
+def merge_kernel(held, lanes, got, out, sent):
+    value = held[...] + spread(got, lanes, place_of(), FIRST)
     out[...] = value[:, 0:ATOMS]
-    send(sent, value[:, SECOND:], 32, 7 - place_of(parity))
-
-
-def finish_kernel(parity, held, lanes, got, out):
-    value = held[...] + spread(got, lanes, 7 - place_of(parity), ATOMS)
+    send(sent, value, SECOND_AT, SECOND_SIZE, 7 - place_of())
+
+
+def finish_kernel(held, lanes, got, out):
+    value = held[...] + spread(got, lanes, 7 - place_of(), ATOMS)
     out[...] = value[0:3]
 
 
@@ -439,10 +463,14 @@
     return basis
 
 
+def start_of(kind, starts):
+    return sum(jnp.where(kind == k, at, 0) for k, at in starts.items())
+
+
 def second_lane(basis, cells, kinds):
     inner = number(basis, [jnp.where(k, 0, c) for c, k in zip(cells, kinds)], [jnp.where(k, 1, 4) for k in kinds])
     kind = 4 * kinds[0] + 2 * kinds[1] + kinds[2]
-    return jnp.where(kind > 0, SECOND + 32 * kind + inner, number(basis, cells, (CX, CY, CZ)))
+    return jnp.where(kind > 0, start_of(kind, SECOND_AT) + inner, number(basis, cells, (CX, CY, CZ)))
 
 
 def landing_lanes(parity):
@@ -498,7 +526,7 @@
     digits = [jnp.where(f, 0, jnp.where(s, 4, c)) for f, s, c in zip(firsts, seconds, cells)]
     inner = number(basis, digits, [jnp.where(f, 1, 5) for f in firsts])
     lanes = second_lane(basis, cells, [s.astype(jnp.int32) for s in seconds])
-    lanes = jnp.where(kind > 0, FIRST + 64 * kind + inner, lanes)
+    lanes = jnp.where(kind > 0, start_of(kind, FIRST_AT) + inner, lanes)
     return slots.astype(jnp.int32), lanes.astype(jnp.int32)
 
 
@@ -509,23 +537,23 @@
 BACK_PLAINS = [plain(ROWS_Z), plain(ROWS_Z)]
 
 
-def exchange(parity, level, own, out1, out2, work):
+def exchange(level, own, out1, out2, work):
     dtype = out1.dtype
     rows_x, rows_y = ((ROWS_X, VECS), F32), ((ROWS_Y, VECS), F32)
     x2, x1 = swapped(out2, "gx", 1), swapped(out1, "gx", 0)
     out2, u1, u2, level = call(
-        second_y_kernel, [((ROWS_Y, VECS), dtype), rows_x, rows_x, ((8, VECS), F32)], [SMEM] + [VMEM] * 4,
-        (parity, x2, x1, level, own), [plain(ATOMS), plain(ROWS_Y)],
+        second_y_kernel, [((ROWS_Y, VECS), dtype), rows_x, rows_x, ((8, VECS), F32)],
+        (x2, x1, level, own), [plain(ATOMS), plain(ROWS_Y)],
     )
     y2 = swapped(out2, "gy", 1)
     (out1,) = call(
-        first_y_kernel, [((ROWS_Y, VECS), dtype)], [SMEM] + [VMEM] * 4, (parity, level, own, u1, u2),
+        first_y_kernel, [((ROWS_Y, VECS), dtype)], (level, own, u1, u2),
         [plain(ATOMS), plain(ROWS_Y)],
     )
     y1 = swapped(out1, "gy", 0)
     out1, out2, v1, v2 = call(
-        faces_z_kernel, [((ROWS_Z, VECS), dtype)] * 2 + [rows_y] * 2, [SMEM] + [VMEM] * 6,
-        (parity, y2, y1, level, own, u1, u2), [plain(ATOMS)] + BACK_PLAINS,
+        faces_z_kernel, [((ROWS_Z, VECS), dtype)] * 2 + [rows_y] * 2,
+        (y2, y1, level, own, u1, u2), [plain(ATOMS)] + BACK_PLAINS,
     )
     z1, z2 = swapped(out1, "gz", 0), swapped(out2, "gz", 1)
     return work(own, u1, u2, v1, v2), (z1, z2)
@@ -534,6 +562,7 @@
 def shards(noise_vectors, hamiltonian, derivative, neighbours, coefficients):
     parity = jnp.stack([lax.axis_index(axis) % 2 for axis in AXES]).astype(jnp.int32)
     slots, lanes = slots_of(neighbours, parity)
+    coefs = jnp.broadcast_to(coefficients[:, None], (4, VECS))
     lattice = noise_vectors.reshape(ORB, 2, CX, CY * CZ, VECS)
     low = lattice[:, :, 0].reshape(ORB * NX, VECS)
     high = lattice[:, :, CX - 1].reshape(ORB * NX, VECS)
@@ -542,7 +571,7 @@
     out1 = jnp.concatenate([jnp.where(even, high, low), room])
     out2 = jnp.concatenate([jnp.where(even, low, high), room])
     (rows,) = call(
-        prep_kernel, [((ATOMS, 16, 256), BF16)], [VMEM], (hamiltonian.transpose(1, 2, 0, 3),),
+        prep_kernel, [((ATOMS, 16, 256), BF16)], (hamiltonian.transpose(1, 2, 0, 3),),
         [plain(256), pltpu.VMEM((2, ATOMS * 16, 128), F32)], flops=1 << 22,
     )
     whole = ((ORB, ATOMS, VECS), F32)
@@ -551,46 +580,48 @@
     half = ((ATOMS // 2 * 16, VECS), F32)
     front_loose, loose, applied = plain(BEFORE_Z * 16), plain((SLOTS - BEFORE_Z) * 16), plain(ATOMS * 16)
     faces = [plain(ROWS_X), plain(ROWS_X)]
+    table = [pltpu.SMEM((NEIGH, ATOMS), jnp.int32), pltpu.SemaphoreType.DMA]
 
     def work(*vectors):
         width = 128 if vectors[0].dtype == BF16 else 256
         return call(
-            front_kernel, [((BEFORE_Z, 16, width), BF16), half], [SMEM] + [VMEM] * 6, (slots, rows) + vectors,
-            [front_loose], flops=1 << 29,
+            front_kernel, [((BEFORE_Z, 16, width), BF16), half], (slots, rows) + vectors,
+            table + [front_loose], flops=1 << 29,
         )
 
-    fronts, ghosts = exchange(parity, jnp.zeros((8, VECS), F32), noise_vectors, out1, out2, work)
+    fronts, ghosts = exchange(jnp.zeros((8, VECS), F32), noise_vectors, out1, out2, work)
     first, total, out1, out2, level, noise_tiles = call(
-        first_kernel, [whole, whole, plane, plane, tile, ((SLOTS, 16, VECS), BF16)], [SMEM] * 3 + [VMEM] * 6,
-        (parity, coefficients, slots, rows, noise_vectors, *fronts, *ghosts),
-        [loose, applied] + faces + BACK_PLAINS, flops=1 << 29, mib=24,
-    )
-    fronts, ghosts = exchange(parity, level, first, out1, out2, work)
+        first_kernel, [whole, whole, plane, plane, tile, ((SLOTS, 16, VECS), BF16)],
+        (coefs, slots, rows, noise_vectors, *fronts, *ghosts),
+        table + [loose, applied] + faces + BACK_PLAINS, flops=1 << 29,
+    )
+    fronts, ghosts = exchange(level, first, out1, out2, work)
     second, total, out1, out2, level = call(
-        second_kernel, [whole, whole, plane, plane, tile], [SMEM] * 3 + [VMEM] * 7,
-        (parity, coefficients, slots, rows, noise_vectors, total, *fronts, *ghosts),
-        [pltpu.VMEM((SLOTS, 16, 256), BF16), loose, applied] + faces + BACK_PLAINS, flops=1 << 29, mib=24,
+        second_kernel, [whole, whole, plane, plane, tile],
+        (coefs, slots, rows, noise_vectors, total, *fronts, *ghosts),
+        table + [pltpu.VMEM((SLOTS, 16, 256), BF16), loose, applied] + faces + BACK_PLAINS, flops=1 << 29,
     )
 
     def last_work(*vectors):
         return call(
-            front_third_kernel, [((BEFORE_Z, 16, 256), BF16), half, ((2,) + half[0], F32)], [SMEM] * 2 + [VMEM] * 9,
-            (coefficients, slots, rows, first, total, noise_tiles) + vectors,
-            [front_loose, applied], flops=1 << 30, mib=24,
+            front_third_kernel, [((BEFORE_Z, 16, 256), BF16), half, ((2,) + half[0], F32)],
+            (coefs, slots, rows, first, total, noise_tiles) + vectors,
+            table + [front_loose, applied], flops=1 << 30,
         )
 
-    fronts, ghosts = exchange(parity, level, second, out1, out2, last_work)
+    fronts, ghosts = exchange(level, second, out1, out2, last_work)
     eight = ((8, 8, 128), F32)
+    slopes = derivative.transpose(0, 2, 3, 1, 4)
     lanes1, lanes2 = landing_lanes(parity)
     weighted, held, sent = call(
-        third_kernel, [whole, ((8, FIRST), F32), eight], [SMEM] * 3 + [VMEM] * 11,
-        (parity, coefficients, slots, lanes, rows, first, total, noise_tiles, derivative.transpose(0, 2, 3, 1, 4), *fronts, *ghosts),
-        [pltpu.VMEM((SLOTS, 16, 256), BF16), loose, applied, pltpu.VMEM((2, ATOMS * 16, 128), F32), plain(256),
-         plain(NEIGH * 16)] + BACK_PLAINS,
-        flops=1 << 30, mib=32,
-    )
-    held, sent = call(merge_kernel, [tile, eight], [SMEM] + [VMEM] * 3, (parity, held, lanes1, trade_all(sent, 0)))
-    (forces,) = call(finish_kernel, [((3, ATOMS), F32)], [SMEM] + [VMEM] * 3, (parity, held, lanes2, trade_all(sent, 1)))
+        third_kernel, [whole, ((8, FIRST), F32), eight],
+        (coefs, slots, lanes, rows, first, total, noise_tiles, slopes, *fronts, *ghosts),
+        table + [pltpu.VMEM((SLOTS, 16, 256), BF16), loose, applied, pltpu.VMEM((2, ATOMS * 16, 128), F32), plain(256),
+         plain(NEIGH * 16), pltpu.VMEM(slopes.shape, BF16), pltpu.SemaphoreType.DMA] + BACK_PLAINS,
+        flops=1 << 30, in_hbm=(7,),
+    )
+    held, sent = call(merge_kernel, [tile, eight], (held, lanes1, trade_all(sent, 0)))
+    (forces,) = call(finish_kernel, [((3, ATOMS), F32)], (held, lanes2, trade_all(sent, 1)))
     return weighted, forces
 
 

time: 155 us -> 144 us (0.929)
  Pallas kernels: 40.5 us -> 24.7 us
  waiting for transfers between devices: 21.3 us -> 24.2 us
    pallas_call x18, Pallas kernels: 40.5 us -> 24.7 us  [call(): pl.pallas_call(kernel, out_shape=shapes, in_specs=[HBM if k in in_hbm els...]
    ppermute x18, waiting for transfers between devices: 16 us -> 18.9 us  [swapped(): return lax.ppermute(value, axis, pairs + [(b, a) for a, b in pairs])]
    unnamed x18 -> x16, local copies, waits for them, and re-layouts: 3.43 us -> 4.66 us
  transfers between devices with their start and end apart: 19 -> 19, of which waited for: 12 -> 12; matrix products, arithmetic and copies ran while one was open for 1% -> 1% of each run, Pallas kernels for 11% -> 7%
where the time goes in v4:
time: 144 us
  starting transfers between devices  76.3 us (53%)
  Pallas kernels  24.7 us (17%)
  waiting for transfers between devices  24.2 us (17%)
  blocking collectives  10.6 us (7%)
  local copies, waits for them, and re-layouts  4.75 us (3%)
  other arithmetic  1.83 us (1%)
    ppermute x18, starting transfers between devices, swapped(): return lax.ppermute(value, axis, pairs + [(b, a) for a, b in pairs])  71 us
    pallas_call x18, Pallas kernels, call(): pl.pallas_call(kernel, out_shape=shapes, in_specs=[HBM if k in in_hbm els...  24.7 us
    ppermute x18, waiting for transfers between devices, swapped(): return lax.ppermute(value, axis, pairs + [(b, a) for a, b in pairs])  18.9 us
    all_to_all x1, blocking collectives, trade_all(): lax.all_to_all(sent, AXES, 0, 0, tiled=True, axis_index_groups=blocks(sec...  10.6 us
    all_to_all x1, waiting for transfers between devices, trade_all(): lax.all_to_all(sent, AXES, 0, 0, tiled=True, axis_index_groups=blocks(sec...  5.25 us
    all_to_all x1, starting transfers between devices, trade_all(): lax.all_to_all(sent, AXES, 0, 0, tiled=True, axis_index_groups=blocks(sec...  5.25 us
    unnamed x16, local copies, waits for them, and re-layouts  4.66 us
  transfers between devices with their start and end apart: 19, of which 12 were waited for; matrix products, arithmetic and copies ran while one was open for 1% of the time, Pallas kernels for 7%

profile of v4, /device:TPU:1, one launch (start us, length us, event | category | flops | bytes accessed | tf_op | source)
XLA Modules:
  0.0 143.5 jit_solution(8909127539219008931)
XLA Ops:
  1.7 7.9 %collective-permute-start = (bf16[304,128]{1,0:T(8,128)(2,1)S(1)}, bf16[304,128]{1,0:T(8,128)(2,1)S(1)}, u32[]{:S(2)}, u32[]{:S(2)}) collective-permute-start(bf16[304,128]{1,0:T(8,128)(2,1)S(1)} %concatenate.6), channel_id=1, source_target_pairs={{64,128},{192,256},{320,384},{448,0},{128,64},{256,192},{384,320},... | collective-permute-start | bytes 233480 | tf_op jit(solution)/shard_map/ppermute | solution.py:61
  13.6 2.7 %collective-permute-done.1.x1 = bf16[304,128]{1,0:T(8,128)(2,1)S(1)} collective-permute-done((bf16[304,128]{1,0:T(8,128)(2,1)S(1)}, bf16[304,128]{1,0:T(8,128)(2,1)S(1)}, u32[]{:S(2)}, u32[]{:S(2)}) %collective-permute-start.1) | collective-permute-done | bytes 77856 | tf_op jit(solution)/shard_map/ppermute | solution.py:61
  17.3 4.2 %collective-permute-start.2 = (bf16[448,128]{1,0:T(8,128)(2,1)S(1)}, bf16[448,128]{1,0:T(8,128)(2,1)S(1)}, u32[]{:S(2)}, u32[]{:S(2)}) collective-permute-start(bf16[448,128]{1,0:T(8,128)(2,1)S(1)} %get-tuple-element.51), channel_id=1, source_target_pairs={{16,32},{48,0},{32,16},{0,48},{17,33},{49,1},{33,17},{1,49},{18,34... | collective-permute-start | bytes 344072 | tf_op jit(solution)/shard_map/ppermute | solution.py:61
  25.0 3.5 %collective-permute-start.4 = (bf16[656,128]{1,0:T(8,128)(2,1)S(1)}, bf16[656,128]{1,0:T(8,128)(2,1)S(1)}, u32[]{:S(2)}, u32[]{:S(2)}) collective-permute-start(bf16[656,128]{1,0:T(8,128)(2,1)S(1)} %get-tuple-element.57), channel_id=1, source_target_pairs={{0,1},{2,3},{4,5},{6,7},{8,9},{10,11},{12,13},{14,15},{1,0},{3,2},... | collective-permute-start | bytes 503816 | tf_op jit(solution)/shard_map/ppermute | solution.py:61
  28.6 10.2 %collective-permute-start.5 = (bf16[656,128]{1,0:T(8,128)(2,1)S(1)}, bf16[656,128]{1,0:T(8,128)(2,1)S(1)}, u32[]{:S(2)}, u32[]{:S(2)}) collective-permute-start(bf16[656,128]{1,0:T(8,128)(2,1)S(1)} %get-tuple-element.58), channel_id=1, source_target_pairs={{1,2},{3,4},{5,6},{7,8},{9,10},{11,12},{13,14},{15,0},{2,1},{4,3},... | collective-permute-start | bytes 503816 | tf_op jit(solution)/shard_map/ppermute | solution.py:61
  42.1 2.2 %shard_map.73 = (f32[9,128,128]{2,1,0:T(8,128)S(1)}, f32[9,128,128]{2,1,0:T(8,128)S(1)}, s16[304,128]{1,0:T(8,128)(2,1)S(1)}, s16[304,128]{1,0:T(8,128)(2,1)S(1)...) custom-call(f32[4,128]{1,0:T(4,128)S(1)} %broadcast_in_dim.201.coef, s32[15,128]{1,0:T(8,128)S(1)} %add_select_fusion.15.slots, ...), custom_call_target="tpu_custom_call" | custom-call | flops 536870912 | bytes 6501888 | tf_op jit(solution)/shard_map/pallas_call | solution.py:43
  45.5 4.3 %collective-permute-start.6 = (s16[304,128]{1,0:T(8,128)(2,1)S(1)}, s16[304,128]{1,0:T(8,128)(2,1)S(1)}, u32[]{:S(2)}, u32[]{:S(2)}) collective-permute-start(s16[304,128]{1,0:T(8,128)(2,1)S(1)} %get-tuple-element.61), channel_id=1, source_target_pairs={{64,128},{192,256},{320,384},{448,0},{128,64},{256,192},{384,320},... | collective-permute-start | bytes 233480 | tf_op jit(solution)/shard_map/ppermute | solution.py:61
  51.8 2.5 %collective-permute-done.6.x2 = s16[304,128]{1,0:T(8,128)(2,1)S(1)} collective-permute-done((s16[304,128]{1,0:T(8,128)(2,1)S(1)}, s16[304,128]{1,0:T(8,128)(2,1)S(1)}, u32[]{:S(2)}, u32[]{:S(2)}) %collective-permute-start.6) | collective-permute-done | bytes 77856 | tf_op jit(solution)/shard_map/ppermute | solution.py:61
  54.3 2.5 %collective-permute-done.7.x1 = s16[304,128]{1,0:T(8,128)(2,1)S(1)} collective-permute-done((s16[304,128]{1,0:T(8,128)(2,1)S(1)}, s16[304,128]{1,0:T(8,128)(2,1)S(1)}, u32[]{:S(2)}, u32[]{:S(2)}) %collective-permute-start.7) | collective-permute-done | bytes 77856 | tf_op jit(solution)/shard_map/ppermute | solution.py:61
  56.9 4.9 %collective-permute-start.8 = (s16[448,128]{1,0:T(8,128)(2,1)S(1)}, s16[448,128]{1,0:T(8,128)(2,1)S(1)}, u32[]{:S(2)}, u32[]{:S(2)}) collective-permute-start(s16[448,128]{1,0:T(8,128)(2,1)S(1)} %get-tuple-element.66), channel_id=1, source_target_pairs={{16,32},{48,0},{32,16},{0,48},{17,33},{49,1},{33,17},{1,49},{18,34... | collective-permute-start | bytes 344072 | tf_op jit(solution)/shard_map/ppermute | solution.py:61
  67.7 4.9 %collective-permute-start.11 = (s16[656,128]{1,0:T(8,128)(2,1)S(1)}, s16[656,128]{1,0:T(8,128)(2,1)S(1)}, u32[]{:S(2)}, u32[]{:S(2)}) collective-permute-start(s16[656,128]{1,0:T(8,128)(2,1)S(1)} %get-tuple-element.73), channel_id=1, source_target_pairs={{1,2},{3,4},{5,6},{7,8},{9,10},{11,12},{13,14},{15,0},{2,1},{4,3},... | collective-permute-start | bytes 503816 | tf_op jit(solution)/shard_map/ppermute | solution.py:61
  72.6 2.6 %shard_map.77 = (bf16[288,16,256]{2,1,0:T(8,128)(2,1)S(1)}, f32[1024,128]{1,0:T(8,128)S(1)}) custom-call(s32[15,128]{1,0:T(8,128)S(1)} %add_select_fusion.15.slots, bf16[128,16,256]{2,1,0:T(8,128)(2,1)S(1)} %shard_map.68.rows, f32[9,128,128]{2,1,0:T(8,128)S(1)} %get-tuple-element.59.own.prev, f32[304,128]{1,0:T(8,128)S(1)} %get-tuple-element.64.u1, ...), custom_call_target="tpu_custom_call" | custom-call | flops 536870912 | bytes 5299712 | tf_op jit(solution)/shard_map/pallas_call | solution.py:43
  76.7 2.9 %shard_map.78 = (f32[9,128,128]{2,1,0:T(8,128)S(1)}, f32[9,128,128]{2,1,0:T(8,128)S(1)}, s16[304,128]{1,0:T(8,128)(2,1)S(1)}, s16[304,128]{1,0:T(8,128)(2,1)S(1)}, f32[8,128]{1,0:T(8,128)S(1)}) custom-call(f32[4,128]{1,0:T(4,128)S(1)} %broadcast_in_dim.201.coef, s32[15,128]{1,0:T(8,128)S(1)} %add_select_fusion.15.slots, ...), custom_call_target="tpu_custom_call" | custom-call | flops 536870912 | bytes 6501888 | tf_op jit(solution)/shard_map/pallas_call | solution.py:43
  79.6 6.4 %collective-permute-start.12 = (s16[304,128]{1,0:T(8,128)(2,1)S(1)}, s16[304,128]{1,0:T(8,128)(2,1)S(1)}, u32[]{:S(2)}, u32[]{:S(2)}) collective-permute-start(s16[304,128]{1,0:T(8,128)(2,1)S(1)} %get-tuple-element.77), channel_id=1, source_target_pairs={{64,128},{192,256},{320,384},{448,0},{128,64},{256,192},{384,320},... | collective-permute-start | bytes 233480 | tf_op jit(solution)/shard_map/ppermute | solution.py:61
  88.4 4.3 %collective-permute-done.13.x1 = s16[304,128]{1,0:T(8,128)(2,1)S(1)} collective-permute-done((s16[304,128]{1,0:T(8,128)(2,1)S(1)}, s16[304,128]{1,0:T(8,128)(2,1)S(1)}, u32[]{:S(2)}, u32[]{:S(2)}) %collective-permute-start.13) | collective-permute-done | bytes 77856 | tf_op jit(solution)/shard_map/ppermute | solution.py:61
  93.5 3.3 %collective-permute-start.14 = (s16[448,128]{1,0:T(8,128)(2,1)}, s16[448,128]{1,0:T(8,128)(2,1)S(1)}, u32[]{:S(2)}, u32[]{:S(2)}) collective-permute-start(s16[448,128]{1,0:T(8,128)(2,1)} %get-tuple-element.82), channel_id=1, source_target_pairs={{16,32},{48,0},{32,16},{0,48},{17,33},{49,1},{33,17},{1,49},{18,34... | collective-permute-start | bytes 344072 | tf_op jit(solution)/shard_map/ppermute | solution.py:61
  96.9 2.9 %collective-permute-start.15 = (s16[448,128]{1,0:T(8,128)(2,1)S(1)}, s16[448,128]{1,0:T(8,128)(2,1)S(1)}, u32[]{:S(2)}, u32[]{:S(2)}) collective-permute-start(s16[448,128]{1,0:T(8,128)(2,1)S(1)} %shard_map.80), channel_id=1, source_target_pairs={{0,16},{32,48},{16,0},{48,32},{1,17},{33,49},{17,1},{49,33},{2,18}... | collective-permute-start | bytes 344072 | tf_op jit(solution)/shard_map/ppermute | solution.py:61
  101.0 2.2 %collective-permute-start.16 = (s16[656,128]{1,0:T(8,128)(2,1)S(1)}, s16[656,128]{1,0:T(8,128)(2,1)S(1)}, u32[]{:S(2)}, u32[]{:S(2)}) collective-permute-start(s16[656,128]{1,0:T(8,128)(2,1)S(1)} %get-tuple-element.89), channel_id=1, source_target_pairs={{0,1},{2,3},{4,5},{6,7},{8,9},{10,11},{12,13},{14,15},{1,0},{3,2},... | collective-permute-start | bytes 503816 | tf_op jit(solution)/shard_map/ppermute | solution.py:61
  103.1 4.8 %collective-permute-start.17 = (s16[656,128]{1,0:T(8,128)(2,1)S(1)}, s16[656,128]{1,0:T(8,128)(2,1)S(1)}, u32[]{:S(2)}, u32[]{:S(2)}) collective-permute-start(s16[656,128]{1,0:T(8,128)(2,1)S(1)} %get-tuple-element.90), channel_id=1, source_target_pairs={{1,2},{3,4},{5,6},{7,8},{9,10},{11,12},{13,14},{15,0},{2,1},{4,3},... | collective-permute-start | bytes 503816 | tf_op jit(solution)/shard_map/ppermute | solution.py:61
  109.4 4.4 %shard_map.82 = (bf16[288,16,256]{2,1,0:T(8,128)(2,1)S(1)}, f32[1024,128]{1,0:T(8,128)S(1)}, f32[2,1024,128]{2,1,0:T(8,128)S(1)}) custom-call(f32[4,128]{1,0:T(4,128)S(1)} %broadcast_in_dim.201.coef, s32[15,128]{1,0:T(8,128)S(1)} %add_select_fusion.15.slots, bf16[128,16,256]{2,1,0:T(8,128)(2,1)S(1)} %shard_map.68.rows, ...), custom_call_target="tpu_custom_call" | custom-call | flops 1073741824 | bytes 9299456 | tf_op jit(solution)/shard_map/pallas_call | solution.py:43
  113.8 6.8 %shard_map.83 = (f32[9,128,128]{2,1,0:T(8,128)}, f32[8,256]{1,0:T(8,128)S(1)}, f32[8,8,128]{2,1,0:T(8,128)}) custom-call(f32[4,128]{1,0:T(4,128)S(1)} %broadcast_in_dim.201.coef, s32[15,128]{1,0:T(8,128)S(1)} %add_select_fusion.15.slots, s32[15,128]{1,0:T(8,128)S(1)} %get-tuple-element.96.lanes, bf16[128,16,256]{2,1,0:T(8,128)(2,1)S(1)} %shard_map.68.rows, ...), custom_call_target="tpu_custom_call" | custom-call | flops 1073741824 | bytes 9847040 | tf_op jit(solution)/shard_map/pallas_call | solution.py:43
  120.6 5.2 %all-to-all-start = ((f32[8,8,128]{2,1,0:T(8,128)}), f32[8,8,128]{2,1,0:T(8,128)S(1)}, u32[]{:S(2)}, u32[]{:S(2)}) async-start(f32[8,8,128]{2,1,0:T(8,128)} %get-tuple-element.93), calls=%async_computation | async-start | bytes 65536 | tf_op jit(solution)/shard_map/all_to_all | solution.py:457
  126.5 5.3 %all-to-all-done.got = f32[8,8,128]{2,1,0:T(8,128)S(1)} async-done(((f32[8,8,128]{2,1,0:T(8,128)}), f32[8,8,128]{2,1,0:T(8,128)S(1)}, u32[]{:S(2)}, u32[]{:S(2)}) %all-to-all-start) | async-done | bytes 32800 | tf_op jit(solution)/shard_map/all_to_all | solution.py:457
  132.1 10.6 %all_to_all.10.got = f32[8,8,128]{2,1,0:T(8,128)S(1)} all-to-all(f32[8,8,128]{2,1,0:T(8,128)S(1)} %get-tuple-element.95), channel_id=1, replica_groups={{81,82,97,98,145,146,161,162},{83,84,99,100,147,148,163,164},{85,86,101..., dimensions={0} | all-to-all | bytes 65536 | tf_op jit(solution)/shard_map/all_to_all | solution.py:457
  (63 shorter events, 30.8 us)
Async XLA Ops:
  0.6 20.9 %copy-start.1 = (bf16[9,128,128]{2,1,0:T(8,128)(2,1)S(1)}, bf16[9,128,128]{2,1,0:T(8,128)(2,1)}, u32[]{:S(2)}) copy-start(bf16[9,128,128]{2,1,0:T(8,128)(2,1)} %prev.1) | copy-start | bytes 884740
  0.6 22.9 %copy-start.6 = (s32[128,15]{0,1:T(8,128)S(1)}, s32[128,15]{0,1:T(8,128)}, u32[]{:S(2)}) copy-start(s32[128,15]{0,1:T(8,128)} %param.8) | copy-start | bytes 23044
  1.7 11.9 %collective-permute-start = (bf16[304,128]{1,0:T(8,128)(2,1)S(1)}, bf16[304,128]{1,0:T(8,128)(2,1)S(1)}, u32[]{:S(2)}, u32[]{:S(2)}) collective-permute-start(bf16[304,128]{1,0:T(8,128)(2,1)S(1)} %concatenate.6), channel_id=1, source_target_pairs={{64,128},{192,256},{320,384},{448,0},{128,64},{256,192},{384,320},... | collective-permute-start | bytes 233480 | tf_op jit(solution)/shard_map/ppermute | solution.py:61
  9.6 6.6 %collective-permute-start.1 = (bf16[304,128]{1,0:T(8,128)(2,1)S(1)}, bf16[304,128]{1,0:T(8,128)(2,1)S(1)}, u32[]{:S(2)}, u32[]{:S(2)}) collective-permute-start(bf16[304,128]{1,0:T(8,128)(2,1)S(1)} %concatenate.7), channel_id=1, source_target_pairs={{0,64},{128,192},{256,320},{384,448},{64,0},{192,128},{320,256},{4... | collective-permute-start | bytes 233480 | tf_op jit(solution)/shard_map/ppermute | solution.py:61
  13.6 28.4 %copy-start.7 = (f32[4]{0:T(128)S(1)}, f32[4]{0:T(128)}, u32[]{:S(2)}) copy-start(f32[4]{0:T(128)} %param.9) | copy-start | bytes 52
  17.3 7.3 %collective-permute-start.2 = (bf16[448,128]{1,0:T(8,128)(2,1)S(1)}, bf16[448,128]{1,0:T(8,128)(2,1)S(1)}, u32[]{:S(2)}, u32[]{:S(2)}) collective-permute-start(bf16[448,128]{1,0:T(8,128)(2,1)S(1)} %get-tuple-element.51), channel_id=1, source_target_pairs={{16,32},{48,0},{32,16},{0,48},{17,33},{49,1},{33,17},{1,49},{18,34... | collective-permute-start | bytes 344072 | tf_op jit(solution)/shard_map/ppermute | solution.py:61
  21.6 3.2 %collective-permute-start.3 = (bf16[448,128]{1,0:T(8,128)(2,1)S(1)}, bf16[448,128]{1,0:T(8,128)(2,1)S(1)}, u32[]{:S(2)}, u32[]{:S(2)}) collective-permute-start(bf16[448,128]{1,0:T(8,128)(2,1)S(1)} %shard_map.70), channel_id=1, source_target_pairs={{0,16},{32,48},{16,0},{48,32},{1,17},{33,49},{17,1},{49,33},{2,18}... | collective-permute-start | bytes 344072 | tf_op jit(solution)/shard_map/ppermute | solution.py:61
  25.0 15.7 %collective-permute-start.4 = (bf16[656,128]{1,0:T(8,128)(2,1)S(1)}, bf16[656,128]{1,0:T(8,128)(2,1)S(1)}, u32[]{:S(2)}, u32[]{:S(2)}) collective-permute-start(bf16[656,128]{1,0:T(8,128)(2,1)S(1)} %get-tuple-element.57), channel_id=1, source_target_pairs={{0,1},{2,3},{4,5},{6,7},{8,9},{10,11},{12,13},{14,15},{1,0},{3,2},... | collective-permute-start | bytes 503816 | tf_op jit(solution)/shard_map/ppermute | solution.py:61
  28.6 13.4 %collective-permute-start.5 = (bf16[656,128]{1,0:T(8,128)(2,1)S(1)}, bf16[656,128]{1,0:T(8,128)(2,1)S(1)}, u32[]{:S(2)}, u32[]{:S(2)}) collective-permute-start(bf16[656,128]{1,0:T(8,128)(2,1)S(1)} %get-tuple-element.58), channel_id=1, source_target_pairs={{1,2},{3,4},{5,6},{7,8},{9,10},{11,12},{13,14},{15,0},{2,1},{4,3},... | collective-permute-start | bytes 503816 | tf_op jit(solution)/shard_map/ppermute | solution.py:61
  45.5 8.7 %collective-permute-start.6 = (s16[304,128]{1,0:T(8,128)(2,1)S(1)}, s16[304,128]{1,0:T(8,128)(2,1)S(1)}, u32[]{:S(2)}, u32[]{:S(2)}) collective-permute-start(s16[304,128]{1,0:T(8,128)(2,1)S(1)} %get-tuple-element.61), channel_id=1, source_target_pairs={{64,128},{192,256},{320,384},{448,0},{128,64},{256,192},{384,320},... | collective-permute-start | bytes 233480 | tf_op jit(solution)/shard_map/ppermute | solution.py:61
  49.9 6.9 %collective-permute-start.7 = (s16[304,128]{1,0:T(8,128)(2,1)S(1)}, s16[304,128]{1,0:T(8,128)(2,1)S(1)}, u32[]{:S(2)}, u32[]{:S(2)}) collective-permute-start(s16[304,128]{1,0:T(8,128)(2,1)S(1)} %get-tuple-element.62), channel_id=1, source_target_pairs={{0,64},{128,192},{256,320},{384,448},{64,0},{192,128},{320,256},{4... | collective-permute-start | bytes 233480 | tf_op jit(solution)/shard_map/ppermute | solution.py:61
  56.9 8.6 %collective-permute-start.8 = (s16[448,128]{1,0:T(8,128)(2,1)S(1)}, s16[448,128]{1,0:T(8,128)(2,1)S(1)}, u32[]{:S(2)}, u32[]{:S(2)}) collective-permute-start(s16[448,128]{1,0:T(8,128)(2,1)S(1)} %get-tuple-element.66), channel_id=1, source_target_pairs={{16,32},{48,0},{32,16},{0,48},{17,33},{49,1},{33,17},{1,49},{18,34... | collective-permute-start | bytes 344072 | tf_op jit(solution)/shard_map/ppermute | solution.py:61
  61.9 3.7 %collective-permute-start.9 = (s16[448,128]{1,0:T(8,128)(2,1)S(1)}, s16[448,128]{1,0:T(8,128)(2,1)S(1)}, u32[]{:S(2)}, u32[]{:S(2)}) collective-permute-start(s16[448,128]{1,0:T(8,128)(2,1)S(1)} %shard_map.75), channel_id=1, source_target_pairs={{0,16},{32,48},{16,0},{48,32},{1,17},{33,49},{17,1},{49,33},{2,18}... | collective-permute-start | bytes 344072 | tf_op jit(solution)/shard_map/ppermute | solution.py:61
  65.8 9.4 %collective-permute-start.10 = (s16[656,128]{1,0:T(8,128)(2,1)S(1)}, s16[656,128]{1,0:T(8,128)(2,1)S(1)}, u32[]{:S(2)}, u32[]{:S(2)}) collective-permute-start(s16[656,128]{1,0:T(8,128)(2,1)S(1)} %get-tuple-element.72), channel_id=1, source_target_pairs={{0,1},{2,3},{4,5},{6,7},{8,9},{10,11},{12,13},{14,15},{1,0},{3,2},... | collective-permute-start | bytes 503816 | tf_op jit(solution)/shard_map/ppermute | solution.py:61
  67.7 9.0 %collective-permute-start.11 = (s16[656,128]{1,0:T(8,128)(2,1)S(1)}, s16[656,128]{1,0:T(8,128)(2,1)S(1)}, u32[]{:S(2)}, u32[]{:S(2)}) collective-permute-start(s16[656,128]{1,0:T(8,128)(2,1)S(1)} %get-tuple-element.73), channel_id=1, source_target_pairs={{1,2},{3,4},{5,6},{7,8},{9,10},{11,12},{13,14},{15,0},{2,1},{4,3},... | collective-permute-start | bytes 503816 | tf_op jit(solution)/shard_map/ppermute | solution.py:61
  79.6 8.8 %collective-permute-start.12 = (s16[304,128]{1,0:T(8,128)(2,1)S(1)}, s16[304,128]{1,0:T(8,128)(2,1)S(1)}, u32[]{:S(2)}, u32[]{:S(2)}) collective-permute-start(s16[304,128]{1,0:T(8,128)(2,1)S(1)} %get-tuple-element.77), channel_id=1, source_target_pairs={{64,128},{192,256},{320,384},{448,0},{128,64},{256,192},{384,320},... | collective-permute-start | bytes 233480 | tf_op jit(solution)/shard_map/ppermute | solution.py:61
  86.1 6.6 %collective-permute-start.13 = (s16[304,128]{1,0:T(8,128)(2,1)S(1)}, s16[304,128]{1,0:T(8,128)(2,1)S(1)}, u32[]{:S(2)}, u32[]{:S(2)}) collective-permute-start(s16[304,128]{1,0:T(8,128)(2,1)S(1)} %get-tuple-element.78), channel_id=1, source_target_pairs={{0,64},{128,192},{256,320},{384,448},{64,0},{192,128},{320,256},{4... | collective-permute-start | bytes 233480 | tf_op jit(solution)/shard_map/ppermute | solution.py:61
  93.5 6.4 %collective-permute-start.14 = (s16[448,128]{1,0:T(8,128)(2,1)}, s16[448,128]{1,0:T(8,128)(2,1)S(1)}, u32[]{:S(2)}, u32[]{:S(2)}) collective-permute-start(s16[448,128]{1,0:T(8,128)(2,1)} %get-tuple-element.82), channel_id=1, source_target_pairs={{16,32},{48,0},{32,16},{0,48},{17,33},{49,1},{33,17},{1,49},{18,34... | collective-permute-start | bytes 344072 | tf_op jit(solution)/shard_map/ppermute | solution.py:61
  96.9 3.8 %collective-permute-start.15 = (s16[448,128]{1,0:T(8,128)(2,1)S(1)}, s16[448,128]{1,0:T(8,128)(2,1)S(1)}, u32[]{:S(2)}, u32[]{:S(2)}) collective-permute-start(s16[448,128]{1,0:T(8,128)(2,1)S(1)} %shard_map.80), channel_id=1, source_target_pairs={{0,16},{32,48},{16,0},{48,32},{1,17},{33,49},{17,1},{49,33},{2,18}... | collective-permute-start | bytes 344072 | tf_op jit(solution)/shard_map/ppermute | solution.py:61
  101.0 12.8 %collective-permute-start.16 = (s16[656,128]{1,0:T(8,128)(2,1)S(1)}, s16[656,128]{1,0:T(8,128)(2,1)S(1)}, u32[]{:S(2)}, u32[]{:S(2)}) collective-permute-start(s16[656,128]{1,0:T(8,128)(2,1)S(1)} %get-tuple-element.89), channel_id=1, source_target_pairs={{0,1},{2,3},{4,5},{6,7},{8,9},{10,11},{12,13},{14,15},{1,0},{3,2},... | collective-permute-start | bytes 503816 | tf_op jit(solution)/shard_map/ppermute | solution.py:61
  103.1 10.7 %collective-permute-start.17 = (s16[656,128]{1,0:T(8,128)(2,1)S(1)}, s16[656,128]{1,0:T(8,128)(2,1)S(1)}, u32[]{:S(2)}, u32[]{:S(2)}) collective-permute-start(s16[656,128]{1,0:T(8,128)(2,1)S(1)} %get-tuple-element.90), channel_id=1, source_target_pairs={{1,2},{3,4},{5,6},{7,8},{9,10},{11,12},{13,14},{15,0},{2,1},{4,3},... | collective-permute-start | bytes 503816 | tf_op jit(solution)/shard_map/ppermute | solution.py:61
  107.9 1.5 %copy-start.3 = (bf16[432,16,128]{2,1,0:T(8,128)(2,1)S(1)}, bf16[432,16,128]{2,1,0:T(8,128)(2,1)}, u32[]{:S(2)}) copy-start(bf16[432,16,128]{2,1,0:T(8,128)(2,1)} %copy-done.2) | copy-start | bytes 5308420
  109.4 4.4 %copy-start.4 = (bf16[3,15,9,9,128]{4,1,3,2,0:T(8,128)(2,1)S(1)}, bf16[3,15,9,9,128]{4,1,3,2,0:T(8,128)(2,1)}, u32[]{:S(2)}) copy-start(bf16[3,15,9,9,128]{4,1,3,2,0:T(8,128)(2,1)} %param.7) | copy-start | bytes 2799364
  120.6 11.1 %all-to-all-start = ((f32[8,8,128]{2,1,0:T(8,128)}), f32[8,8,128]{2,1,0:T(8,128)S(1)}, u32[]{:S(2)}, u32[]{:S(2)}) async-start(f32[8,8,128]{2,1,0:T(8,128)} %get-tuple-element.93), calls=%async_computation | async-start | bytes 65536 | tf_op jit(solution)/shard_map/all_to_all | solution.py:457
  (3 other events, 3.2 us)

commit v5 on v4

--- a/solution.py
+++ b/solution.py
@@ -37,14 +37,14 @@
 HBM = pl.BlockSpec(memory_space=pltpu.HBM)
 
 
-def call(kernel, outs, args, scratch=(), flops=0, mib=16, in_hbm=()):
+def call(kernel, outs, args, scratch=(), flops=0, mib=12, in_hbm=(), out_hbm=()):
     shapes = [jax.ShapeDtypeStruct(shape, dtype) for shape, dtype in outs]
     moved = sum(a.size * a.dtype.itemsize for a in args) + sum(s.size * s.dtype.itemsize for s in shapes)
     return pl.pallas_call(
         kernel,
         out_shape=shapes,
         in_specs=[HBM if k in in_hbm else VMEM for k in range(len(args))],
-        out_specs=[VMEM] * len(shapes),
+        out_specs=[HBM if k in out_hbm else VMEM for k in range(len(shapes))],
         scratch_shapes=list(scratch),
         compiler_params=pltpu.CompilerParams(vmem_limit_bytes=mib << 20),
         cost_estimate=pl.CostEstimate(flops=flops, bytes_accessed=moved, transcendentals=0),
@@ -123,49 +123,47 @@
     return functools.reduce(jnp.maximum, levels)
 
 
-def pick_y(upper, own, u1, u2, held, picked):
+def pick_y(upper, own, u1, u2, picked):
     picked[ROWS_Y - 16 :] = jnp.zeros((16, VECS), F32)
     for b in range(ORB):
-        if own.dtype == F32:
-            take = [own[b, 16 * q : 16 * q + 16] for q in range(2 * CX)]
-        else:
-            held[...] = own[b].astype(F32)
-            take = [held[16 * q : 16 * q + 16] for q in range(2 * CX)]
+        take = [own[b, 16 * q : 16 * q + 16] for q in range(2 * CX)]
         take += [u[b * NX + 16 * q : b * NX + 16 * q + 16] for u in (u1, u2) for q in range(2)]
         for q, rows in enumerate(take):
             picked[b * NY + 4 * q : b * NY + 4 * q + 4] = jnp.where(upper, rows[12:16], rows[0:4])
 
 
-def second_y_kernel(x2, x1, level, own, out, u1, u2, tall, held, picked):
+def second_y_kernel(x2, x1, level, own, out, u1, u2, tall, picked):
     unpack(x1, u1)
     unpack(x2, u2)
     tall[...] = level[...]
     if out.dtype == jnp.int16:
         tall[...] = highest([level[...], level_of(x1), level_of(x2)])
-    pick_y(odd("gy") == 1, own, u1, u2, held, picked)
+    pick_y(odd("gy") == 1, own, u1, u2, picked)
     pack(picked, out, tall[...])
 
 
-def first_y_kernel(tall, own, u1, u2, out, held, picked):
-    pick_y(odd("gy") == 0, own, u1, u2, held, picked)
+def first_y_kernel(tall, own, u1, u2, out, picked):
+    pick_y(odd("gy") == 0, own, u1, u2, picked)
     pack(picked, out, tall[...])
 
 
-def faces_z_kernel(y2, y1, level, own, u1, u2, out1, out2, v1, v2, held, p1, p2):
+def unpack_kernel(message, level, plain, tall):
+    unpack(message, plain)
+    tall[...] = highest([level[...], level_of(message)]) if message.dtype == jnp.int16 else level[...]
+
+
+def faces_z_kernel(y1, level, own, u1, u2, v2, out1, out2, v1, p1, p2):
     fixed = out1.dtype == jnp.int16
     unpack(y1, v1)
-    unpack(y2, v2)
     even = odd("gz") == 0
     p1[ROWS_Z - 8 :] = jnp.zeros((8, VECS), F32)
     p2[ROWS_Z - 8 :] = jnp.zeros((8, VECS), F32)
     ghosts = ((u1, NX), (u2, NX), (v1, NY), (v2, NY))
     for b in range(ORB):
         faces = []
-        if not fixed:
-            held[...] = own[b].astype(F32)
         for z in (0, CZ - 1):
             at = pl.ds(z, ATOMS // CZ, stride=CZ)
-            faces.append([own[b, at, :] if fixed else held[at, :]])
+            faces.append([own[b, at, :]])
             faces[-1] += [ref[pl.ds(b * rows + z, rows // CZ, stride=CZ), :] for ref, rows in ghosts]
         at = b * NZ
         for low, high in zip(*faces):
@@ -173,7 +171,7 @@
             p1[at : at + rows] = jnp.where(even, high, low)
             p2[at : at + rows] = jnp.where(even, low, high)
             at += rows
-    level = highest([level[...], level_of(y1), level_of(y2)]) if fixed else level[...]
+    level = highest([level[...], level_of(y1)]) if fixed else level[...]
     pack(p1, out1, level)
     pack(p2, out2, level)
 
@@ -214,23 +212,27 @@
     loop(slots, split, 16)
 
 
-def front_tiles(own, plains, loose, tiles):
-    pieces = [(lambda b: own[b].astype(F32), ATOMS)]
+def front_pieces(own, plains):
+    pieces = [(lambda b: own[b], ATOMS)]
     for plain, count in zip(plains, (NX, NX, NY, NY)):
         pieces.append((lambda b, plain=plain, count=count: plain[b * count : b * count + count], count))
-    make_tiles(pieces, loose, tiles, 0)
-
-
-def back_tiles(front, messages, plains, loose, tiles):
-    def copy(j):
-        tiles[j] = front[j]
-
-    loop(BEFORE_Z, copy, 16)
+    return pieces
+
+
+def back_pieces(messages, plains):
     pieces = []
     for message, plain in zip(messages, plains):
         unpack(message, plain)
         pieces.append((lambda b, plain=plain: plain[b * NZ : b * NZ + NZ], NZ))
-    make_tiles(pieces, loose, tiles, BEFORE_Z)
+    return pieces
+
+
+def back_tiles(front, messages, plains, loose, tiles):
+    def copy(j):
+        tiles[j] = front[j]
+
+    loop(BEFORE_Z, copy, 16)
+    make_tiles(back_pieces(messages, plains), loose, tiles, BEFORE_Z)
 
 
 def middle(k):
@@ -282,6 +284,10 @@
     loop(ATOMS // 2, atom, ATOMS // 2)
 
 
+def tiles_kernel(level, own, z1, z2, u1, u2, v1, v2, tiles, loose, *plains):
+    make_tiles(front_pieces(own, (u1, u2, v1, v2)) + back_pieces((z1, z2), plains), loose, tiles, 0)
+
+
 def spread_middle(half, applied):
     def put(k):
         applied[aligned(middle(k) * 16), :] = half[aligned(k * 16), :]
@@ -291,22 +297,22 @@
 
 def front_kernel(slots, rows, own, u1, u2, v1, v2, front, half, table, arrived, loose):
     copy = fetch(slots, table, arrived)
-    front_tiles(own, (u1, u2, v1, v2), loose, front)
+    make_tiles(front_pieces(own, (u1, u2, v1, v2)), loose, front, 0)
     copy.wait()
     apply_atoms(table, rows, front, half, middle, lambda k: k)
 
 
-def front_third_kernel(coef, slots, rows, prev, sum_in, noise_tiles, own, u1, u2, v1, v2, front, half, dense,
+def front_third_kernel(coef, slots, rows, sum_in, noise_tiles, own, u1, u2, v1, v2, front, half, dense,
                        table, arrived, loose, applied):
     copy = fetch(slots, table, arrived)
-    front_tiles(own, (u1, u2, v1, v2), loose, front)
+    make_tiles(front_pieces(own, (u1, u2, v1, v2)), loose, front, 0)
     copy.wait()
     apply_atoms(table, rows, front, half, middle, lambda k: k)
     applied[...] = jnp.zeros_like(applied)
     spread_middle(half, applied)
     for a in range(ORB):
         at = pl.ds(a, ATOMS, stride=16)
-        applied[at, :] = sum_in[a] + coef[3 : 4, :] * (2.0 * applied[at, :] - prev[a])
+        applied[at, :] = sum_in[a] + (2.0 * coef[3 : 4, :]) * applied[at, :]
     densities(table, noise_tiles, applied, dense, middle, lambda k: k)
 
 
@@ -339,36 +345,38 @@
     spread_middle(half, applied)
 
 
-def first_kernel(coef, slots, rows, own, front, half, z1, z2, now, total, out1, out2, level, tiles,
-                 table, arrived, loose, applied, p1, p2, *plains):
+def first_kernel(coef, slots, rows, own, front, half, z1, z2, now, total, out1, out2, level,
+                 table, arrived, tiles, loose, applied, p1, p2, *plains):
     rest(slots, table, arrived, rows, front, half, (z1, z2), plains, loose, tiles, applied)
     for a in range(ORB):
         value = applied[pl.ds(a, ATOMS, stride=16), :]
         now[a] = value
-        total[a] = coef[0 : 1, :] * own[a].astype(F32) + coef[1 : 2, :] * value
+        total[a] = coef[0 : 1, :] * own[a] + coef[1 : 2, :] * value
     put_faces(now, out1, out2, level, p1, p2)
 
 
-def second_kernel(coef, slots, rows, prev, sum_in, front, half, z1, z2, now, total, out1, out2, level,
+def second_kernel(coef, slots, rows, prev, sum_in, first, front, half, z1, z2, now, total, out1, out2, level,
                   table, arrived, tiles, loose, applied, p1, p2, *plains):
     rest(slots, table, arrived, rows, front, half, (z1, z2), plains, loose, tiles, applied)
     for a in range(ORB):
-        value = 2.0 * applied[pl.ds(a, ATOMS, stride=16), :] - prev[a].astype(F32)
+        value = 2.0 * applied[pl.ds(a, ATOMS, stride=16), :] - prev[a]
         now[a] = value
-        total[a] = sum_in[a] + coef[2 : 3, :] * value
+        total[a] = sum_in[a] + coef[2 : 3, :] * value - coef[3 : 4, :] * first[a]
     put_faces(now, out1, out2, level, p1, p2)
 
 
-def third_kernel(coef, slots, lanes, rows, prev, sum_in, noise_tiles, deriv, front, half, dense_half, z1, z2,
-                 total, forces, sent, table, arrived, tiles, loose, applied, dense, turned, stacked, slopes, loaded, *plains):
+def third_kernel(coef, slots, lanes, rows, sum_in, noise_tiles, deriv, front, half, dense_half, z1, z2,
+                 total, forces, sent, table, arrived, tiles, loose, applied, dense, turned, stacked, slopes, loaded, written, left, *plains):
     load = pltpu.make_async_copy(deriv, slopes, loaded)
     load.start()
     rest(slots, table, arrived, rows, front, half, (z1, z2), plains, loose, tiles, applied)
     for a in range(ORB):
         at = pl.ds(a, ATOMS, stride=16)
-        value = sum_in[a] + coef[3 : 4, :] * (2.0 * applied[at, :] - prev[a])
-        total[a] = value
+        value = sum_in[a] + (2.0 * coef[3 : 4, :]) * applied[at, :]
+        written[a] = value
         applied[at, :] = value
+    leave = pltpu.make_async_copy(written, total, left)
+    leave.start()
     densities(table, noise_tiles, applied, dense, outer, outer)
     for side in range(2):
         spread_middle(dense_half.at[side], dense.at[side])
@@ -403,6 +411,7 @@
     for c in range(3):
         forces[c : c + 1, 0:ATOMS] = forces[c : c + 1, 0:ATOMS] - own_rows[c]
     send(sent, summed, FIRST_AT, FIRST_SIZE, place_of())
+    leave.wait()
 
 
 def place_of():
@@ -433,14 +442,14 @@
     return summed[0:8] + summed[8:16] + summed[16:24]
 
 
-def merge_kernel(held, lanes, got, out, sent):
-    value = held[...] + spread(got, lanes, place_of(), FIRST)
+def merge_kernel(held, got, out, sent):
+    value = held[...] + spread(got, landing_lanes(0), place_of(), FIRST)
     out[...] = value[:, 0:ATOMS]
     send(sent, value, SECOND_AT, SECOND_SIZE, 7 - place_of())
 
 
-def finish_kernel(held, lanes, got, out):
-    value = held[...] + spread(got, lanes, 7 - place_of(), ATOMS)
+def finish_kernel(held, got, out):
+    value = held[...] + spread(got, landing_lanes(1), 7 - place_of(), ATOMS)
     out[...] = value[0:3]
 
 
@@ -468,28 +477,24 @@
 
 
 def second_lane(basis, cells, kinds):
-    inner = number(basis, [jnp.where(k, 0, c) for c, k in zip(cells, kinds)], [jnp.where(k, 1, 4) for k in kinds])
+    inner = number(basis, [jnp.where(k == 1, 0, c) for c, k in zip(cells, kinds)], [jnp.where(k == 1, 1, 4) for k in kinds])
     kind = 4 * kinds[0] + 2 * kinds[1] + kinds[2]
     return jnp.where(kind > 0, start_of(kind, SECOND_AT) + inner, number(basis, cells, (CX, CY, CZ)))
 
 
-def landing_lanes(parity):
-    tables = []
-    for second in (0, 1):
-        base = 4 if second else 5
-        kind = lax.broadcasted_iota(jnp.int32, (8, VECS), 0)
-        rest = lax.broadcasted_iota(jnp.int32, (8, VECS), 1)
-        cells = [None] * 3
-        for d in (2, 1, 0):
-            traded = (kind >> (2 - d)) % 2 == 1
-            radix = jnp.where(traded, 1, base)
-            near = jnp.where((parity[d] == 0) != (second == 1), CX - 1, 0)
-            cells[d] = jnp.where(traded, near, rest % radix)
-            rest = rest // radix
-        ghost = [(c == CX).astype(jnp.int32) for c in cells]
-        lane = second_lane(rest, cells, ghost)
-        tables.append(jnp.where((rest < 2) & (kind > 0), lane, -1).astype(jnp.int32))
-    return tables
+def landing_lanes(second):
+    kind = lax.broadcasted_iota(jnp.int32, (8, VECS), 0)
+    rest = lax.broadcasted_iota(jnp.int32, (8, VECS), 1)
+    cells = [None] * 3
+    for d in (2, 1, 0):
+        traded = ((kind >> (2 - d)) & 1) == 1
+        near = jnp.where(odd(AXES[d]) == second, CX - 1, 0)
+        less = rest >> 2 if second else (rest * 205) >> 10
+        cells[d] = jnp.where(traded, near, rest - (4 if second else 5) * less)
+        rest = jnp.where(traded, rest, less)
+    ghost = [jnp.where(c == CX, 1, 0) for c in cells]
+    lane = second_lane(rest, cells, ghost)
+    return jnp.where((rest < 2) & (kind > 0), lane, -1)
 
 
 def slots_of(neighbours, parity):
@@ -530,6 +535,13 @@
     return slots.astype(jnp.int32), lanes.astype(jnp.int32)
 
 
+def passing(kernel, count, held):
+    def with_held(*refs):
+        kernel(*refs[:count], *refs[count + len(held) :])
+
+    return with_held
+
+
 def plain(rows):
     return pltpu.VMEM((rows, VECS), F32)
 
@@ -537,26 +549,27 @@
 BACK_PLAINS = [plain(ROWS_Z), plain(ROWS_Z)]
 
 
-def exchange(level, own, out1, out2, work):
+def exchange(level, own, out1, out2, work, held=()):
     dtype = out1.dtype
     rows_x, rows_y = ((ROWS_X, VECS), F32), ((ROWS_Y, VECS), F32)
     x2, x1 = swapped(out2, "gx", 1), swapped(out1, "gx", 0)
     out2, u1, u2, level = call(
-        second_y_kernel, [((ROWS_Y, VECS), dtype), rows_x, rows_x, ((8, VECS), F32)],
-        (x2, x1, level, own), [plain(ATOMS), plain(ROWS_Y)],
+        passing(second_y_kernel, 4, held), [((ROWS_Y, VECS), dtype), rows_x, rows_x, ((8, VECS), F32)],
+        (x2, x1, level, own) + held, [plain(ROWS_Y)],
     )
     y2 = swapped(out2, "gy", 1)
     (out1,) = call(
         first_y_kernel, [((ROWS_Y, VECS), dtype)], (level, own, u1, u2),
-        [plain(ATOMS), plain(ROWS_Y)],
+        [plain(ROWS_Y)],
     )
     y1 = swapped(out1, "gy", 0)
-    out1, out2, v1, v2 = call(
-        faces_z_kernel, [((ROWS_Z, VECS), dtype)] * 2 + [rows_y] * 2,
-        (y2, y1, level, own, u1, u2), [plain(ATOMS)] + BACK_PLAINS,
+    v2, level = call(unpack_kernel, [rows_y, ((8, VECS), F32)], (y2, level), flops=1 << 31)
+    out1, out2, v1 = call(
+        faces_z_kernel, [((ROWS_Z, VECS), dtype)] * 2 + [rows_y],
+        (y1, level, own, u1, u2, v2), BACK_PLAINS,
     )
     z1, z2 = swapped(out1, "gz", 0), swapped(out2, "gz", 1)
-    return work(own, u1, u2, v1, v2), (z1, z2)
+    return work(own, u1, u2, v1, v2), (z1, z2), (u1, u2, v1, v2)
 
 
 def shards(noise_vectors, hamiltonian, derivative, neighbours, coefficients):
@@ -574,6 +587,7 @@
         prep_kernel, [((ATOMS, 16, 256), BF16)], (hamiltonian.transpose(1, 2, 0, 3),),
         [plain(256), pltpu.VMEM((2, ATOMS * 16, 128), F32)], flops=1 << 22,
     )
+    noise = noise_vectors.astype(F32)
     whole = ((ORB, ATOMS, VECS), F32)
     plane = ((ROWS_X, VECS), jnp.int16)
     tile = ((8, 128), F32)
@@ -582,46 +596,48 @@
     faces = [plain(ROWS_X), plain(ROWS_X)]
     table = [pltpu.SMEM((NEIGH, ATOMS), jnp.int32), pltpu.SemaphoreType.DMA]
 
-    def work(*vectors):
-        width = 128 if vectors[0].dtype == BF16 else 256
+    def work(*vectors, width=256):
         return call(
             front_kernel, [((BEFORE_Z, 16, width), BF16), half], (slots, rows) + vectors,
             table + [front_loose], flops=1 << 29,
         )
 
-    fronts, ghosts = exchange(jnp.zeros((8, VECS), F32), noise_vectors, out1, out2, work)
-    first, total, out1, out2, level, noise_tiles = call(
-        first_kernel, [whole, whole, plane, plane, tile, ((SLOTS, 16, VECS), BF16)],
-        (coefs, slots, rows, noise_vectors, *fronts, *ghosts),
-        table + [loose, applied] + faces + BACK_PLAINS, flops=1 << 29,
-    )
-    fronts, ghosts = exchange(level, first, out1, out2, work)
+    fronts, ghosts, plains = exchange(jnp.zeros((8, VECS), F32), noise, out1, out2, functools.partial(work, width=128))
+    first, total, out1, out2, level = call(
+        first_kernel, [whole, whole, plane, plane, tile],
+        (coefs, slots, rows, noise, *fronts, *ghosts),
+        table + [pltpu.VMEM((SLOTS, 16, VECS), BF16), loose, applied] + faces + BACK_PLAINS, flops=1 << 29,
+    )
+    (noise_tiles,) = call(
+        tiles_kernel, [((SLOTS, 16, VECS), BF16)], (level, noise, *ghosts, *plains), [plain(SLOTS * 16)] + BACK_PLAINS
+    )
+    fronts, ghosts, _ = exchange(level, first, out1, out2, work, (noise_tiles,))
     second, total, out1, out2, level = call(
         second_kernel, [whole, whole, plane, plane, tile],
-        (coefs, slots, rows, noise_vectors, total, *fronts, *ghosts),
+        (coefs, slots, rows, noise, total, first, *fronts, *ghosts),
         table + [pltpu.VMEM((SLOTS, 16, 256), BF16), loose, applied] + faces + BACK_PLAINS, flops=1 << 29,
     )
 
     def last_work(*vectors):
         return call(
             front_third_kernel, [((BEFORE_Z, 16, 256), BF16), half, ((2,) + half[0], F32)],
-            (coefs, slots, rows, first, total, noise_tiles) + vectors,
+            (coefs, slots, rows, total, noise_tiles) + vectors,
             table + [front_loose, applied], flops=1 << 30,
         )
 
-    fronts, ghosts = exchange(level, second, out1, out2, last_work)
+    fronts, ghosts, _ = exchange(level, second, out1, out2, last_work)
     eight = ((8, 8, 128), F32)
     slopes = derivative.transpose(0, 2, 3, 1, 4)
-    lanes1, lanes2 = landing_lanes(parity)
     weighted, held, sent = call(
         third_kernel, [whole, ((8, FIRST), F32), eight],
-        (coefs, slots, lanes, rows, first, total, noise_tiles, slopes, *fronts, *ghosts),
+        (coefs, slots, lanes, rows, total, noise_tiles, slopes, *fronts, *ghosts),
         table + [pltpu.VMEM((SLOTS, 16, 256), BF16), loose, applied, pltpu.VMEM((2, ATOMS * 16, 128), F32), plain(256),
-         plain(NEIGH * 16), pltpu.VMEM(slopes.shape, BF16), pltpu.SemaphoreType.DMA] + BACK_PLAINS,
-        flops=1 << 30, in_hbm=(7,),
-    )
-    held, sent = call(merge_kernel, [tile, eight], (held, lanes1, trade_all(sent, 0)))
-    (forces,) = call(finish_kernel, [((3, ATOMS), F32)], (held, lanes2, trade_all(sent, 1)))
+         plain(NEIGH * 16), pltpu.VMEM(slopes.shape, BF16), pltpu.SemaphoreType.DMA,
+         pltpu.VMEM((ORB, ATOMS, VECS), F32), pltpu.SemaphoreType.DMA] + BACK_PLAINS,
+        flops=1 << 30, in_hbm=(6,), out_hbm=(0,),
+    )
+    held, sent = call(merge_kernel, [tile, eight], (held, trade_all(sent, 0)))
+    (forces,) = call(finish_kernel, [((3, ATOMS), F32)], (held, trade_all(sent, 1)))
     return weighted, forces
 
 

time: 144 us -> 138 us (0.958)
  waiting for transfers between devices: 24.2 us -> 13.4 us
  blocking collectives: 10.6 us -> 20.7 us
  local copies, waits for them, and re-layouts: 4.75 us -> 1.07 us
  starting transfers between devices: 76.3 us -> 73.7 us
    all_to_all x1 -> x2, blocking collectives: 10.6 us -> 20.7 us  [trade_all(): lax.all_to_all(sent, AXES, 0, 0, tiled=True, axis_index_groups=blocks(sec...]
    ppermute x18, waiting for transfers between devices: 18.9 us -> 13.4 us  [swapped(): return lax.ppermute(value, axis, pairs + [(b, a) for a, b in pairs])]
    all_to_all x1 -> x0, waiting for transfers between devices: 5.25 us -> none  [trade_all(): lax.all_to_all(sent, AXES, 0, 0, tiled=True, axis_index_groups=blocks(sec...]
    all_to_all x1 -> x0, starting transfers between devices: 5.25 us -> none  [trade_all(): lax.all_to_all(sent, AXES, 0, 0, tiled=True, axis_index_groups=blocks(sec...]
    unnamed x16 -> x8, local copies, waits for them, and re-layouts: 4.66 us -> 0.99 us
    ppermute x18, starting transfers between devices: 71 us -> 73.7 us  [swapped(): return lax.ppermute(value, axis, pairs + [(b, a) for a, b in pairs])]
    pallas_call x18 -> x22, Pallas kernels: 24.7 us -> 25 us  [call(): pl.pallas_call(kernel, out_shape=shapes, in_specs=[HBM if k in in_hbm els...]
  transfers between devices with their start and end apart: 19 -> 18, of which waited for: 12 -> 9; matrix products, arithmetic and copies ran while one was open for 1% -> 1% of each run, Pallas kernels for 7% -> 9%
where the time goes in v5:
time: 138 us; the launch traced here: 137 us
  starting transfers between devices  73.7 us (53%)
  Pallas kernels  25 us (18%)
  blocking collectives  20.7 us (15%)
  waiting for transfers between devices  13.4 us (10%)
  other arithmetic  2.12 us (2%)
    ppermute x18, starting transfers between devices, swapped(): return lax.ppermute(value, axis, pairs + [(b, a) for a, b in pairs])  73.7 us
    pallas_call x22, Pallas kernels, call(): pl.pallas_call(kernel, out_shape=shapes, in_specs=[HBM if k in in_hbm els...  25 us
    all_to_all x2, blocking collectives, trade_all(): lax.all_to_all(sent, AXES, 0, 0, tiled=True, axis_index_groups=blocks(sec...  20.7 us
    ppermute x18, waiting for transfers between devices, swapped(): return lax.ppermute(value, axis, pairs + [(b, a) for a, b in pairs])  13.4 us
  transfers between devices with their start and end apart: 18, of which 9 were waited for; matrix products, arithmetic and copies ran while one was open for 1% of the time, Pallas kernels for 9%

profile of v5, /device:TPU:1, one launch (start us, length us, event | category | flops | bytes accessed | tf_op | source)
XLA Modules:
  0.0 137.1 jit_solution(5845530513145857595)
XLA Ops:
  1.6 5.5 %collective-permute-start.1 = (bf16[304,128]{1,0:T(8,128)(2,1)S(1)}, bf16[304,128]{1,0:T(8,128)(2,1)S(1)}, u32[]{:S(2)}, u32[]{:S(2)}) collective-permute-start(bf16[304,128]{1,0:T(8,128)(2,1)S(1)} %concatenate.7), channel_id=1, source_target_pairs={{0,64},{128,192},{256,320},{384,448},{64,0},{192,128},{320,256},{4... | collective-permute-start | bytes 233480 | tf_op jit(solution)/shard_map/ppermute | solution.py:61
  7.1 4.6 %collective-permute-start = (bf16[304,128]{1,0:T(8,128)(2,1)S(1)}, bf16[304,128]{1,0:T(8,128)(2,1)S(1)}, u32[]{:S(2)}, u32[]{:S(2)}) collective-permute-start(bf16[304,128]{1,0:T(8,128)(2,1)S(1)} %concatenate.6), channel_id=1, source_target_pairs={{64,128},{192,256},{320,384},{448,0},{128,64},{256,192},{384,320},... | collective-permute-start | bytes 233480 | tf_op jit(solution)/shard_map/ppermute | solution.py:61
  16.0 4.2 %collective-permute-start.3 = (bf16[448,128]{1,0:T(8,128)(2,1)S(1)}, bf16[448,128]{1,0:T(8,128)(2,1)S(1)}, u32[]{:S(2)}, u32[]{:S(2)}) collective-permute-start(bf16[448,128]{1,0:T(8,128)(2,1)S(1)} %get-tuple-element.54), channel_id=1, source_target_pairs={{16,32},{48,0},{32,16},{0,48},{17,33},{49,1},{33,17},{1,49},{18,34... | collective-permute-start | bytes 344072 | tf_op jit(solution)/shard_map/ppermute | solution.py:61
  20.4 4.1 %collective-permute-start.2 = (bf16[448,128]{1,0:T(8,128)(2,1)S(1)}, bf16[448,128]{1,0:T(8,128)(2,1)S(1)}, u32[]{:S(2)}, u32[]{:S(2)}) collective-permute-start(bf16[448,128]{1,0:T(8,128)(2,1)S(1)} %shard_map.70), channel_id=1, source_target_pairs={{0,16},{32,48},{16,0},{48,32},{1,17},{33,49},{17,1},{49,33},{2,18}... | collective-permute-start | bytes 344072 | tf_op jit(solution)/shard_map/ppermute | solution.py:61
  25.5 1.9 %collective-permute-start.4 = (bf16[656,128]{1,0:T(8,128)(2,1)S(1)}, bf16[656,128]{1,0:T(8,128)(2,1)S(1)}, u32[]{:S(2)}, u32[]{:S(2)}) collective-permute-start(bf16[656,128]{1,0:T(8,128)(2,1)S(1)} %get-tuple-element.60), channel_id=1, source_target_pairs={{0,1},{2,3},{4,5},{6,7},{8,9},{10,11},{12,13},{14,15},{1,0},{3,2},... | collective-permute-start | bytes 503816 | tf_op jit(solution)/shard_map/ppermute | solution.py:61
  27.4 10.0 %collective-permute-start.5 = (bf16[656,128]{1,0:T(8,128)(2,1)S(1)}, bf16[656,128]{1,0:T(8,128)(2,1)S(1)}, u32[]{:S(2)}, u32[]{:S(2)}) collective-permute-start(bf16[656,128]{1,0:T(8,128)(2,1)S(1)} %get-tuple-element.61), channel_id=1, source_target_pairs={{1,2},{3,4},{5,6},{7,8},{9,10},{11,12},{13,14},{15,0},{2,1},{4,3},... | collective-permute-start | bytes 503816 | tf_op jit(solution)/shard_map/ppermute | solution.py:61
  40.8 2.2 %shard_map.74 = (f32[9,128,128]{2,1,0:T(8,128)S(1)}, f32[9,128,128]{2,1,0:T(8,128)S(1)}, s16[304,128]{1,0:T(8,128)(2,1)S(1)}, s16[304,128]{1,0:T(8,128)(2,1)S(1)}, f32[8,128]{1,0:T(8,128)S(1)}) custom-call(f32[4,128]{1,0:T(4,128)S(1)} %broadcast_in_dim.90.coef, s32[15,128]{1,0:T(8,128)S(1)} %add_select_fusion.15.slots, ...), custom_call_target="tpu_custom_call" | custom-call | flops 536870912 | bytes 5027328 | tf_op jit(solution)/shard_map/pallas_call | solution.py:43
  43.0 7.1 %collective-permute-start.6 = (s16[304,128]{1,0:T(8,128)(2,1)S(1)}, s16[304,128]{1,0:T(8,128)(2,1)S(1)}, u32[]{:S(2)}, u32[]{:S(2)}) collective-permute-start(s16[304,128]{1,0:T(8,128)(2,1)S(1)} %get-tuple-element.64), channel_id=1, source_target_pairs={{64,128},{192,256},{320,384},{448,0},{128,64},{256,192},{384,320},... | collective-permute-start | bytes 233480 | tf_op jit(solution)/shard_map/ppermute | solution.py:61
  53.6 3.2 %collective-permute-done.7.refs_1_ = s16[304,128]{1,0:T(8,128)(2,1)S(1)} collective-permute-done((s16[304,128]{1,0:T(8,128)(2,1)S(1)}, s16[304,128]{1,0:T(8,128)(2,1)S(1)}, u32[]{:S(2)}, u32[]{:S(2)}) %collective-permute-start.7) | collective-permute-done | bytes 77856 | tf_op jit(solution)/shard_map/ppermute | solution.py:61
  56.9 3.4 %collective-permute-start.9 = (s16[448,128]{1,0:T(8,128)(2,1)S(1)}, s16[448,128]{1,0:T(8,128)(2,1)S(1)}, u32[]{:S(2)}, u32[]{:S(2)}) collective-permute-start(s16[448,128]{1,0:T(8,128)(2,1)S(1)} %get-tuple-element.70), channel_id=1, source_target_pairs={{16,32},{48,0},{32,16},{0,48},{17,33},{49,1},{33,17},{1,49},{18,34... | collective-permute-start | bytes 344072 | tf_op jit(solution)/shard_map/ppermute | solution.py:61
  60.3 2.9 %collective-permute-start.8 = (s16[448,128]{1,0:T(8,128)(2,1)S(1)}, s16[448,128]{1,0:T(8,128)(2,1)S(1)}, u32[]{:S(2)}, u32[]{:S(2)}) collective-permute-start(s16[448,128]{1,0:T(8,128)(2,1)S(1)} %shard_map.77), channel_id=1, source_target_pairs={{0,16},{32,48},{16,0},{48,32},{1,17},{33,49},{17,1},{49,33},{2,18}... | collective-permute-start | bytes 344072 | tf_op jit(solution)/shard_map/ppermute | solution.py:61
  66.2 4.6 %collective-permute-start.11 = (s16[656,128]{1,0:T(8,128)(2,1)S(1)}, s16[656,128]{1,0:T(8,128)(2,1)S(1)}, u32[]{:S(2)}, u32[]{:S(2)}) collective-permute-start(s16[656,128]{1,0:T(8,128)(2,1)S(1)} %get-tuple-element.77), channel_id=1, source_target_pairs={{1,2},{3,4},{5,6},{7,8},{9,10},{11,12},{13,14},{15,0},{2,1},{4,3},... | collective-permute-start | bytes 503816 | tf_op jit(solution)/shard_map/ppermute | solution.py:61
  70.8 2.6 %shard_map.80 = (bf16[288,16,256]{2,1,0:T(8,128)(2,1)S(1)}, f32[1024,128]{1,0:T(8,128)S(1)}) custom-call(s32[15,128]{1,0:T(8,128)S(1)} %add_select_fusion.15.slots, bf16[128,16,256]{2,1,0:T(8,128)(2,1)S(1)} %shard_map.68.rows, f32[9,128,128]{2,1,0:T(8,128)S(1)} %get-tuple-element.63.refs_3_.own.first, f32[304,128]{1,0:T(8,128)S(1)} %get-tuple-element.67.u1, ...), custom_call_target="tpu_custom_call" | custom-call | flops 536870912 | bytes 5299712 | tf_op jit(solution)/shard_map/pallas_call | solution.py:43
  73.9 3.0 %shard_map.81 = (f32[9,128,128]{2,1,0:T(8,128)S(1)}, f32[9,128,128]{2,1,0:T(8,128)S(1)}, s16[304,128]{1,0:T(8,128)(2,1)S(1)}, s16[304,128]{1,0:T(8,128)(2,1)S(1)}, f32[8,128]{1,0:T(8,128)S(1)}) custom-call(f32[4,128]{1,0:T(4,128)S(1)} %broadcast_in_dim.90.coef, s32[15,128]{1,0:T(8,128)S(1)} %add_select_fusion.15.slots, ...), custom_call_target="tpu_custom_call" | custom-call | flops 536870912 | bytes 7386624 | tf_op jit(solution)/shard_map/pallas_call | solution.py:43
  76.8 6.6 %collective-permute-start.12 = (s16[304,128]{1,0:T(8,128)(2,1)S(1)}, s16[304,128]{1,0:T(8,128)(2,1)S(1)}, u32[]{:S(2)}, u32[]{:S(2)}) collective-permute-start(s16[304,128]{1,0:T(8,128)(2,1)S(1)} %get-tuple-element.80), channel_id=1, source_target_pairs={{64,128},{192,256},{320,384},{448,0},{128,64},{256,192},{384,320},... | collective-permute-start | bytes 233480 | tf_op jit(solution)/shard_map/ppermute | solution.py:61
  85.6 4.5 %collective-permute-done.13.refs_1_ = s16[304,128]{1,0:T(8,128)(2,1)S(1)} collective-permute-done((s16[304,128]{1,0:T(8,128)(2,1)S(1)}, s16[304,128]{1,0:T(8,128)(2,1)S(1)}, u32[]{:S(2)}, u32[]{:S(2)}) %collective-permute-start.13) | collective-permute-done | bytes 77856 | tf_op jit(solution)/shard_map/ppermute | solution.py:61
  90.2 3.4 %collective-permute-start.15 = (s16[448,128]{1,0:T(8,128)(2,1)S(1)}, s16[448,128]{1,0:T(8,128)(2,1)S(1)}, u32[]{:S(2)}, u32[]{:S(2)}) collective-permute-start(s16[448,128]{1,0:T(8,128)(2,1)S(1)} %get-tuple-element.86), channel_id=1, source_target_pairs={{16,32},{48,0},{32,16},{0,48},{17,33},{49,1},{33,17},{1,49},{18,34... | collective-permute-start | bytes 344072 | tf_op jit(solution)/shard_map/ppermute | solution.py:61
  93.7 2.9 %collective-permute-start.14 = (s16[448,128]{1,0:T(8,128)(2,1)S(1)}, s16[448,128]{1,0:T(8,128)(2,1)S(1)}, u32[]{:S(2)}, u32[]{:S(2)}) collective-permute-start(s16[448,128]{1,0:T(8,128)(2,1)S(1)} %shard_map.83), channel_id=1, source_target_pairs={{0,16},{32,48},{16,0},{48,32},{1,17},{33,49},{17,1},{49,33},{2,18}... | collective-permute-start | bytes 344072 | tf_op jit(solution)/shard_map/ppermute | solution.py:61
  97.7 2.2 %collective-permute-start.16 = (s16[656,128]{1,0:T(8,128)(2,1)S(1)}, s16[656,128]{1,0:T(8,128)(2,1)S(1)}, u32[]{:S(2)}, u32[]{:S(2)}) collective-permute-start(s16[656,128]{1,0:T(8,128)(2,1)S(1)} %get-tuple-element.93), channel_id=1, source_target_pairs={{0,1},{2,3},{4,5},{6,7},{8,9},{10,11},{12,13},{14,15},{1,0},{3,2},... | collective-permute-start | bytes 503816 | tf_op jit(solution)/shard_map/ppermute | solution.py:61
  99.8 4.8 %collective-permute-start.17 = (s16[656,128]{1,0:T(8,128)(2,1)S(1)}, s16[656,128]{1,0:T(8,128)(2,1)S(1)}, u32[]{:S(2)}, u32[]{:S(2)}) collective-permute-start(s16[656,128]{1,0:T(8,128)(2,1)S(1)} %get-tuple-element.94), channel_id=1, source_target_pairs={{1,2},{3,4},{5,6},{7,8},{9,10},{11,12},{13,14},{15,0},{2,1},{4,3},... | collective-permute-start | bytes 503816 | tf_op jit(solution)/shard_map/ppermute | solution.py:61
  104.6 4.4 %shard_map.86 = (bf16[288,16,256]{2,1,0:T(8,128)(2,1)S(1)}, f32[1024,128]{1,0:T(8,128)S(1)}, f32[2,1024,128]{2,1,0:T(8,128)S(1)}) custom-call(f32[4,128]{1,0:T(4,128)S(1)} %broadcast_in_dim.90.coef, s32[15,128]{1,0:T(8,128)S(1)} %add_select_fusion.15.slots, bf16[128,16,256]{2,1,0:T(8,128)(2,1)S(1)} %shard_map.68.rows, ...), custom_call_target="tpu_custom_call" | custom-call | flops 1073741824 | bytes 8709632 | tf_op jit(solution)/shard_map/pallas_call | solution.py:43
  109.0 6.2 %shard_map.87 = (f32[9,128,128]{2,1,0:T(8,128)}, f32[8,256]{1,0:T(8,128)S(1)}, f32[8,8,128]{2,1,0:T(8,128)S(1)}) custom-call(f32[4,128]{1,0:T(4,128)S(1)} %broadcast_in_dim.90.coef, s32[15,128]{1,0:T(8,128)S(1)} %add_select_fusion.15.slots, s32[15,128]{1,0:T(8,128)S(1)} %get-tuple-element.100.lanes, bf16[128,16,256]{2,1,0:T(8,128)(2,1)S(1)} %shard_map.68.rows, ...), custom_call_target="tpu_custom_call" | custom-call | flops 1073741824 | bytes 9257216 | tf_op jit(solution)/shard_map/pallas_call | solution.py:43
  115.2 10.1 %all_to_all.10.got = f32[8,8,128]{2,1,0:T(8,128)S(1)} all-to-all(f32[8,8,128]{2,1,0:T(8,128)S(1)} %get-tuple-element.97), channel_id=1, replica_groups={{0,1,16,17,64,65,80,81},{2,3,18,19,66,67,82,83},{4,5,20,21,68,69,84,85}..., dimensions={0} | all-to-all | bytes 65536 | tf_op jit(solution)/shard_map/all_to_all | solution.py:466
  125.6 10.6 %all_to_all.11.got = f32[8,8,128]{2,1,0:T(8,128)S(1)} all-to-all(f32[8,8,128]{2,1,0:T(8,128)S(1)} %get-tuple-element.99), channel_id=1, replica_groups={{81,82,97,98,145,146,161,162},{83,84,99,100,147,148,163,164},{85,86,101..., dimensions={0} | all-to-all | bytes 65536 | tf_op jit(solution)/shard_map/all_to_all | solution.py:466
  (52 shorter events, 21.4 us)
Async XLA Ops:
  0.6 19.6 %copy-start.2 = (s32[128,15]{0,1:T(8,128)S(1)}, s32[128,15]{0,1:T(8,128)}, u32[]{:S(2)}) copy-start(s32[128,15]{0,1:T(8,128)} %param.8) | copy-start | bytes 23044
  1.6 13.1 %collective-permute-start.1 = (bf16[304,128]{1,0:T(8,128)(2,1)S(1)}, bf16[304,128]{1,0:T(8,128)(2,1)S(1)}, u32[]{:S(2)}, u32[]{:S(2)}) collective-permute-start(bf16[304,128]{1,0:T(8,128)(2,1)S(1)} %concatenate.7), channel_id=1, source_target_pairs={{0,64},{128,192},{256,320},{384,448},{64,0},{192,128},{320,256},{4... | collective-permute-start | bytes 233480 | tf_op jit(solution)/shard_map/ppermute | solution.py:61
  7.1 8.8 %collective-permute-start = (bf16[304,128]{1,0:T(8,128)(2,1)S(1)}, bf16[304,128]{1,0:T(8,128)(2,1)S(1)}, u32[]{:S(2)}, u32[]{:S(2)}) collective-permute-start(bf16[304,128]{1,0:T(8,128)(2,1)S(1)} %concatenate.6), channel_id=1, source_target_pairs={{64,128},{192,256},{320,384},{448,0},{128,64},{256,192},{384,320},... | collective-permute-start | bytes 233480 | tf_op jit(solution)/shard_map/ppermute | solution.py:61
  12.8 1.0 copy-start.1
  16.0 8.5 %collective-permute-start.3 = (bf16[448,128]{1,0:T(8,128)(2,1)S(1)}, bf16[448,128]{1,0:T(8,128)(2,1)S(1)}, u32[]{:S(2)}, u32[]{:S(2)}) collective-permute-start(bf16[448,128]{1,0:T(8,128)(2,1)S(1)} %get-tuple-element.54), channel_id=1, source_target_pairs={{16,32},{48,0},{32,16},{0,48},{17,33},{49,1},{33,17},{1,49},{18,34... | collective-permute-start | bytes 344072 | tf_op jit(solution)/shard_map/ppermute | solution.py:61
  20.4 5.0 %collective-permute-start.2 = (bf16[448,128]{1,0:T(8,128)(2,1)S(1)}, bf16[448,128]{1,0:T(8,128)(2,1)S(1)}, u32[]{:S(2)}, u32[]{:S(2)}) collective-permute-start(bf16[448,128]{1,0:T(8,128)(2,1)S(1)} %shard_map.70), channel_id=1, source_target_pairs={{0,16},{32,48},{16,0},{48,32},{1,17},{33,49},{17,1},{49,33},{2,18}... | collective-permute-start | bytes 344072 | tf_op jit(solution)/shard_map/ppermute | solution.py:61
  24.5 16.2 %copy-start.3 = (f32[4]{0:T(128)S(1)}, f32[4]{0:T(128)}, u32[]{:S(2)}) copy-start(f32[4]{0:T(128)} %param.9) | copy-start | bytes 52
  25.5 13.9 %collective-permute-start.4 = (bf16[656,128]{1,0:T(8,128)(2,1)S(1)}, bf16[656,128]{1,0:T(8,128)(2,1)S(1)}, u32[]{:S(2)}, u32[]{:S(2)}) collective-permute-start(bf16[656,128]{1,0:T(8,128)(2,1)S(1)} %get-tuple-element.60), channel_id=1, source_target_pairs={{0,1},{2,3},{4,5},{6,7},{8,9},{10,11},{12,13},{14,15},{1,0},{3,2},... | collective-permute-start | bytes 503816 | tf_op jit(solution)/shard_map/ppermute | solution.py:61
  27.4 13.3 %collective-permute-start.5 = (bf16[656,128]{1,0:T(8,128)(2,1)S(1)}, bf16[656,128]{1,0:T(8,128)(2,1)S(1)}, u32[]{:S(2)}, u32[]{:S(2)}) collective-permute-start(bf16[656,128]{1,0:T(8,128)(2,1)S(1)} %get-tuple-element.61), channel_id=1, source_target_pairs={{1,2},{3,4},{5,6},{7,8},{9,10},{11,12},{13,14},{15,0},{2,1},{4,3},... | collective-permute-start | bytes 503816 | tf_op jit(solution)/shard_map/ppermute | solution.py:61
  43.0 10.5 %collective-permute-start.6 = (s16[304,128]{1,0:T(8,128)(2,1)S(1)}, s16[304,128]{1,0:T(8,128)(2,1)S(1)}, u32[]{:S(2)}, u32[]{:S(2)}) collective-permute-start(s16[304,128]{1,0:T(8,128)(2,1)S(1)} %get-tuple-element.64), channel_id=1, source_target_pairs={{64,128},{192,256},{320,384},{448,0},{128,64},{256,192},{384,320},... | collective-permute-start | bytes 233480 | tf_op jit(solution)/shard_map/ppermute | solution.py:61
  50.1 6.6 %collective-permute-start.7 = (s16[304,128]{1,0:T(8,128)(2,1)S(1)}, s16[304,128]{1,0:T(8,128)(2,1)S(1)}, u32[]{:S(2)}, u32[]{:S(2)}) collective-permute-start(s16[304,128]{1,0:T(8,128)(2,1)S(1)} %get-tuple-element.65), channel_id=1, source_target_pairs={{0,64},{128,192},{256,320},{384,448},{64,0},{192,128},{320,256},{4... | collective-permute-start | bytes 233480 | tf_op jit(solution)/shard_map/ppermute | solution.py:61
  56.9 6.3 %collective-permute-start.9 = (s16[448,128]{1,0:T(8,128)(2,1)S(1)}, s16[448,128]{1,0:T(8,128)(2,1)S(1)}, u32[]{:S(2)}, u32[]{:S(2)}) collective-permute-start(s16[448,128]{1,0:T(8,128)(2,1)S(1)} %get-tuple-element.70), channel_id=1, source_target_pairs={{16,32},{48,0},{32,16},{0,48},{17,33},{49,1},{33,17},{1,49},{18,34... | collective-permute-start | bytes 344072 | tf_op jit(solution)/shard_map/ppermute | solution.py:61
  60.3 3.8 %collective-permute-start.8 = (s16[448,128]{1,0:T(8,128)(2,1)S(1)}, s16[448,128]{1,0:T(8,128)(2,1)S(1)}, u32[]{:S(2)}, u32[]{:S(2)}) collective-permute-start(s16[448,128]{1,0:T(8,128)(2,1)S(1)} %shard_map.77), channel_id=1, source_target_pairs={{0,16},{32,48},{16,0},{48,32},{1,17},{33,49},{17,1},{49,33},{2,18}... | collective-permute-start | bytes 344072 | tf_op jit(solution)/shard_map/ppermute | solution.py:61
  64.3 9.1 %collective-permute-start.10 = (s16[656,128]{1,0:T(8,128)(2,1)S(1)}, s16[656,128]{1,0:T(8,128)(2,1)S(1)}, u32[]{:S(2)}, u32[]{:S(2)}) collective-permute-start(s16[656,128]{1,0:T(8,128)(2,1)S(1)} %get-tuple-element.76), channel_id=1, source_target_pairs={{0,1},{2,3},{4,5},{6,7},{8,9},{10,11},{12,13},{14,15},{1,0},{3,2},... | collective-permute-start | bytes 503816 | tf_op jit(solution)/shard_map/ppermute | solution.py:61
  66.2 7.6 %collective-permute-start.11 = (s16[656,128]{1,0:T(8,128)(2,1)S(1)}, s16[656,128]{1,0:T(8,128)(2,1)S(1)}, u32[]{:S(2)}, u32[]{:S(2)}) collective-permute-start(s16[656,128]{1,0:T(8,128)(2,1)S(1)} %get-tuple-element.77), channel_id=1, source_target_pairs={{1,2},{3,4},{5,6},{7,8},{9,10},{11,12},{13,14},{15,0},{2,1},{4,3},... | collective-permute-start | bytes 503816 | tf_op jit(solution)/shard_map/ppermute | solution.py:61
  76.8 8.8 %collective-permute-start.12 = (s16[304,128]{1,0:T(8,128)(2,1)S(1)}, s16[304,128]{1,0:T(8,128)(2,1)S(1)}, u32[]{:S(2)}, u32[]{:S(2)}) collective-permute-start(s16[304,128]{1,0:T(8,128)(2,1)S(1)} %get-tuple-element.80), channel_id=1, source_target_pairs={{64,128},{192,256},{320,384},{448,0},{128,64},{256,192},{384,320},... | collective-permute-start | bytes 233480 | tf_op jit(solution)/shard_map/ppermute | solution.py:61
  83.5 6.6 %collective-permute-start.13 = (s16[304,128]{1,0:T(8,128)(2,1)S(1)}, s16[304,128]{1,0:T(8,128)(2,1)S(1)}, u32[]{:S(2)}, u32[]{:S(2)}) collective-permute-start(s16[304,128]{1,0:T(8,128)(2,1)S(1)} %get-tuple-element.81), channel_id=1, source_target_pairs={{0,64},{128,192},{256,320},{384,448},{64,0},{192,128},{320,256},{4... | collective-permute-start | bytes 233480 | tf_op jit(solution)/shard_map/ppermute | solution.py:61
  90.2 6.3 %collective-permute-start.15 = (s16[448,128]{1,0:T(8,128)(2,1)S(1)}, s16[448,128]{1,0:T(8,128)(2,1)S(1)}, u32[]{:S(2)}, u32[]{:S(2)}) collective-permute-start(s16[448,128]{1,0:T(8,128)(2,1)S(1)} %get-tuple-element.86), channel_id=1, source_target_pairs={{16,32},{48,0},{32,16},{0,48},{17,33},{49,1},{33,17},{1,49},{18,34... | collective-permute-start | bytes 344072 | tf_op jit(solution)/shard_map/ppermute | solution.py:61
  93.7 3.8 %collective-permute-start.14 = (s16[448,128]{1,0:T(8,128)(2,1)S(1)}, s16[448,128]{1,0:T(8,128)(2,1)S(1)}, u32[]{:S(2)}, u32[]{:S(2)}) collective-permute-start(s16[448,128]{1,0:T(8,128)(2,1)S(1)} %shard_map.83), channel_id=1, source_target_pairs={{0,16},{32,48},{16,0},{48,32},{1,17},{33,49},{17,1},{49,33},{2,18}... | collective-permute-start | bytes 344072 | tf_op jit(solution)/shard_map/ppermute | solution.py:61
  97.7 11.3 %collective-permute-start.16 = (s16[656,128]{1,0:T(8,128)(2,1)S(1)}, s16[656,128]{1,0:T(8,128)(2,1)S(1)}, u32[]{:S(2)}, u32[]{:S(2)}) collective-permute-start(s16[656,128]{1,0:T(8,128)(2,1)S(1)} %get-tuple-element.93), channel_id=1, source_target_pairs={{0,1},{2,3},{4,5},{6,7},{8,9},{10,11},{12,13},{14,15},{1,0},{3,2},... | collective-permute-start | bytes 503816 | tf_op jit(solution)/shard_map/ppermute | solution.py:61
  99.8 9.2 %collective-permute-start.17 = (s16[656,128]{1,0:T(8,128)(2,1)S(1)}, s16[656,128]{1,0:T(8,128)(2,1)S(1)}, u32[]{:S(2)}, u32[]{:S(2)}) collective-permute-start(s16[656,128]{1,0:T(8,128)(2,1)S(1)} %get-tuple-element.94), channel_id=1, source_target_pairs={{1,2},{3,4},{5,6},{7,8},{9,10},{11,12},{13,14},{15,0},{2,1},{4,3},... | collective-permute-start | bytes 503816 | tf_op jit(solution)/shard_map/ppermute | solution.py:61
  104.6 4.4 %copy-start = (bf16[3,15,9,9,128]{4,1,3,2,0:T(8,128)(2,1)S(1)}, bf16[3,15,9,9,128]{4,1,3,2,0:T(8,128)(2,1)}, u32[]{:S(2)}) copy-start(bf16[3,15,9,9,128]{4,1,3,2,0:T(8,128)(2,1)} %param.7) | copy-start | bytes 2799364

commit v6 on v5

--- a/solution.py
+++ b/solution.py
@@ -195,7 +195,7 @@
     def clear(j):
         loose[aligned(j * 16 + 8, 8), :] = zero
 
-    loop(slots, clear, 16)
+    loop(slots, clear, 72)
     for b in range(ORB):
         at = 0
         for rows_of, count in pieces:
@@ -209,7 +209,7 @@
         if tiles.shape[2] == 256:
             tiles[base + j, :, 128:256] = (value - high.astype(F32)).astype(BF16)
 
-    loop(slots, split, 16)
+    loop(slots, split, 72)
 
 
 def front_pieces(own, plains):
@@ -231,7 +231,7 @@
     def copy(j):
         tiles[j] = front[j]
 
-    loop(BEFORE_Z, copy, 16)
+    loop(BEFORE_Z, copy, 72)
     make_tiles(back_pieces(messages, plains), loose, tiles, BEFORE_Z)
 
 
@@ -292,7 +292,7 @@
     def put(k):
         applied[aligned(middle(k) * 16), :] = half[aligned(k * 16), :]
 
-    loop(ATOMS // 2, put, 16)
+    loop(ATOMS // 2, put, ATOMS // 2)
 
 
 def front_kernel(slots, rows, own, u1, u2, v1, v2, front, half, table, arrived, loose):

time: 138 us -> 136 us (0.986)
  Pallas kernels: 25 us -> 22.5 us
    pallas_call x22, Pallas kernels: 25 us -> 22.5 us  [call(): pl.pallas_call(kernel, out_shape=shapes, in_specs=[HBM if k in in_hbm els...]
  transfers between devices with their start and end apart: 18 -> 18, of which waited for: 9 -> 9; matrix products, arithmetic and copies ran while one was open for 1% -> 1% of each run, Pallas kernels for 9% -> 8%
where the time goes in v6:
time: 136 us; the launch traced here: 135 us
  starting transfers between devices  73.7 us (54%)
  Pallas kernels  22.5 us (17%)
  blocking collectives  20.7 us (15%)
  waiting for transfers between devices  13.7 us (10%)
  other arithmetic  2.12 us (2%)
    ppermute x18, starting transfers between devices, swapped(): return lax.ppermute(value, axis, pairs + [(b, a) for a, b in pairs])  73.7 us
    pallas_call x22, Pallas kernels, call(): pl.pallas_call(kernel, out_shape=shapes, in_specs=[HBM if k in in_hbm els...  22.5 us
    all_to_all x2, blocking collectives, trade_all(): lax.all_to_all(sent, AXES, 0, 0, tiled=True, axis_index_groups=blocks(sec...  20.7 us
    ppermute x18, waiting for transfers between devices, swapped(): return lax.ppermute(value, axis, pairs + [(b, a) for a, b in pairs])  13.7 us
  transfers between devices with their start and end apart: 18, of which 9 were waited for; matrix products, arithmetic and copies ran while one was open for 1% of the time, Pallas kernels for 8%

profile of v6, /device:TPU:1, one launch (start us, length us, event | category | flops | bytes accessed | tf_op | source)
XLA Modules:
  0.0 134.8 jit_solution(2415201219374657702)
XLA Ops:
  1.6 5.5 %collective-permute-start.1 = (bf16[304,128]{1,0:T(8,128)(2,1)S(1)}, bf16[304,128]{1,0:T(8,128)(2,1)S(1)}, u32[]{:S(2)}, u32[]{:S(2)}) collective-permute-start(bf16[304,128]{1,0:T(8,128)(2,1)S(1)} %concatenate.7), channel_id=1, source_target_pairs={{0,64},{128,192},{256,320},{384,448},{64,0},{192,128},{320,256},{4... | collective-permute-start | bytes 233480 | tf_op jit(solution)/shard_map/ppermute | solution.py:61
  7.1 4.6 %collective-permute-start = (bf16[304,128]{1,0:T(8,128)(2,1)S(1)}, bf16[304,128]{1,0:T(8,128)(2,1)S(1)}, u32[]{:S(2)}, u32[]{:S(2)}) collective-permute-start(bf16[304,128]{1,0:T(8,128)(2,1)S(1)} %concatenate.6), channel_id=1, source_target_pairs={{64,128},{192,256},{320,384},{448,0},{128,64},{256,192},{384,320},... | collective-permute-start | bytes 233480 | tf_op jit(solution)/shard_map/ppermute | solution.py:61
  16.0 4.2 %collective-permute-start.3 = (bf16[448,128]{1,0:T(8,128)(2,1)S(1)}, bf16[448,128]{1,0:T(8,128)(2,1)S(1)}, u32[]{:S(2)}, u32[]{:S(2)}) collective-permute-start(bf16[448,128]{1,0:T(8,128)(2,1)S(1)} %get-tuple-element.54), channel_id=1, source_target_pairs={{16,32},{48,0},{32,16},{0,48},{17,33},{49,1},{33,17},{1,49},{18,34... | collective-permute-start | bytes 344072 | tf_op jit(solution)/shard_map/ppermute | solution.py:61
  20.4 4.1 %collective-permute-start.2 = (bf16[448,128]{1,0:T(8,128)(2,1)S(1)}, bf16[448,128]{1,0:T(8,128)(2,1)S(1)}, u32[]{:S(2)}, u32[]{:S(2)}) collective-permute-start(bf16[448,128]{1,0:T(8,128)(2,1)S(1)} %shard_map.70), channel_id=1, source_target_pairs={{0,16},{32,48},{16,0},{48,32},{1,17},{33,49},{17,1},{49,33},{2,18}... | collective-permute-start | bytes 344072 | tf_op jit(solution)/shard_map/ppermute | solution.py:61
  25.5 1.9 %collective-permute-start.4 = (bf16[656,128]{1,0:T(8,128)(2,1)S(1)}, bf16[656,128]{1,0:T(8,128)(2,1)S(1)}, u32[]{:S(2)}, u32[]{:S(2)}) collective-permute-start(bf16[656,128]{1,0:T(8,128)(2,1)S(1)} %get-tuple-element.60), channel_id=1, source_target_pairs={{0,1},{2,3},{4,5},{6,7},{8,9},{10,11},{12,13},{14,15},{1,0},{3,2},... | collective-permute-start | bytes 503816 | tf_op jit(solution)/shard_map/ppermute | solution.py:61
  27.4 10.0 %collective-permute-start.5 = (bf16[656,128]{1,0:T(8,128)(2,1)S(1)}, bf16[656,128]{1,0:T(8,128)(2,1)S(1)}, u32[]{:S(2)}, u32[]{:S(2)}) collective-permute-start(bf16[656,128]{1,0:T(8,128)(2,1)S(1)} %get-tuple-element.61), channel_id=1, source_target_pairs={{1,2},{3,4},{5,6},{7,8},{9,10},{11,12},{13,14},{15,0},{2,1},{4,3},... | collective-permute-start | bytes 503816 | tf_op jit(solution)/shard_map/ppermute | solution.py:61
  42.6 7.1 %collective-permute-start.6 = (s16[304,128]{1,0:T(8,128)(2,1)S(1)}, s16[304,128]{1,0:T(8,128)(2,1)S(1)}, u32[]{:S(2)}, u32[]{:S(2)}) collective-permute-start(s16[304,128]{1,0:T(8,128)(2,1)S(1)} %get-tuple-element.64), channel_id=1, source_target_pairs={{64,128},{192,256},{320,384},{448,0},{128,64},{256,192},{384,320},... | collective-permute-start | bytes 233480 | tf_op jit(solution)/shard_map/ppermute | solution.py:61
  53.0 3.3 %collective-permute-done.7.refs_1_ = s16[304,128]{1,0:T(8,128)(2,1)S(1)} collective-permute-done((s16[304,128]{1,0:T(8,128)(2,1)S(1)}, s16[304,128]{1,0:T(8,128)(2,1)S(1)}, u32[]{:S(2)}, u32[]{:S(2)}) %collective-permute-start.7) | collective-permute-done | bytes 77856 | tf_op jit(solution)/shard_map/ppermute | solution.py:61
  56.4 3.4 %collective-permute-start.9 = (s16[448,128]{1,0:T(8,128)(2,1)S(1)}, s16[448,128]{1,0:T(8,128)(2,1)S(1)}, u32[]{:S(2)}, u32[]{:S(2)}) collective-permute-start(s16[448,128]{1,0:T(8,128)(2,1)S(1)} %get-tuple-element.70), channel_id=1, source_target_pairs={{16,32},{48,0},{32,16},{0,48},{17,33},{49,1},{33,17},{1,49},{18,34... | collective-permute-start | bytes 344072 | tf_op jit(solution)/shard_map/ppermute | solution.py:61
  59.9 2.9 %collective-permute-start.8 = (s16[448,128]{1,0:T(8,128)(2,1)S(1)}, s16[448,128]{1,0:T(8,128)(2,1)S(1)}, u32[]{:S(2)}, u32[]{:S(2)}) collective-permute-start(s16[448,128]{1,0:T(8,128)(2,1)S(1)} %shard_map.77), channel_id=1, source_target_pairs={{0,16},{32,48},{16,0},{48,32},{1,17},{33,49},{17,1},{49,33},{2,18}... | collective-permute-start | bytes 344072 | tf_op jit(solution)/shard_map/ppermute | solution.py:61
  63.8 1.9 %collective-permute-start.10 = (s16[656,128]{1,0:T(8,128)(2,1)S(1)}, s16[656,128]{1,0:T(8,128)(2,1)S(1)}, u32[]{:S(2)}, u32[]{:S(2)}) collective-permute-start(s16[656,128]{1,0:T(8,128)(2,1)S(1)} %get-tuple-element.76), channel_id=1, source_target_pairs={{0,1},{2,3},{4,5},{6,7},{8,9},{10,11},{12,13},{14,15},{1,0},{3,2},... | collective-permute-start | bytes 503816 | tf_op jit(solution)/shard_map/ppermute | solution.py:61
  65.8 4.6 %collective-permute-start.11 = (s16[656,128]{1,0:T(8,128)(2,1)S(1)}, s16[656,128]{1,0:T(8,128)(2,1)S(1)}, u32[]{:S(2)}, u32[]{:S(2)}) collective-permute-start(s16[656,128]{1,0:T(8,128)(2,1)S(1)} %get-tuple-element.77), channel_id=1, source_target_pairs={{1,2},{3,4},{5,6},{7,8},{9,10},{11,12},{13,14},{15,0},{2,1},{4,3},... | collective-permute-start | bytes 503816 | tf_op jit(solution)/shard_map/ppermute | solution.py:61
  70.4 2.5 %shard_map.80 = (bf16[288,16,256]{2,1,0:T(8,128)(2,1)S(1)}, f32[1024,128]{1,0:T(8,128)S(1)}) custom-call(s32[15,128]{1,0:T(8,128)S(1)} %add_select_fusion.15.slots, bf16[128,16,256]{2,1,0:T(8,128)(2,1)S(1)} %shard_map.68.rows, f32[9,128,128]{2,1,0:T(8,128)S(1)} %get-tuple-element.63.refs_3_.own.first, f32[304,128]{1,0:T(8,128)S(1)} %get-tuple-element.67.u1, ...), custom_call_target="tpu_custom_call" | custom-call | flops 536870912 | bytes 5299712 | tf_op jit(solution)/shard_map/pallas_call | solution.py:43
  73.4 2.3 %shard_map.81 = (f32[9,128,128]{2,1,0:T(8,128)S(1)}, f32[9,128,128]{2,1,0:T(8,128)S(1)}, s16[304,128]{1,0:T(8,128)(2,1)S(1)}, s16[304,128]{1,0:T(8,128)(2,1)S(1)}, f32[8,128]{1,0:T(8,128)S(1)}) custom-call(f32[4,128]{1,0:T(4,128)S(1)} %broadcast_in_dim.90.coef, s32[15,128]{1,0:T(8,128)S(1)} %add_select_fusion.15.slots, ...), custom_call_target="tpu_custom_call" | custom-call | flops 536870912 | bytes 7386624 | tf_op jit(solution)/shard_map/pallas_call | solution.py:43
  75.7 6.6 %collective-permute-start.12 = (s16[304,128]{1,0:T(8,128)(2,1)S(1)}, s16[304,128]{1,0:T(8,128)(2,1)S(1)}, u32[]{:S(2)}, u32[]{:S(2)}) collective-permute-start(s16[304,128]{1,0:T(8,128)(2,1)S(1)} %get-tuple-element.80), channel_id=1, source_target_pairs={{64,128},{192,256},{320,384},{448,0},{128,64},{256,192},{384,320},... | collective-permute-start | bytes 233480 | tf_op jit(solution)/shard_map/ppermute | solution.py:61
  84.4 4.5 %collective-permute-done.13.refs_1_ = s16[304,128]{1,0:T(8,128)(2,1)S(1)} collective-permute-done((s16[304,128]{1,0:T(8,128)(2,1)S(1)}, s16[304,128]{1,0:T(8,128)(2,1)S(1)}, u32[]{:S(2)}, u32[]{:S(2)}) %collective-permute-start.13) | collective-permute-done | bytes 77856 | tf_op jit(solution)/shard_map/ppermute | solution.py:61
  89.1 3.3 %collective-permute-start.15 = (s16[448,128]{1,0:T(8,128)(2,1)S(1)}, s16[448,128]{1,0:T(8,128)(2,1)S(1)}, u32[]{:S(2)}, u32[]{:S(2)}) collective-permute-start(s16[448,128]{1,0:T(8,128)(2,1)S(1)} %get-tuple-element.86), channel_id=1, source_target_pairs={{16,32},{48,0},{32,16},{0,48},{17,33},{49,1},{33,17},{1,49},{18,34... | collective-permute-start | bytes 344072 | tf_op jit(solution)/shard_map/ppermute | solution.py:61
  92.5 2.9 %collective-permute-start.14 = (s16[448,128]{1,0:T(8,128)(2,1)S(1)}, s16[448,128]{1,0:T(8,128)(2,1)S(1)}, u32[]{:S(2)}, u32[]{:S(2)}) collective-permute-start(s16[448,128]{1,0:T(8,128)(2,1)S(1)} %shard_map.83), channel_id=1, source_target_pairs={{0,16},{32,48},{16,0},{48,32},{1,17},{33,49},{17,1},{49,33},{2,18}... | collective-permute-start | bytes 344072 | tf_op jit(solution)/shard_map/ppermute | solution.py:61
  96.5 2.1 %collective-permute-start.16 = (s16[656,128]{1,0:T(8,128)(2,1)S(1)}, s16[656,128]{1,0:T(8,128)(2,1)S(1)}, u32[]{:S(2)}, u32[]{:S(2)}) collective-permute-start(s16[656,128]{1,0:T(8,128)(2,1)S(1)} %get-tuple-element.93), channel_id=1, source_target_pairs={{0,1},{2,3},{4,5},{6,7},{8,9},{10,11},{12,13},{14,15},{1,0},{3,2},... | collective-permute-start | bytes 503816 | tf_op jit(solution)/shard_map/ppermute | solution.py:61
  98.7 4.8 %collective-permute-start.17 = (s16[656,128]{1,0:T(8,128)(2,1)S(1)}, s16[656,128]{1,0:T(8,128)(2,1)S(1)}, u32[]{:S(2)}, u32[]{:S(2)}) collective-permute-start(s16[656,128]{1,0:T(8,128)(2,1)S(1)} %get-tuple-element.94), channel_id=1, source_target_pairs={{1,2},{3,4},{5,6},{7,8},{9,10},{11,12},{13,14},{15,0},{2,1},{4,3},... | collective-permute-start | bytes 503816 | tf_op jit(solution)/shard_map/ppermute | solution.py:61
  103.5 4.0 %shard_map.86 = (bf16[288,16,256]{2,1,0:T(8,128)(2,1)S(1)}, f32[1024,128]{1,0:T(8,128)S(1)}, f32[2,1024,128]{2,1,0:T(8,128)S(1)}) custom-call(f32[4,128]{1,0:T(4,128)S(1)} %broadcast_in_dim.90.coef, s32[15,128]{1,0:T(8,128)S(1)} %add_select_fusion.15.slots, bf16[128,16,256]{2,1,0:T(8,128)(2,1)S(1)} %shard_map.68.rows, ...), custom_call_target="tpu_custom_call" | custom-call | flops 1073741824 | bytes 8709632 | tf_op jit(solution)/shard_map/pallas_call | solution.py:43
  107.5 5.5 %shard_map.87 = (f32[9,128,128]{2,1,0:T(8,128)}, f32[8,256]{1,0:T(8,128)S(1)}, f32[8,8,128]{2,1,0:T(8,128)S(1)}) custom-call(f32[4,128]{1,0:T(4,128)S(1)} %broadcast_in_dim.90.coef, s32[15,128]{1,0:T(8,128)S(1)} %add_select_fusion.15.slots, s32[15,128]{1,0:T(8,128)S(1)} %get-tuple-element.100.lanes, bf16[128,16,256]{2,1,0:T(8,128)(2,1)S(1)} %shard_map.68.rows, ...), custom_call_target="tpu_custom_call" | custom-call | flops 1073741824 | bytes 9257216 | tf_op jit(solution)/shard_map/pallas_call | solution.py:43
  113.0 10.1 %all_to_all.10.got = f32[8,8,128]{2,1,0:T(8,128)S(1)} all-to-all(f32[8,8,128]{2,1,0:T(8,128)S(1)} %get-tuple-element.97), channel_id=1, replica_groups={{0,1,16,17,64,65,80,81},{2,3,18,19,66,67,82,83},{4,5,20,21,68,69,84,85}..., dimensions={0} | all-to-all | bytes 65536 | tf_op jit(solution)/shard_map/all_to_all | solution.py:466
  123.4 10.6 %all_to_all.11.got = f32[8,8,128]{2,1,0:T(8,128)S(1)} all-to-all(f32[8,8,128]{2,1,0:T(8,128)S(1)} %get-tuple-element.99), channel_id=1, replica_groups={{81,82,97,98,145,146,161,162},{83,84,99,100,147,148,163,164},{85,86,101..., dimensions={0} | all-to-all | bytes 65536 | tf_op jit(solution)/shard_map/all_to_all | solution.py:466
  (52 shorter events, 21.2 us)
Async XLA Ops:
  0.6 19.6 %copy-start.2 = (s32[128,15]{0,1:T(8,128)S(1)}, s32[128,15]{0,1:T(8,128)}, u32[]{:S(2)}) copy-start(s32[128,15]{0,1:T(8,128)} %param.8) | copy-start | bytes 23044
  1.6 13.1 %collective-permute-start.1 = (bf16[304,128]{1,0:T(8,128)(2,1)S(1)}, bf16[304,128]{1,0:T(8,128)(2,1)S(1)}, u32[]{:S(2)}, u32[]{:S(2)}) collective-permute-start(bf16[304,128]{1,0:T(8,128)(2,1)S(1)} %concatenate.7), channel_id=1, source_target_pairs={{0,64},{128,192},{256,320},{384,448},{64,0},{192,128},{320,256},{4... | collective-permute-start | bytes 233480 | tf_op jit(solution)/shard_map/ppermute | solution.py:61
  7.1 8.8 %collective-permute-start = (bf16[304,128]{1,0:T(8,128)(2,1)S(1)}, bf16[304,128]{1,0:T(8,128)(2,1)S(1)}, u32[]{:S(2)}, u32[]{:S(2)}) collective-permute-start(bf16[304,128]{1,0:T(8,128)(2,1)S(1)} %concatenate.6), channel_id=1, source_target_pairs={{64,128},{192,256},{320,384},{448,0},{128,64},{256,192},{384,320},... | collective-permute-start | bytes 233480 | tf_op jit(solution)/shard_map/ppermute | solution.py:61
  12.8 1.0 copy-start.1
  16.0 8.5 %collective-permute-start.3 = (bf16[448,128]{1,0:T(8,128)(2,1)S(1)}, bf16[448,128]{1,0:T(8,128)(2,1)S(1)}, u32[]{:S(2)}, u32[]{:S(2)}) collective-permute-start(bf16[448,128]{1,0:T(8,128)(2,1)S(1)} %get-tuple-element.54), channel_id=1, source_target_pairs={{16,32},{48,0},{32,16},{0,48},{17,33},{49,1},{33,17},{1,49},{18,34... | collective-permute-start | bytes 344072 | tf_op jit(solution)/shard_map/ppermute | solution.py:61
  20.4 5.0 %collective-permute-start.2 = (bf16[448,128]{1,0:T(8,128)(2,1)S(1)}, bf16[448,128]{1,0:T(8,128)(2,1)S(1)}, u32[]{:S(2)}, u32[]{:S(2)}) collective-permute-start(bf16[448,128]{1,0:T(8,128)(2,1)S(1)} %shard_map.70), channel_id=1, source_target_pairs={{0,16},{32,48},{16,0},{48,32},{1,17},{33,49},{17,1},{49,33},{2,18}... | collective-permute-start | bytes 344072 | tf_op jit(solution)/shard_map/ppermute | solution.py:61
  24.5 16.2 %copy-start.3 = (f32[4]{0:T(128)S(1)}, f32[4]{0:T(128)}, u32[]{:S(2)}) copy-start(f32[4]{0:T(128)} %param.9) | copy-start | bytes 52
  25.5 13.9 %collective-permute-start.4 = (bf16[656,128]{1,0:T(8,128)(2,1)S(1)}, bf16[656,128]{1,0:T(8,128)(2,1)S(1)}, u32[]{:S(2)}, u32[]{:S(2)}) collective-permute-start(bf16[656,128]{1,0:T(8,128)(2,1)S(1)} %get-tuple-element.60), channel_id=1, source_target_pairs={{0,1},{2,3},{4,5},{6,7},{8,9},{10,11},{12,13},{14,15},{1,0},{3,2},... | collective-permute-start | bytes 503816 | tf_op jit(solution)/shard_map/ppermute | solution.py:61
  27.4 13.3 %collective-permute-start.5 = (bf16[656,128]{1,0:T(8,128)(2,1)S(1)}, bf16[656,128]{1,0:T(8,128)(2,1)S(1)}, u32[]{:S(2)}, u32[]{:S(2)}) collective-permute-start(bf16[656,128]{1,0:T(8,128)(2,1)S(1)} %get-tuple-element.61), channel_id=1, source_target_pairs={{1,2},{3,4},{5,6},{7,8},{9,10},{11,12},{13,14},{15,0},{2,1},{4,3},... | collective-permute-start | bytes 503816 | tf_op jit(solution)/shard_map/ppermute | solution.py:61
  42.6 10.4 %collective-permute-start.6 = (s16[304,128]{1,0:T(8,128)(2,1)S(1)}, s16[304,128]{1,0:T(8,128)(2,1)S(1)}, u32[]{:S(2)}, u32[]{:S(2)}) collective-permute-start(s16[304,128]{1,0:T(8,128)(2,1)S(1)} %get-tuple-element.64), channel_id=1, source_target_pairs={{64,128},{192,256},{320,384},{448,0},{128,64},{256,192},{384,320},... | collective-permute-start | bytes 233480 | tf_op jit(solution)/shard_map/ppermute | solution.py:61
  49.6 6.6 %collective-permute-start.7 = (s16[304,128]{1,0:T(8,128)(2,1)S(1)}, s16[304,128]{1,0:T(8,128)(2,1)S(1)}, u32[]{:S(2)}, u32[]{:S(2)}) collective-permute-start(s16[304,128]{1,0:T(8,128)(2,1)S(1)} %get-tuple-element.65), channel_id=1, source_target_pairs={{0,64},{128,192},{256,320},{384,448},{64,0},{192,128},{320,256},{4... | collective-permute-start | bytes 233480 | tf_op jit(solution)/shard_map/ppermute | solution.py:61
  56.4 6.3 %collective-permute-start.9 = (s16[448,128]{1,0:T(8,128)(2,1)S(1)}, s16[448,128]{1,0:T(8,128)(2,1)S(1)}, u32[]{:S(2)}, u32[]{:S(2)}) collective-permute-start(s16[448,128]{1,0:T(8,128)(2,1)S(1)} %get-tuple-element.70), channel_id=1, source_target_pairs={{16,32},{48,0},{32,16},{0,48},{17,33},{49,1},{33,17},{1,49},{18,34... | collective-permute-start | bytes 344072 | tf_op jit(solution)/shard_map/ppermute | solution.py:61
  59.9 3.8 %collective-permute-start.8 = (s16[448,128]{1,0:T(8,128)(2,1)S(1)}, s16[448,128]{1,0:T(8,128)(2,1)S(1)}, u32[]{:S(2)}, u32[]{:S(2)}) collective-permute-start(s16[448,128]{1,0:T(8,128)(2,1)S(1)} %shard_map.77), channel_id=1, source_target_pairs={{0,16},{32,48},{16,0},{48,32},{1,17},{33,49},{17,1},{49,33},{2,18}... | collective-permute-start | bytes 344072 | tf_op jit(solution)/shard_map/ppermute | solution.py:61
  63.8 9.0 %collective-permute-start.10 = (s16[656,128]{1,0:T(8,128)(2,1)S(1)}, s16[656,128]{1,0:T(8,128)(2,1)S(1)}, u32[]{:S(2)}, u32[]{:S(2)}) collective-permute-start(s16[656,128]{1,0:T(8,128)(2,1)S(1)} %get-tuple-element.76), channel_id=1, source_target_pairs={{0,1},{2,3},{4,5},{6,7},{8,9},{10,11},{12,13},{14,15},{1,0},{3,2},... | collective-permute-start | bytes 503816 | tf_op jit(solution)/shard_map/ppermute | solution.py:61
  65.8 7.6 %collective-permute-start.11 = (s16[656,128]{1,0:T(8,128)(2,1)S(1)}, s16[656,128]{1,0:T(8,128)(2,1)S(1)}, u32[]{:S(2)}, u32[]{:S(2)}) collective-permute-start(s16[656,128]{1,0:T(8,128)(2,1)S(1)} %get-tuple-element.77), channel_id=1, source_target_pairs={{1,2},{3,4},{5,6},{7,8},{9,10},{11,12},{13,14},{15,0},{2,1},{4,3},... | collective-permute-start | bytes 503816 | tf_op jit(solution)/shard_map/ppermute | solution.py:61
  75.7 8.8 %collective-permute-start.12 = (s16[304,128]{1,0:T(8,128)(2,1)S(1)}, s16[304,128]{1,0:T(8,128)(2,1)S(1)}, u32[]{:S(2)}, u32[]{:S(2)}) collective-permute-start(s16[304,128]{1,0:T(8,128)(2,1)S(1)} %get-tuple-element.80), channel_id=1, source_target_pairs={{64,128},{192,256},{320,384},{448,0},{128,64},{256,192},{384,320},... | collective-permute-start | bytes 233480 | tf_op jit(solution)/shard_map/ppermute | solution.py:61
  82.3 6.6 %collective-permute-start.13 = (s16[304,128]{1,0:T(8,128)(2,1)S(1)}, s16[304,128]{1,0:T(8,128)(2,1)S(1)}, u32[]{:S(2)}, u32[]{:S(2)}) collective-permute-start(s16[304,128]{1,0:T(8,128)(2,1)S(1)} %get-tuple-element.81), channel_id=1, source_target_pairs={{0,64},{128,192},{256,320},{384,448},{64,0},{192,128},{320,256},{4... | collective-permute-start | bytes 233480 | tf_op jit(solution)/shard_map/ppermute | solution.py:61
  89.1 6.3 %collective-permute-start.15 = (s16[448,128]{1,0:T(8,128)(2,1)S(1)}, s16[448,128]{1,0:T(8,128)(2,1)S(1)}, u32[]{:S(2)}, u32[]{:S(2)}) collective-permute-start(s16[448,128]{1,0:T(8,128)(2,1)S(1)} %get-tuple-element.86), channel_id=1, source_target_pairs={{16,32},{48,0},{32,16},{0,48},{17,33},{49,1},{33,17},{1,49},{18,34... | collective-permute-start | bytes 344072 | tf_op jit(solution)/shard_map/ppermute | solution.py:61
  92.5 3.8 %collective-permute-start.14 = (s16[448,128]{1,0:T(8,128)(2,1)S(1)}, s16[448,128]{1,0:T(8,128)(2,1)S(1)}, u32[]{:S(2)}, u32[]{:S(2)}) collective-permute-start(s16[448,128]{1,0:T(8,128)(2,1)S(1)} %shard_map.83), channel_id=1, source_target_pairs={{0,16},{32,48},{16,0},{48,32},{1,17},{33,49},{17,1},{49,33},{2,18}... | collective-permute-start | bytes 344072 | tf_op jit(solution)/shard_map/ppermute | solution.py:61
  96.5 10.9 %collective-permute-start.16 = (s16[656,128]{1,0:T(8,128)(2,1)S(1)}, s16[656,128]{1,0:T(8,128)(2,1)S(1)}, u32[]{:S(2)}, u32[]{:S(2)}) collective-permute-start(s16[656,128]{1,0:T(8,128)(2,1)S(1)} %get-tuple-element.93), channel_id=1, source_target_pairs={{0,1},{2,3},{4,5},{6,7},{8,9},{10,11},{12,13},{14,15},{1,0},{3,2},... | collective-permute-start | bytes 503816 | tf_op jit(solution)/shard_map/ppermute | solution.py:61
  98.7 8.8 %collective-permute-start.17 = (s16[656,128]{1,0:T(8,128)(2,1)S(1)}, s16[656,128]{1,0:T(8,128)(2,1)S(1)}, u32[]{:S(2)}, u32[]{:S(2)}) collective-permute-start(s16[656,128]{1,0:T(8,128)(2,1)S(1)} %get-tuple-element.94), channel_id=1, source_target_pairs={{1,2},{3,4},{5,6},{7,8},{9,10},{11,12},{13,14},{15,0},{2,1},{4,3},... | collective-permute-start | bytes 503816 | tf_op jit(solution)/shard_map/ppermute | solution.py:61
  103.4 4.0 %copy-start = (bf16[3,15,9,9,128]{4,1,3,2,0:T(8,128)(2,1)S(1)}, bf16[3,15,9,9,128]{4,1,3,2,0:T(8,128)(2,1)}, u32[]{:S(2)}) copy-start(bf16[3,15,9,9,128]{4,1,3,2,0:T(8,128)(2,1)} %param.7) | copy-start | bytes 2799364

commit v7 on v6

--- a/solution.py
+++ b/solution.py
@@ -632,7 +632,7 @@
         third_kernel, [whole, ((8, FIRST), F32), eight],
         (coefs, slots, lanes, rows, total, noise_tiles, slopes, *fronts, *ghosts),
         table + [pltpu.VMEM((SLOTS, 16, 256), BF16), loose, applied, pltpu.VMEM((2, ATOMS * 16, 128), F32), plain(256),
-         plain(NEIGH * 16), pltpu.VMEM(slopes.shape, BF16), pltpu.SemaphoreType.DMA,
+         plain(256), pltpu.VMEM(slopes.shape, BF16), pltpu.SemaphoreType.DMA,
          pltpu.VMEM((ORB, ATOMS, VECS), F32), pltpu.SemaphoreType.DMA] + BACK_PLAINS,
         flops=1 << 30, in_hbm=(6,), out_hbm=(0,),
     )

time: 136 us -> 136 us (level)
  no operation moved by 1% of the time
where the time goes in v7:
time: 136 us; the launch traced here: 135 us
  starting transfers between devices  73.7 us (54%)
  Pallas kernels  22.5 us (17%)
  blocking collectives  20.7 us (15%)
  waiting for transfers between devices  13.7 us (10%)
  other arithmetic  2.12 us (2%)
    ppermute x18, starting transfers between devices, swapped(): return lax.ppermute(value, axis, pairs + [(b, a) for a, b in pairs])  73.7 us
    pallas_call x22, Pallas kernels, call(): pl.pallas_call(kernel, out_shape=shapes, in_specs=[HBM if k in in_hbm els...  22.5 us
    all_to_all x2, blocking collectives, trade_all(): lax.all_to_all(sent, AXES, 0, 0, tiled=True, axis_index_groups=blocks(sec...  20.7 us
    ppermute x18, waiting for transfers between devices, swapped(): return lax.ppermute(value, axis, pairs + [(b, a) for a, b in pairs])  13.7 us
  transfers between devices with their start and end apart: 18, of which 9 were waited for; matrix products, arithmetic and copies ran while one was open for 1% of the time, Pallas kernels for 8%

profile of v7, /device:TPU:1, one launch (start us, length us, event | category | flops | bytes accessed | tf_op | source)
XLA Modules:
  0.0 134.8 jit_solution(9607203623082332046)
XLA Ops:
  1.6 5.5 %collective-permute-start.1 = (bf16[304,128]{1,0:T(8,128)(2,1)S(1)}, bf16[304,128]{1,0:T(8,128)(2,1)S(1)}, u32[]{:S(2)}, u32[]{:S(2)}) collective-permute-start(bf16[304,128]{1,0:T(8,128)(2,1)S(1)} %concatenate.7), channel_id=1, source_target_pairs={{0,64},{128,192},{256,320},{384,448},{64,0},{192,128},{320,256},{4... | collective-permute-start | bytes 233480 | tf_op jit(solution)/shard_map/ppermute | solution.py:61
  7.1 4.6 %collective-permute-start = (bf16[304,128]{1,0:T(8,128)(2,1)S(1)}, bf16[304,128]{1,0:T(8,128)(2,1)S(1)}, u32[]{:S(2)}, u32[]{:S(2)}) collective-permute-start(bf16[304,128]{1,0:T(8,128)(2,1)S(1)} %concatenate.6), channel_id=1, source_target_pairs={{64,128},{192,256},{320,384},{448,0},{128,64},{256,192},{384,320},... | collective-permute-start | bytes 233480 | tf_op jit(solution)/shard_map/ppermute | solution.py:61
  16.0 4.2 %collective-permute-start.3 = (bf16[448,128]{1,0:T(8,128)(2,1)S(1)}, bf16[448,128]{1,0:T(8,128)(2,1)S(1)}, u32[]{:S(2)}, u32[]{:S(2)}) collective-permute-start(bf16[448,128]{1,0:T(8,128)(2,1)S(1)} %get-tuple-element.54), channel_id=1, source_target_pairs={{16,32},{48,0},{32,16},{0,48},{17,33},{49,1},{33,17},{1,49},{18,34... | collective-permute-start | bytes 344072 | tf_op jit(solution)/shard_map/ppermute | solution.py:61
  20.4 4.1 %collective-permute-start.2 = (bf16[448,128]{1,0:T(8,128)(2,1)S(1)}, bf16[448,128]{1,0:T(8,128)(2,1)S(1)}, u32[]{:S(2)}, u32[]{:S(2)}) collective-permute-start(bf16[448,128]{1,0:T(8,128)(2,1)S(1)} %shard_map.70), channel_id=1, source_target_pairs={{0,16},{32,48},{16,0},{48,32},{1,17},{33,49},{17,1},{49,33},{2,18}... | collective-permute-start | bytes 344072 | tf_op jit(solution)/shard_map/ppermute | solution.py:61
  25.5 1.9 %collective-permute-start.4 = (bf16[656,128]{1,0:T(8,128)(2,1)S(1)}, bf16[656,128]{1,0:T(8,128)(2,1)S(1)}, u32[]{:S(2)}, u32[]{:S(2)}) collective-permute-start(bf16[656,128]{1,0:T(8,128)(2,1)S(1)} %get-tuple-element.60), channel_id=1, source_target_pairs={{0,1},{2,3},{4,5},{6,7},{8,9},{10,11},{12,13},{14,15},{1,0},{3,2},... | collective-permute-start | bytes 503816 | tf_op jit(solution)/shard_map/ppermute | solution.py:61
  27.4 10.0 %collective-permute-start.5 = (bf16[656,128]{1,0:T(8,128)(2,1)S(1)}, bf16[656,128]{1,0:T(8,128)(2,1)S(1)}, u32[]{:S(2)}, u32[]{:S(2)}) collective-permute-start(bf16[656,128]{1,0:T(8,128)(2,1)S(1)} %get-tuple-element.61), channel_id=1, source_target_pairs={{1,2},{3,4},{5,6},{7,8},{9,10},{11,12},{13,14},{15,0},{2,1},{4,3},... | collective-permute-start | bytes 503816 | tf_op jit(solution)/shard_map/ppermute | solution.py:61
  42.6 7.1 %collective-permute-start.6 = (s16[304,128]{1,0:T(8,128)(2,1)S(1)}, s16[304,128]{1,0:T(8,128)(2,1)S(1)}, u32[]{:S(2)}, u32[]{:S(2)}) collective-permute-start(s16[304,128]{1,0:T(8,128)(2,1)S(1)} %get-tuple-element.64), channel_id=1, source_target_pairs={{64,128},{192,256},{320,384},{448,0},{128,64},{256,192},{384,320},... | collective-permute-start | bytes 233480 | tf_op jit(solution)/shard_map/ppermute | solution.py:61
  49.6 1.9 %collective-permute-start.7 = (s16[304,128]{1,0:T(8,128)(2,1)S(1)}, s16[304,128]{1,0:T(8,128)(2,1)S(1)}, u32[]{:S(2)}, u32[]{:S(2)}) collective-permute-start(s16[304,128]{1,0:T(8,128)(2,1)S(1)} %get-tuple-element.65), channel_id=1, source_target_pairs={{0,64},{128,192},{256,320},{384,448},{64,0},{192,128},{320,256},{4... | collective-permute-start | bytes 233480 | tf_op jit(solution)/shard_map/ppermute | solution.py:61
  53.0 3.3 %collective-permute-done.7.refs_1_ = s16[304,128]{1,0:T(8,128)(2,1)S(1)} collective-permute-done((s16[304,128]{1,0:T(8,128)(2,1)S(1)}, s16[304,128]{1,0:T(8,128)(2,1)S(1)}, u32[]{:S(2)}, u32[]{:S(2)}) %collective-permute-start.7) | collective-permute-done | bytes 77856 | tf_op jit(solution)/shard_map/ppermute | solution.py:61
  56.4 3.4 %collective-permute-start.9 = (s16[448,128]{1,0:T(8,128)(2,1)S(1)}, s16[448,128]{1,0:T(8,128)(2,1)S(1)}, u32[]{:S(2)}, u32[]{:S(2)}) collective-permute-start(s16[448,128]{1,0:T(8,128)(2,1)S(1)} %get-tuple-element.70), channel_id=1, source_target_pairs={{16,32},{48,0},{32,16},{0,48},{17,33},{49,1},{33,17},{1,49},{18,34... | collective-permute-start | bytes 344072 | tf_op jit(solution)/shard_map/ppermute | solution.py:61
  59.9 2.9 %collective-permute-start.8 = (s16[448,128]{1,0:T(8,128)(2,1)S(1)}, s16[448,128]{1,0:T(8,128)(2,1)S(1)}, u32[]{:S(2)}, u32[]{:S(2)}) collective-permute-start(s16[448,128]{1,0:T(8,128)(2,1)S(1)} %shard_map.77), channel_id=1, source_target_pairs={{0,16},{32,48},{16,0},{48,32},{1,17},{33,49},{17,1},{49,33},{2,18}... | collective-permute-start | bytes 344072 | tf_op jit(solution)/shard_map/ppermute | solution.py:61
  65.8 4.6 %collective-permute-start.11 = (s16[656,128]{1,0:T(8,128)(2,1)S(1)}, s16[656,128]{1,0:T(8,128)(2,1)S(1)}, u32[]{:S(2)}, u32[]{:S(2)}) collective-permute-start(s16[656,128]{1,0:T(8,128)(2,1)S(1)} %get-tuple-element.77), channel_id=1, source_target_pairs={{1,2},{3,4},{5,6},{7,8},{9,10},{11,12},{13,14},{15,0},{2,1},{4,3},... | collective-permute-start | bytes 503816 | tf_op jit(solution)/shard_map/ppermute | solution.py:61
  70.4 2.5 %shard_map.80 = (bf16[288,16,256]{2,1,0:T(8,128)(2,1)S(1)}, f32[1024,128]{1,0:T(8,128)S(1)}) custom-call(s32[15,128]{1,0:T(8,128)S(1)} %add_select_fusion.15.slots, bf16[128,16,256]{2,1,0:T(8,128)(2,1)S(1)} %shard_map.68.rows, f32[9,128,128]{2,1,0:T(8,128)S(1)} %get-tuple-element.63.refs_3_.own.first, f32[304,128]{1,0:T(8,128)S(1)} %get-tuple-element.67.u1, ...), custom_call_target="tpu_custom_call" | custom-call | flops 536870912 | bytes 5299712 | tf_op jit(solution)/shard_map/pallas_call | solution.py:43
  73.4 2.3 %shard_map.81 = (f32[9,128,128]{2,1,0:T(8,128)S(1)}, f32[9,128,128]{2,1,0:T(8,128)S(1)}, s16[304,128]{1,0:T(8,128)(2,1)S(1)}, s16[304,128]{1,0:T(8,128)(2,1)S(1)}, f32[8,128]{1,0:T(8,128)S(1)}) custom-call(f32[4,128]{1,0:T(4,128)S(1)} %broadcast_in_dim.90.coef, s32[15,128]{1,0:T(8,128)S(1)} %add_select_fusion.15.slots, ...), custom_call_target="tpu_custom_call" | custom-call | flops 536870912 | bytes 7386624 | tf_op jit(solution)/shard_map/pallas_call | solution.py:43
  75.7 6.6 %collective-permute-start.12 = (s16[304,128]{1,0:T(8,128)(2,1)S(1)}, s16[304,128]{1,0:T(8,128)(2,1)S(1)}, u32[]{:S(2)}, u32[]{:S(2)}) collective-permute-start(s16[304,128]{1,0:T(8,128)(2,1)S(1)} %get-tuple-element.80), channel_id=1, source_target_pairs={{64,128},{192,256},{320,384},{448,0},{128,64},{256,192},{384,320},... | collective-permute-start | bytes 233480 | tf_op jit(solution)/shard_map/ppermute | solution.py:61
  84.4 4.5 %collective-permute-done.13.refs_1_ = s16[304,128]{1,0:T(8,128)(2,1)S(1)} collective-permute-done((s16[304,128]{1,0:T(8,128)(2,1)S(1)}, s16[304,128]{1,0:T(8,128)(2,1)S(1)}, u32[]{:S(2)}, u32[]{:S(2)}) %collective-permute-start.13) | collective-permute-done | bytes 77856 | tf_op jit(solution)/shard_map/ppermute | solution.py:61
  89.1 3.3 %collective-permute-start.15 = (s16[448,128]{1,0:T(8,128)(2,1)S(1)}, s16[448,128]{1,0:T(8,128)(2,1)S(1)}, u32[]{:S(2)}, u32[]{:S(2)}) collective-permute-start(s16[448,128]{1,0:T(8,128)(2,1)S(1)} %get-tuple-element.86), channel_id=1, source_target_pairs={{16,32},{48,0},{32,16},{0,48},{17,33},{49,1},{33,17},{1,49},{18,34... | collective-permute-start | bytes 344072 | tf_op jit(solution)/shard_map/ppermute | solution.py:61
  92.5 2.9 %collective-permute-start.14 = (s16[448,128]{1,0:T(8,128)(2,1)S(1)}, s16[448,128]{1,0:T(8,128)(2,1)S(1)}, u32[]{:S(2)}, u32[]{:S(2)}) collective-permute-start(s16[448,128]{1,0:T(8,128)(2,1)S(1)} %shard_map.83), channel_id=1, source_target_pairs={{0,16},{32,48},{16,0},{48,32},{1,17},{33,49},{17,1},{49,33},{2,18}... | collective-permute-start | bytes 344072 | tf_op jit(solution)/shard_map/ppermute | solution.py:61
  96.5 2.2 %collective-permute-start.16 = (s16[656,128]{1,0:T(8,128)(2,1)S(1)}, s16[656,128]{1,0:T(8,128)(2,1)S(1)}, u32[]{:S(2)}, u32[]{:S(2)}) collective-permute-start(s16[656,128]{1,0:T(8,128)(2,1)S(1)} %get-tuple-element.93), channel_id=1, source_target_pairs={{0,1},{2,3},{4,5},{6,7},{8,9},{10,11},{12,13},{14,15},{1,0},{3,2},... | collective-permute-start | bytes 503816 | tf_op jit(solution)/shard_map/ppermute | solution.py:61
  98.7 4.8 %collective-permute-start.17 = (s16[656,128]{1,0:T(8,128)(2,1)S(1)}, s16[656,128]{1,0:T(8,128)(2,1)S(1)}, u32[]{:S(2)}, u32[]{:S(2)}) collective-permute-start(s16[656,128]{1,0:T(8,128)(2,1)S(1)} %get-tuple-element.94), channel_id=1, source_target_pairs={{1,2},{3,4},{5,6},{7,8},{9,10},{11,12},{13,14},{15,0},{2,1},{4,3},... | collective-permute-start | bytes 503816 | tf_op jit(solution)/shard_map/ppermute | solution.py:61
  103.5 4.0 %shard_map.86 = (bf16[288,16,256]{2,1,0:T(8,128)(2,1)S(1)}, f32[1024,128]{1,0:T(8,128)S(1)}, f32[2,1024,128]{2,1,0:T(8,128)S(1)}) custom-call(f32[4,128]{1,0:T(4,128)S(1)} %broadcast_in_dim.90.coef, s32[15,128]{1,0:T(8,128)S(1)} %add_select_fusion.15.slots, bf16[128,16,256]{2,1,0:T(8,128)(2,1)S(1)} %shard_map.68.rows, ...), custom_call_target="tpu_custom_call" | custom-call | flops 1073741824 | bytes 8709632 | tf_op jit(solution)/shard_map/pallas_call | solution.py:43
  107.5 5.5 %shard_map.87 = (f32[9,128,128]{2,1,0:T(8,128)}, f32[8,256]{1,0:T(8,128)S(1)}, f32[8,8,128]{2,1,0:T(8,128)S(1)}) custom-call(f32[4,128]{1,0:T(4,128)S(1)} %broadcast_in_dim.90.coef, s32[15,128]{1,0:T(8,128)S(1)} %add_select_fusion.15.slots, s32[15,128]{1,0:T(8,128)S(1)} %get-tuple-element.100.lanes, bf16[128,16,256]{2,1,0:T(8,128)(2,1)S(1)} %shard_map.68.rows, ...), custom_call_target="tpu_custom_call" | custom-call | flops 1073741824 | bytes 9257216 | tf_op jit(solution)/shard_map/pallas_call | solution.py:43
  113.0 10.1 %all_to_all.10.got = f32[8,8,128]{2,1,0:T(8,128)S(1)} all-to-all(f32[8,8,128]{2,1,0:T(8,128)S(1)} %get-tuple-element.97), channel_id=1, replica_groups={{0,1,16,17,64,65,80,81},{2,3,18,19,66,67,82,83},{4,5,20,21,68,69,84,85}..., dimensions={0} | all-to-all | bytes 65536 | tf_op jit(solution)/shard_map/all_to_all | solution.py:466
  123.4 10.6 %all_to_all.11.got = f32[8,8,128]{2,1,0:T(8,128)S(1)} all-to-all(f32[8,8,128]{2,1,0:T(8,128)S(1)} %get-tuple-element.99), channel_id=1, replica_groups={{81,82,97,98,145,146,161,162},{83,84,99,100,147,148,163,164},{85,86,101..., dimensions={0} | all-to-all | bytes 65536 | tf_op jit(solution)/shard_map/all_to_all | solution.py:466
  (52 shorter events, 21.2 us)
Async XLA Ops:
  0.6 19.6 %copy-start.2 = (s32[128,15]{0,1:T(8,128)S(1)}, s32[128,15]{0,1:T(8,128)}, u32[]{:S(2)}) copy-start(s32[128,15]{0,1:T(8,128)} %param.8) | copy-start | bytes 23044
  1.6 13.1 %collective-permute-start.1 = (bf16[304,128]{1,0:T(8,128)(2,1)S(1)}, bf16[304,128]{1,0:T(8,128)(2,1)S(1)}, u32[]{:S(2)}, u32[]{:S(2)}) collective-permute-start(bf16[304,128]{1,0:T(8,128)(2,1)S(1)} %concatenate.7), channel_id=1, source_target_pairs={{0,64},{128,192},{256,320},{384,448},{64,0},{192,128},{320,256},{4... | collective-permute-start | bytes 233480 | tf_op jit(solution)/shard_map/ppermute | solution.py:61
  7.1 8.8 %collective-permute-start = (bf16[304,128]{1,0:T(8,128)(2,1)S(1)}, bf16[304,128]{1,0:T(8,128)(2,1)S(1)}, u32[]{:S(2)}, u32[]{:S(2)}) collective-permute-start(bf16[304,128]{1,0:T(8,128)(2,1)S(1)} %concatenate.6), channel_id=1, source_target_pairs={{64,128},{192,256},{320,384},{448,0},{128,64},{256,192},{384,320},... | collective-permute-start | bytes 233480 | tf_op jit(solution)/shard_map/ppermute | solution.py:61
  12.8 1.0 copy-start.1
  16.0 8.5 %collective-permute-start.3 = (bf16[448,128]{1,0:T(8,128)(2,1)S(1)}, bf16[448,128]{1,0:T(8,128)(2,1)S(1)}, u32[]{:S(2)}, u32[]{:S(2)}) collective-permute-start(bf16[448,128]{1,0:T(8,128)(2,1)S(1)} %get-tuple-element.54), channel_id=1, source_target_pairs={{16,32},{48,0},{32,16},{0,48},{17,33},{49,1},{33,17},{1,49},{18,34... | collective-permute-start | bytes 344072 | tf_op jit(solution)/shard_map/ppermute | solution.py:61
  20.4 5.0 %collective-permute-start.2 = (bf16[448,128]{1,0:T(8,128)(2,1)S(1)}, bf16[448,128]{1,0:T(8,128)(2,1)S(1)}, u32[]{:S(2)}, u32[]{:S(2)}) collective-permute-start(bf16[448,128]{1,0:T(8,128)(2,1)S(1)} %shard_map.70), channel_id=1, source_target_pairs={{0,16},{32,48},{16,0},{48,32},{1,17},{33,49},{17,1},{49,33},{2,18}... | collective-permute-start | bytes 344072 | tf_op jit(solution)/shard_map/ppermute | solution.py:61
  24.5 16.2 %copy-start.3 = (f32[4]{0:T(128)S(1)}, f32[4]{0:T(128)}, u32[]{:S(2)}) copy-start(f32[4]{0:T(128)} %param.9) | copy-start | bytes 52
  25.5 13.9 %collective-permute-start.4 = (bf16[656,128]{1,0:T(8,128)(2,1)S(1)}, bf16[656,128]{1,0:T(8,128)(2,1)S(1)}, u32[]{:S(2)}, u32[]{:S(2)}) collective-permute-start(bf16[656,128]{1,0:T(8,128)(2,1)S(1)} %get-tuple-element.60), channel_id=1, source_target_pairs={{0,1},{2,3},{4,5},{6,7},{8,9},{10,11},{12,13},{14,15},{1,0},{3,2},... | collective-permute-start | bytes 503816 | tf_op jit(solution)/shard_map/ppermute | solution.py:61
  27.4 13.3 %collective-permute-start.5 = (bf16[656,128]{1,0:T(8,128)(2,1)S(1)}, bf16[656,128]{1,0:T(8,128)(2,1)S(1)}, u32[]{:S(2)}, u32[]{:S(2)}) collective-permute-start(bf16[656,128]{1,0:T(8,128)(2,1)S(1)} %get-tuple-element.61), channel_id=1, source_target_pairs={{1,2},{3,4},{5,6},{7,8},{9,10},{11,12},{13,14},{15,0},{2,1},{4,3},... | collective-permute-start | bytes 503816 | tf_op jit(solution)/shard_map/ppermute | solution.py:61
  42.6 10.4 %collective-permute-start.6 = (s16[304,128]{1,0:T(8,128)(2,1)S(1)}, s16[304,128]{1,0:T(8,128)(2,1)S(1)}, u32[]{:S(2)}, u32[]{:S(2)}) collective-permute-start(s16[304,128]{1,0:T(8,128)(2,1)S(1)} %get-tuple-element.64), channel_id=1, source_target_pairs={{64,128},{192,256},{320,384},{448,0},{128,64},{256,192},{384,320},... | collective-permute-start | bytes 233480 | tf_op jit(solution)/shard_map/ppermute | solution.py:61
  49.6 6.6 %collective-permute-start.7 = (s16[304,128]{1,0:T(8,128)(2,1)S(1)}, s16[304,128]{1,0:T(8,128)(2,1)S(1)}, u32[]{:S(2)}, u32[]{:S(2)}) collective-permute-start(s16[304,128]{1,0:T(8,128)(2,1)S(1)} %get-tuple-element.65), channel_id=1, source_target_pairs={{0,64},{128,192},{256,320},{384,448},{64,0},{192,128},{320,256},{4... | collective-permute-start | bytes 233480 | tf_op jit(solution)/shard_map/ppermute | solution.py:61
  56.4 6.3 %collective-permute-start.9 = (s16[448,128]{1,0:T(8,128)(2,1)S(1)}, s16[448,128]{1,0:T(8,128)(2,1)S(1)}, u32[]{:S(2)}, u32[]{:S(2)}) collective-permute-start(s16[448,128]{1,0:T(8,128)(2,1)S(1)} %get-tuple-element.70), channel_id=1, source_target_pairs={{16,32},{48,0},{32,16},{0,48},{17,33},{49,1},{33,17},{1,49},{18,34... | collective-permute-start | bytes 344072 | tf_op jit(solution)/shard_map/ppermute | solution.py:61
  59.9 3.8 %collective-permute-start.8 = (s16[448,128]{1,0:T(8,128)(2,1)S(1)}, s16[448,128]{1,0:T(8,128)(2,1)S(1)}, u32[]{:S(2)}, u32[]{:S(2)}) collective-permute-start(s16[448,128]{1,0:T(8,128)(2,1)S(1)} %shard_map.77), channel_id=1, source_target_pairs={{0,16},{32,48},{16,0},{48,32},{1,17},{33,49},{17,1},{49,33},{2,18}... | collective-permute-start | bytes 344072 | tf_op jit(solution)/shard_map/ppermute | solution.py:61
  63.8 9.0 %collective-permute-start.10 = (s16[656,128]{1,0:T(8,128)(2,1)S(1)}, s16[656,128]{1,0:T(8,128)(2,1)S(1)}, u32[]{:S(2)}, u32[]{:S(2)}) collective-permute-start(s16[656,128]{1,0:T(8,128)(2,1)S(1)} %get-tuple-element.76), channel_id=1, source_target_pairs={{0,1},{2,3},{4,5},{6,7},{8,9},{10,11},{12,13},{14,15},{1,0},{3,2},... | collective-permute-start | bytes 503816 | tf_op jit(solution)/shard_map/ppermute | solution.py:61
  65.8 7.6 %collective-permute-start.11 = (s16[656,128]{1,0:T(8,128)(2,1)S(1)}, s16[656,128]{1,0:T(8,128)(2,1)S(1)}, u32[]{:S(2)}, u32[]{:S(2)}) collective-permute-start(s16[656,128]{1,0:T(8,128)(2,1)S(1)} %get-tuple-element.77), channel_id=1, source_target_pairs={{1,2},{3,4},{5,6},{7,8},{9,10},{11,12},{13,14},{15,0},{2,1},{4,3},... | collective-permute-start | bytes 503816 | tf_op jit(solution)/shard_map/ppermute | solution.py:61
  75.7 8.8 %collective-permute-start.12 = (s16[304,128]{1,0:T(8,128)(2,1)S(1)}, s16[304,128]{1,0:T(8,128)(2,1)S(1)}, u32[]{:S(2)}, u32[]{:S(2)}) collective-permute-start(s16[304,128]{1,0:T(8,128)(2,1)S(1)} %get-tuple-element.80), channel_id=1, source_target_pairs={{64,128},{192,256},{320,384},{448,0},{128,64},{256,192},{384,320},... | collective-permute-start | bytes 233480 | tf_op jit(solution)/shard_map/ppermute | solution.py:61
  82.3 6.6 %collective-permute-start.13 = (s16[304,128]{1,0:T(8,128)(2,1)S(1)}, s16[304,128]{1,0:T(8,128)(2,1)S(1)}, u32[]{:S(2)}, u32[]{:S(2)}) collective-permute-start(s16[304,128]{1,0:T(8,128)(2,1)S(1)} %get-tuple-element.81), channel_id=1, source_target_pairs={{0,64},{128,192},{256,320},{384,448},{64,0},{192,128},{320,256},{4... | collective-permute-start | bytes 233480 | tf_op jit(solution)/shard_map/ppermute | solution.py:61
  89.1 6.3 %collective-permute-start.15 = (s16[448,128]{1,0:T(8,128)(2,1)S(1)}, s16[448,128]{1,0:T(8,128)(2,1)S(1)}, u32[]{:S(2)}, u32[]{:S(2)}) collective-permute-start(s16[448,128]{1,0:T(8,128)(2,1)S(1)} %get-tuple-element.86), channel_id=1, source_target_pairs={{16,32},{48,0},{32,16},{0,48},{17,33},{49,1},{33,17},{1,49},{18,34... | collective-permute-start | bytes 344072 | tf_op jit(solution)/shard_map/ppermute | solution.py:61
  92.5 3.8 %collective-permute-start.14 = (s16[448,128]{1,0:T(8,128)(2,1)S(1)}, s16[448,128]{1,0:T(8,128)(2,1)S(1)}, u32[]{:S(2)}, u32[]{:S(2)}) collective-permute-start(s16[448,128]{1,0:T(8,128)(2,1)S(1)} %shard_map.83), channel_id=1, source_target_pairs={{0,16},{32,48},{16,0},{48,32},{1,17},{33,49},{17,1},{49,33},{2,18}... | collective-permute-start | bytes 344072 | tf_op jit(solution)/shard_map/ppermute | solution.py:61
  96.5 10.9 %collective-permute-start.16 = (s16[656,128]{1,0:T(8,128)(2,1)S(1)}, s16[656,128]{1,0:T(8,128)(2,1)S(1)}, u32[]{:S(2)}, u32[]{:S(2)}) collective-permute-start(s16[656,128]{1,0:T(8,128)(2,1)S(1)} %get-tuple-element.93), channel_id=1, source_target_pairs={{0,1},{2,3},{4,5},{6,7},{8,9},{10,11},{12,13},{14,15},{1,0},{3,2},... | collective-permute-start | bytes 503816 | tf_op jit(solution)/shard_map/ppermute | solution.py:61
  98.7 8.8 %collective-permute-start.17 = (s16[656,128]{1,0:T(8,128)(2,1)S(1)}, s16[656,128]{1,0:T(8,128)(2,1)S(1)}, u32[]{:S(2)}, u32[]{:S(2)}) collective-permute-start(s16[656,128]{1,0:T(8,128)(2,1)S(1)} %get-tuple-element.94), channel_id=1, source_target_pairs={{1,2},{3,4},{5,6},{7,8},{9,10},{11,12},{13,14},{15,0},{2,1},{4,3},... | collective-permute-start | bytes 503816 | tf_op jit(solution)/shard_map/ppermute | solution.py:61
  103.4 4.0 %copy-start = (bf16[3,15,9,9,128]{4,1,3,2,0:T(8,128)(2,1)S(1)}, bf16[3,15,9,9,128]{4,1,3,2,0:T(8,128)(2,1)}, u32[]{:S(2)}) copy-start(bf16[3,15,9,9,128]{4,1,3,2,0:T(8,128)(2,1)} %param.7) | copy-start | bytes 2799364
